TPU v7x, 32 devices: a whole 2x2x4 slice. The times are simulated.
32 devices in a mesh: seq: 16 (over z, y, core), tp: 2 (over x).
Axes of the slice: x: 2, y: 2, z: 4, core: 2. Of those that a mesh axis runs over, the one named last changes fastest.
Arguments:
- residual_in: bfloat16 [4096, 1024], P('seq', 'tp'), may hold values from -6 to 6
- queries: bfloat16 [4096, 1024], P('seq', 'tp'), may hold values from -240 to 240
- keys: bfloat16 [4096, 1024], P('seq', 'tp'), may hold values from -12 to 12
- values: bfloat16 [4096, 1024], P('seq', 'tp'), may hold values from -6 to 6
- head_offset: int32 [6, 16], P(None, 'tp'), may hold values from 0 to 31
- out_weight: bfloat16 [1024, 1024], P('tp'), may hold values from -0.1875 to 0.1875
- norm_gain: float32 [1024], replicated, may hold values from 0.5 to 1.5
- gate_weight: bfloat16 [1024, 2048], P(None, 'tp'), may hold values from -0.1875 to 0.1875
- up_weight: bfloat16 [1024, 2048], P(None, 'tp'), may hold values from -0.1875 to 0.1875
- down_weight: bfloat16 [2048, 1024], P('tp'), may hold values from -0.125 to 0.125
Outputs:
- layer_out: bfloat16 [4096, 1024], P('seq', 'tp')
All inputs are finite; a program needn't handle non-finite values.
Results may differ from a plain program's by a relative error of at most 0.0095.
Values may be sent and summed in bfloat16 or wider, within the bound.
No kernel may reach another device: no remote copies, remote signals or barrier semaphores. Data moves between devices by JAX's collectives and lax.ppermute only.
A program may use at most 128 MiB of HBM per device.

v0:
```python
import math

import jax
import jax.numpy as jnp
from jax import lax
from jax.sharding import PartitionSpec as P

BRANCHES = 6


masked_score = -1e30


def from_partner(block, axis, distance):
    count = lax.axis_size(axis)
    route = []
    for low in range(count):
        high = low | 1 << distance
        if high != low and high < count:
            route += [(low, high), (high, low)]
    return lax.ppermute(block, axis, route)


def pick_rows(array, choose, rate):
    count = array.shape[0] // rate
    shaped = array.reshape(count, rate, array.shape[1], array.shape[2])
    return jnp.sum(shaped * choose[None, :, :, None].astype(array.dtype), axis=1)


def place_bit(blocks, partner, upper):
    first = jnp.where(upper, partner, blocks)
    second = jnp.where(upper, blocks, partner)
    return jnp.concatenate([first, second], axis=0)


def shards(
    residual_in,
    queries,
    keys,
    values,
    head_offset,
    out_weight,
    norm_gain,
    gate_weight,
    up_weight,
    down_weight,
):
    rows = queries.shape[0]
    cols = queries.shape[1]
    heads_here = head_offset.shape[1]
    head_dim = cols // heads_here
    seq_count = lax.axis_size("seq")
    seq_index = lax.axis_index("seq")
    top_bits = min(seq_count.bit_length() - 1, BRANCHES)
    scale = 1.0 / math.sqrt(head_dim)
    query_heads = queries.reshape(rows, heads_here, head_dim)
    key_heads = keys.reshape(rows, heads_here, head_dim)
    value_heads = values.reshape(rows, heads_here, head_dim)
    order = list(range(top_bits))
    chooses = []
    picked_queries = []
    stacks = []
    bit_counts = []
    for branch in range(BRANCHES):
        rate = 2**branch
        offsets = head_offset[branch] % rate
        choose = jnp.arange(rate, dtype=jnp.int32)[:, None] == offsets[None, :]
        chooses.append(choose)
        picked_queries.append(pick_rows(query_heads, choose, rate))
        picked_key = pick_rows(key_heads, choose, rate).reshape(rows // rate, cols)
        picked_value = pick_rows(value_heads, choose, rate).reshape(rows // rate, cols)
        stacks.append(jnp.concatenate([picked_key, picked_value], axis=1)[None])
        bit_counts.append(min(branch + 1, top_bits))
    for branch in range(BRANCHES):
        blocks = stacks[branch]
        for bit in order:
            if bit < bit_counts[branch]:
                partner = from_partner(blocks, "seq", bit)
                blocks = place_bit(blocks, partner, seq_index // 2**bit % 2 == 1)
        stacks[branch] = blocks
    peak = None
    total = None
    accum = None
    for branch in range(BRANCHES):
        rate = 2**branch
        group = 2 ** bit_counts[branch]
        count = rows // rate
        whole = stacks[branch].reshape(group * count, 2 * cols)
        key_rows = whole[:, :cols].reshape(group * count, heads_here, head_dim).transpose(1, 0, 2)
        value_rows = whole[:, cols:].reshape(group * count, heads_here, head_dim).transpose(1, 0, 2)
        query_rows = picked_queries[branch].transpose(1, 0, 2)
        position = seq_index % group * count + jnp.arange(count, dtype=jnp.int32)
        causal = jnp.arange(group * count, dtype=jnp.int32)[None, :] <= position[:, None]

        def attend(block):
            query, key_block, value_block = block
            scores = jnp.dot(query, key_block.T, preferred_element_type=jnp.float32) * scale
            scores = jnp.where(causal, scores, masked_score)
            top = jnp.max(scores, axis=1, keepdims=True)
            log_total = top + jnp.log(jnp.sum(jnp.exp(scores - top), axis=1, keepdims=True))
            weights = jnp.exp(scores - log_total).astype(jnp.bfloat16)
            output = jnp.dot(weights, value_block, preferred_element_type=jnp.float32)
            return (output, log_total[:, 0])

        outputs, logs = lax.map(attend, (query_rows, key_rows, value_rows))
        choose = chooses[branch]
        chosen = choose.astype(jnp.float32)
        spread = (outputs.transpose(1, 0, 2)[:, None] * chosen[None, :, :, None]).reshape(
            rows, heads_here, head_dim
        )
        spread_log = jnp.broadcast_to(logs.T[:, None, :], (count, rate, heads_here)).reshape(
            rows, heads_here
        )
        covered = jnp.broadcast_to(choose[None], (count, rate, heads_here)).reshape(
            rows, heads_here
        )
        if branch == 0:
            peak = spread_log
            total = jnp.ones((rows, heads_here), jnp.float32)
            accum = spread
        else:
            new_peak = jnp.where(covered, jnp.maximum(peak, spread_log), peak)
            keep = jnp.exp(peak - new_peak)
            branch_weight = jnp.where(
                covered, jnp.exp(jnp.where(covered, spread_log, new_peak) - new_peak), 0.0
            )
            total = total * keep + branch_weight
            accum = accum * keep[..., None] + branch_weight[..., None] * spread
            peak = new_peak
    mix = (accum / total[..., None]).astype(jnp.bfloat16).reshape(rows, cols)
    partial_value = jnp.dot(mix, out_weight, preferred_element_type=jnp.float32)
    width = residual_in.shape[1]
    start = lax.axis_index("tp") * width
    model_width = norm_gain.shape[0]
    share = lax.psum_scatter(
        partial_value, "tp", scatter_dimension=1, tiled=True
    ) + residual_in.astype(jnp.float32)
    squares = lax.psum(jnp.sum(share * share, axis=1), "tp")
    inverse = lax.rsqrt(squares / model_width + 1e-05)
    gain_share = lax.dynamic_slice_in_dim(norm_gain, start, width)
    normed = (share * inverse[:, None] * gain_share[None, :]).astype(jnp.bfloat16)
    piece = lax.all_gather(normed, "tp", axis=1, tiled=True)
    gate = jnp.dot(piece, gate_weight, preferred_element_type=jnp.float32)
    up = jnp.dot(piece, up_weight, preferred_element_type=jnp.float32)
    act = (jax.nn.silu(gate) * up).astype(jnp.bfloat16)
    ffn = lax.psum_scatter(
        jnp.dot(act, down_weight, preferred_element_type=jnp.float32).astype(jnp.bfloat16),
        "tp",
        scatter_dimension=1,
        tiled=True,
    ).astype(jnp.float32)
    return (share + ffn).astype(jnp.bfloat16)


def solution(mesh):
    placed = (
        P("seq", "tp"),
        P("seq", "tp"),
        P("seq", "tp"),
        P("seq", "tp"),
        P(None, "tp"),
        P("tp", None),
        P(),
        P(None, "tp"),
        P(None, "tp"),
        P("tp", None),
    )
    return jax.shard_map(
        shards, mesh=mesh, in_specs=placed, out_specs=P("seq", "tp"), check_vma=False
    )
```

profile of v0, /device:TPU:0, one launch (start us, length us, event | category | flops | bytes accessed | tf_op | source)
XLA Modules:
  0.0 339.8 jit_solution(5387988852914135091)
XLA Ops:
  6.5 1.5 fusion.110
  9.8 2.1 reshape_reshape.52
  11.9 2.1 reshape_reshape.53
  14.0 2.9 multiply_reduce_fusion.14
  23.4 2.7 multiply_reduce_fusion.11
  32.2 2.5 multiply_reduce_fusion.8
  41.6 2.3 multiply_reduce_fusion.2
  52.4 2.3 multiply_reduce_fusion.5
  58.4 1.7 copy.195
  60.1 1.6 copy.209
  61.7 1.5 copy.224
  75.0 2.7 collective-permute-start.15
  77.7 1.9 collective-permute-done.15
  79.6 2.0 collective-permute-start.11
  81.6 1.6 collective-permute-start.16
  84.2 1.7 collective-permute-start.7
  85.9 1.6 collective-permute-start.12
  87.6 2.7 collective-permute-start.17
  95.0 2.3 collective-permute-start.13
  99.2 1.7 copy.240
  100.9 21.4 %while.83 = (s32[]{:T(128)}, f32[8,8,64]{2,1,0:T(8,128)}, f32[8,8]{1,0:T(8,128)S(1)}, bf16[8,8,64]{2,1,0:T(8,128)(2,1)}, bf16[8,128,64]{1,2,0:T(8,128)(2,1)S(1)}...) while((s32[]{:T(128)}, f32[8,8,64]{2,1,0:T(8,128)}, ...), condition=%wide.region_38.39_spmd.clone, body=%wide.region_35.38_spmd.clone.sunk | while | flops 270330 | bytes 54145 | solution.py:105
  102.2 1.5 fusion.188
  104.8 1.5 fusion.188
  107.4 1.5 fusion.188
  110.1 1.5 fusion.188
  112.8 1.5 fusion.188
  115.4 1.5 fusion.188
  118.1 1.5 fusion.188
  120.7 1.5 fusion.188
  124.2 1.5 mul.515
  128.8 1.9 collective-permute-start.2
  134.6 1.4 collective-permute-start.9
  137.9 1.8 copy.230
  139.7 1.8 copy.231
  141.5 17.6 %while.82 = (s32[]{:T(128)}, f32[8,16,64]{2,1,0:T(8,128)S(1)}, f32[8,16]{1,0:T(8,128)S(1)}, bf16[8,16,64]{2,1,0:T(8,128)(2,1)}, bf16[8,256,64]{1,2,0:T(8,128)(2,...) while((s32[]{:T(128)}, f32[8,16,64]{2,1,0:T(8,128)S(1)}, ...), condition=%wide.region_31.32_spmd.clone, body=%wide.region_28.31_spmd.clone.sunk | while | flops 1081330 | bytes 130209 | solution.py:105
  160.3 2.3 mul.497
  162.6 2.1 copy.237
  167.0 2.1 copy.261
  170.0 25.9 %while.78 = (s32[]{:T(128)}, f32[8,256,64]{1,2,0:T(8,128)}, f32[8,256]{1,0:T(8,128)S(1)}, bf16[8,256,64]{1,2,0:T(8,128)(2,1)}, bf16[8,512,64]{1,2,0:T(8,128)(2,1...) while((s32[]{:T(128)}, f32[8,256,64]{1,2,0:T(8,128)}, ...), condition=%wide.region_3.4_spmd.clone, body=%wide.region_0.0_spmd.clone.sunk | while | flops 34602752 | bytes 1814625 | solution.py:105
  171.5 1.8 fusion.173
  174.7 1.8 fusion.173
  178.0 1.8 fusion.173
  181.2 1.8 fusion.173
  184.5 1.8 fusion.173
  187.7 1.8 fusion.173
  190.9 1.8 fusion.173
  194.2 1.8 fusion.173
  198.2 1.5 copy.192
  203.3 17.0 %while.79 = (s32[]{:T(128)}, f32[8,128,64]{1,2,0:T(8,128)}, f32[8,128]{1,0:T(8,128)S(1)}, bf16[8,128,64]{2,1,0:T(8,128)(2,1)}, bf16[8,512,64]{1,2,0:T(8,128)(2,1...) while((s32[]{:T(128)}, f32[8,128,64]{1,2,0:T(8,128)}, ...), condition=%wide.region_10.11_spmd.clone, body=%wide.region_7.0_spmd.clone.sunk | while | flops 17301376 | bytes 990305 | solution.py:105
  220.5 2.0 copy.204
  224.7 2.0 copy.206
  229.4 17.5 %while.80 = (s32[]{:T(128)}, f32[8,64,64]{2,1,0:T(8,128)}, f32[8,64]{1,0:T(8,128)S(1)}, bf16[8,64,64]{2,1,0:T(8,128)(2,1)}, bf16[8,512,64]{1,2,0:T(8,128)(2,1)},...) while((s32[]{:T(128)}, f32[8,64,64]{2,1,0:T(8,128)}, ...), condition=%wide.region_17.18_spmd.clone, body=%wide.region_14.0_spmd.clone.sunk | while | flops 8650690 | bytes 578401 | solution.py:105
  249.4 2.0 copy.220
  254.1 12.5 %while.81 = (s32[]{:T(128)}, f32[8,32,64]{2,1,0:T(8,128)S(1)}, f32[8,32]{1,0:T(8,128)S(1)}, bf16[8,32,64]{2,1,0:T(8,128)(2,1)}, bf16[8,512,64]{1,2,0:T(8,128)(2,...) while((s32[]{:T(128)}, f32[8,32,64]{2,1,0:T(8,128)S(1)}, ...), condition=%wide.region_24.25_spmd.clone, body=%wide.region_21.24_spmd.clone.sunk | while | flops 4325346 | bytes 356065 | solution.py:105
  268.1 2.1 copy.228
  271.6 1.8 fusion.79
  273.4 1.5 fusion.144
  275.0 20.0 %reduce-scatter.3.cloned.1.call-done = f32[256,512]{1,0:T(8,128)} async-done(((f32[256,1024]{1,0:T(8,128)}), f32[256,512]{1,0:T(8,128)}) %reduce-scatter.3.cloned.1.call-update) | async-done | bytes 524304 | tf_op jit(solution)/shard_map/reduce_scatter | solution.py:135
  296.2 4.9 %psum.7 = f32[256]{0:T(256)S(1)} all-reduce(f32[256]{0:T(256)S(1)} %multiply_reduce_fusion), channel_id=1, replica_groups=mesh['seq'=16,'tp'=2] {'tp'}, use_global_device_ids=true, to_apply=%region_41.42 | all-reduce | flops 256 | bytes 2048 | tf_op jit(solution)/shard_map/psum | solution.py:138
  302.3 7.6 %all_gather.3 = bf16[256,1024]{1,0:T(8,128)(2,1)S(1)} all-gather(bf16[256,512]{1,0:T(8,128)(2,1)S(1)} %multiply_convert_fusion), channel_id=1, replica_groups=mesh['seq'=16,'tp'=2] {'tp'}, dimensions={1}, use_global_device_ids=true | all-gather | bytes 786432 | tf_op jit(solution)/shard_map/all_gather | solution.py:142
  309.9 1.7 fusion.145
  311.6 4.8 %convolution_convert_fusion = bf16[256,1024]{1,0:T(8,128)(2,1)} fusion(bf16[1024,1024]{1,0:T(8,128)(2,1)} %param.31, bf16[256,1024]{1,0:T(8,128)(2,1)S(1)} %all_gather.3, bf16[1024,1024]{1,0:T(8,128)(2,1)} %param.30, f32[256,1024]{1,0:T(8,128)} %fusion.145), kind=kOutput, calls=%fused_computation.109 | convolution fusion | flops 1075576832 | bytes 6291456 | tf_op jit(solution)/shard_map/dot_general | solution.py:147
  316.4 14.7 %reduce-scatter.5.cloned.1.call-done = bf16[256,512]{1,0:T(8,128)(2,1)} async-done(((bf16[256,1024]{1,0:T(8,128)(2,1)}), bf16[256,512]{1,0:T(8,128)(2,1)}) %reduce-scatter.5.cloned.1.call-update) | async-done | bytes 262160 | tf_op jit(solution)/shard_map/reduce_scatter | solution.py:146
  331.2 1.8 add_convert_fusion
  (553 shorter events, 173.7 us)
Async XLA Ops:
  6.5 303.4 %copy-start = (bf16[1024,1024]{1,0:T(8,128)(2,1)S(1)}, bf16[1024,1024]{1,0:T(8,128)(2,1)}, u32[]{:S(2)}) copy-start(bf16[1024,1024]{1,0:T(8,128)(2,1)} %param.29) | copy-start | bytes 6291460
  6.5 288.5 %reduce-scatter.3.cloned.1.call-start = ((), (), s32[]{:S(2)}) async-start(), calls=%async_computation.2 | async-start | bytes 1572864 | tf_op jit(solution)/shard_map/reduce_scatter | solution.py:135
  11.9 8.5 %copy-start.3 = (bf16[256,512]{1,0:T(8,128)(2,1)S(1)}, bf16[256,512]{1,0:T(8,128)(2,1)}, u32[]{:S(2)}) copy-start(bf16[256,512]{1,0:T(8,128)(2,1)} %param.23) | copy-start | bytes 786436
  14.0 6.7 %copy-start.1 = (bf16[256,512]{1,0:T(8,128)(2,1)S(1)}, bf16[256,512]{1,0:T(8,128)(2,1)}, u32[]{:S(2)}) copy-start(bf16[256,512]{1,0:T(8,128)(2,1)} %param.24) | copy-start | bytes 786436
  14.0 7.7 %copy-start.2 = (bf16[256,512]{1,0:T(8,128)(2,1)S(1)}, bf16[256,512]{1,0:T(8,128)(2,1)}, u32[]{:S(2)}) copy-start(bf16[256,512]{1,0:T(8,128)(2,1)} %param.25) | copy-start | bytes 786436
  19.9 106.8 %collective-permute-start.1 = (bf16[1,128,1024]{1,2,0:T(8,128)(2,1)}, bf16[1,128,1024]{1,2,0:T(8,128)(2,1)}, u32[]{:S(2)}, u32[]{:S(2)}) collective-permute-start(bf16[1,128,1024]{1,2,0:T(8,128)(2,1)} %maximum_bitcast_fusion.1), channel_id=1, source_target_pairs={{0,2},{2,0},{4,6},{6,4},{8,10},{10,8},{12,14},{14,12},{16,18},{18,... | collective-permute-start | bytes 786440 | tf_op jit(solution)/shard_map/ppermute | solution.py:21
  28.9 58.6 %collective-permute-start.3 = (bf16[1,64,1024]{2,1,0:T(8,128)(2,1)}, bf16[1,64,1024]{2,1,0:T(8,128)(2,1)}, u32[]{:S(2)}, u32[]{:S(2)}) collective-permute-start(bf16[1,64,1024]{2,1,0:T(8,128)(2,1)} %maximum_bitcast_fusion.3), channel_id=1, source_target_pairs={{0,2},{2,0},{4,6},{6,4},{8,10},{10,8},{12,14},{14,12},{16,18},{18,... | collective-permute-start | bytes 393224 | tf_op jit(solution)/shard_map/ppermute | solution.py:21
  37.2 44.4 %collective-permute-start.6 = (bf16[1,32,1024]{2,1,0:T(8,128)(2,1)}, bf16[1,32,1024]{2,1,0:T(8,128)(2,1)}, u32[]{:S(2)}, u32[]{:S(2)}) collective-permute-start(bf16[1,32,1024]{2,1,0:T(8,128)(2,1)} %maximum_bitcast_fusion.4), channel_id=1, source_target_pairs={{0,2},{2,0},{4,6},{6,4},{8,10},{10,8},{12,14},{14,12},{16,18},{18,... | collective-permute-start | bytes 196616 | tf_op jit(solution)/shard_map/ppermute | solution.py:21
  38.5 126.2 %collective-permute-start = (bf16[1,256,1024]{2,1,0:T(8,128)(2,1)}, bf16[1,256,1024]{2,1,0:T(8,128)(2,1)}, u32[]{:S(2)}, u32[]{:S(2)}) collective-permute-start(bf16[1,256,1024]{2,1,0:T(8,128)(2,1)} %maximum_bitcast_fusion), channel_id=1, source_target_pairs={{0,2},{2,0},{4,6},{6,4},{8,10},{10,8},{12,14},{14,12},{16,18},{18,... | collective-permute-start | bytes 1572872 | tf_op jit(solution)/shard_map/ppermute | solution.py:21
  46.2 27.6 %collective-permute-start.14 = (bf16[1,8,1024]{2,1,0:T(8,128)(2,1)}, bf16[1,8,1024]{2,1,0:T(8,128)(2,1)}, u32[]{:S(2)}, u32[]{:S(2)}) collective-permute-start(bf16[1,8,1024]{2,1,0:T(8,128)(2,1)} %maximum_bitcast_fusion.6), channel_id=1, source_target_pairs={{0,2},{2,0},{4,6},{6,4},{8,10},{10,8},{12,14},{14,12},{16,18},{18,... | collective-permute-start | bytes 49160 | tf_op jit(solution)/shard_map/ppermute | solution.py:21
  54.7 12.6 %copy-start.62 = (pred[4,8]{1,0:T(4,128)(4,1)S(1)}, pred[4,8]{1,0:T(4,128)(4,1)}, u32[]{:S(2)}) copy-start(pred[4,8]{1,0:T(4,128)(4,1)} %get-tuple-element.697) | copy-start | bytes 100
  54.7 13.3 %copy-start.54 = (pred[16,8]{1,0:T(8,128)(4,1)S(1)}, pred[16,8]{1,0:T(8,128)(4,1)}, u32[]{:S(2)}) copy-start(pred[16,8]{1,0:T(8,128)(4,1)} %get-tuple-element.703) | copy-start | bytes 388
  54.7 14.0 %copy-start.35 = (bf16[8,8,64]{2,1,0:T(8,128)(2,1)S(1)}, bf16[8,8,64]{2,1,0:T(8,128)(2,1)}, u32[]{:S(2)}) copy-start(bf16[8,8,64]{2,1,0:T(8,128)(2,1)} %get-tuple-element.517) | copy-start | bytes 24580
  54.7 14.7 %copy-start.49 = (pred[32,8]{1,0:T(8,128)(4,1)S(1)}, pred[32,8]{1,0:T(8,128)(4,1)}, u32[]{:S(2)}) copy-start(pred[32,8]{1,0:T(8,128)(4,1)} %get-tuple-element.706) | copy-start | bytes 772
  54.7 15.4 %copy-start.50 = (f32[8,8]{0,1:T(8,128)S(1)}, f32[8,8]{0,1:T(8,128)}, u32[]{:S(2)}) copy-start(f32[8,8]{0,1:T(8,128)} %get-tuple-element.698) | copy-start | bytes 772
  54.7 16.1 %copy-start.53 = (f32[4,8]{1,0:T(4,128)S(1)}, f32[4,8]{1,0:T(4,128)}, u32[]{:S(2)}) copy-start(f32[4,8]{1,0:T(4,128)} %get-tuple-element.695) | copy-start | bytes 388
  54.7 16.8 %copy-start.56 = (f32[2,8]{1,0:T(2,128)S(1)}, f32[2,8]{1,0:T(2,128)}, u32[]{:S(2)}) copy-start(f32[2,8]{1,0:T(2,128)} %get-tuple-element.692) | copy-start | bytes 196
  54.7 17.5 %copy-start.43 = (f32[16,8]{1,0:T(8,128)S(1)}, f32[16,8]{1,0:T(8,128)}, u32[]{:S(2)}) copy-start(f32[16,8]{1,0:T(8,128)} %get-tuple-element.701) | copy-start | bytes 1540
  54.7 18.3 %copy-start.36 = (f32[32,8]{1,0:T(8,128)S(1)}, f32[32,8]{1,0:T(8,128)}, u32[]{:S(2)}) copy-start(f32[32,8]{1,0:T(8,128)} %get-tuple-element.704) | copy-start | bytes 3076
  54.8 28.5 %copy-start.31 = (bf16[32,512]{1,0:T(8,128)(2,1)S(1)}, bf16[32,512]{1,0:T(8,128)(2,1)}, u32[]{:S(2)}) copy-start(bf16[32,512]{1,0:T(8,128)(2,1)} %copy-done.30) | copy-start | bytes 98308
  54.8 28.5 %copy-start.33 = (bf16[32,512]{1,0:T(8,128)(2,1)S(1)}, bf16[32,512]{1,0:T(8,128)(2,1)}, u32[]{:S(2)}) copy-start(bf16[32,512]{1,0:T(8,128)(2,1)} %copy-done.32) | copy-start | bytes 98308
  60.1 30.1 %copy-start.27 = (bf16[64,512]{1,0:T(8,128)(2,1)S(1)}, bf16[64,512]{1,0:T(8,128)(2,1)}, u32[]{:S(2)}) copy-start(bf16[64,512]{1,0:T(8,128)(2,1)} %copy-done.26) | copy-start | bytes 196612
  60.1 30.1 %copy-start.29 = (bf16[64,512]{1,0:T(8,128)(2,1)S(1)}, bf16[64,512]{1,0:T(8,128)(2,1)}, u32[]{:S(2)}) copy-start(bf16[64,512]{1,0:T(8,128)(2,1)} %copy-done.28) | copy-start | bytes 196612
  73.8 1.2 collective-permute-start.10
  75.0 4.6 %collective-permute-start.15 = (bf16[2,8,1024]{2,1,0:T(8,128)(2,1)S(1)}, bf16[2,8,1024]{2,1,0:T(8,128)(2,1)S(1)}, u32[]{:S(2)}, u32[]{:S(2)}) collective-permute-start(bf16[2,8,1024]{2,1,0:T(8,128)(2,1)S(1)} %pad_maximum_fusion.16), channel_id=1, source_target_pairs={{0,4},{4,0},{2,6},{6,2},{8,12},{12,8},{10,14},{14,10},{16,20},{20,... | collective-permute-start | bytes 98312 | tf_op jit(solution)/shard_map/ppermute | solution.py:21
  79.6 4.6 %collective-permute-start.11 = (bf16[2,16,1024]{2,1,0:T(8,128)(2,1)S(1)}, bf16[2,16,1024]{2,1,0:T(8,128)(2,1)S(1)}, u32[]{:S(2)}, u32[]{:S(2)}) collective-permute-start(bf16[2,16,1024]{2,1,0:T(8,128)(2,1)S(1)} %pad_maximum_fusion.14), channel_id=1, source_target_pairs={{0,4},{4,0},{2,6},{6,2},{8,12},{12,8},{10,14},{14,10},{16,20},{20,... | collective-permute-start | bytes 196616 | tf_op jit(solution)/shard_map/ppermute | solution.py:21
  81.6 4.3 %collective-permute-start.16 = (bf16[4,8,1024]{2,1,0:T(8,128)(2,1)S(1)}, bf16[4,8,1024]{2,1,0:T(8,128)(2,1)S(1)}, u32[]{:S(2)}, u32[]{:S(2)}) collective-permute-start(bf16[4,8,1024]{2,1,0:T(8,128)(2,1)S(1)} %pad_maximum_fusion.15), channel_id=1, source_target_pairs={{0,8},{8,0},{2,10},{10,2},{4,12},{12,4},{6,14},{14,6},{16,24},{24,... | collective-permute-start | bytes 196616 | tf_op jit(solution)/shard_map/ppermute | solution.py:21
  84.2 7.8 %collective-permute-start.7 = (bf16[2,32,1024]{2,1,0:T(8,128)(2,1)S(1)}, bf16[2,32,1024]{2,1,0:T(8,128)(2,1)S(1)}, u32[]{:S(2)}, u32[]{:S(2)}) collective-permute-start(bf16[2,32,1024]{2,1,0:T(8,128)(2,1)S(1)} %pad_maximum_fusion.11), channel_id=1, source_target_pairs={{0,4},{4,0},{2,6},{6,2},{8,12},{12,8},{10,14},{14,10},{16,20},{20,... | collective-permute-start | bytes 393224 | tf_op jit(solution)/shard_map/ppermute | solution.py:21
  85.9 7.3 %collective-permute-start.12 = (bf16[4,16,1024]{2,1,0:T(8,128)(2,1)S(1)}, bf16[4,16,1024]{2,1,0:T(8,128)(2,1)S(1)}, u32[]{:S(2)}, u32[]{:S(2)}) collective-permute-start(bf16[4,16,1024]{2,1,0:T(8,128)(2,1)S(1)} %pad_maximum_fusion.12), channel_id=1, source_target_pairs={{0,8},{8,0},{2,10},{10,2},{4,12},{12,4},{6,14},{14,6},{16,24},{24,... | collective-permute-start | bytes 393224 | tf_op jit(solution)/shard_map/ppermute | solution.py:21
  87.6 7.4 %collective-permute-start.17 = (bf16[8,8,1024]{2,1,0:T(8,128)(2,1)S(1)}, bf16[8,8,1024]{2,1,0:T(8,128)(2,1)S(1)}, u32[]{:S(2)}, u32[]{:S(2)}) collective-permute-start(bf16[8,8,1024]{2,1,0:T(8,128)(2,1)S(1)} %pad_maximum_fusion.13), channel_id=1, source_target_pairs={{0,16},{16,0},{2,18},{18,2},{4,20},{20,4},{6,22},{22,6},{8,24},{24... | collective-permute-start | bytes 393224 | tf_op jit(solution)/shard_map/ppermute | solution.py:21
  91.2 6.9 %copy-start.15 = (bf16[1,64,1024]{2,1,0:T(8,128)(2,1)}, bf16[1,64,1024]{2,1,0:T(8,128)(2,1)S(1)}, u32[]{:S(2)}) copy-start(bf16[1,64,1024]{2,1,0:T(8,128)(2,1)S(1)} %get-tuple-element.666) | copy-start | bytes 393220
  92.0 8.9 %copy-start.61 = (f32[8,8]{1,0:T(8,128)S(1)}, f32[8,8]{1,0:T(8,128)}, u32[]{:S(2)}) copy-start(f32[8,8]{1,0:T(8,128)} %custom-call.11) | copy-start | bytes 772
  92.0 8.9 %copy-start.67 = (s32[8]{0:T(128)S(1)}, s32[8]{0:T(128)}, u32[]{:S(2)}) copy-start(s32[8]{0:T(128)} %iota_add_fusion.1) | copy-start | bytes 100
  92.0 38.7 %collective-permute-start.4 = (bf16[2,64,1024]{2,1,0:T(8,128)(2,1)}, bf16[2,64,1024]{2,1,0:T(8,128)(2,1)}, u32[]{:S(2)}, u32[]{:S(2)}) collective-permute-start(bf16[2,64,1024]{2,1,0:T(8,128)(2,1)} %pad_maximum_fusion.8), channel_id=1, source_target_pairs={{0,4},{4,0},{2,6},{6,2},{8,12},{12,8},{10,14},{14,10},{16,20},{20,... | collective-permute-start | bytes 786440 | tf_op jit(solution)/shard_map/ppermute | solution.py:21
  92.5 8.3 %copy-start.17 = (bf16[2,32,1024]{2,1,0:T(8,128)(2,1)}, bf16[2,32,1024]{2,1,0:T(8,128)(2,1)S(1)}, u32[]{:S(2)}) copy-start(bf16[2,32,1024]{2,1,0:T(8,128)(2,1)S(1)} %get-tuple-element.667) | copy-start | bytes 393220
  92.5 8.3 %copy-start.19 = (bf16[2,32,1024]{2,1,0:T(8,128)(2,1)}, bf16[2,32,1024]{2,1,0:T(8,128)(2,1)S(1)}, u32[]{:S(2)}) copy-start(bf16[2,32,1024]{2,1,0:T(8,128)(2,1)S(1)} %get-tuple-element.668) | copy-start | bytes 393220
  93.3 39.4 %collective-permute-start.8 = (bf16[4,32,1024]{2,1,0:T(8,128)(2,1)}, bf16[4,32,1024]{2,1,0:T(8,128)(2,1)}, u32[]{:S(2)}, u32[]{:S(2)}) collective-permute-start(bf16[4,32,1024]{2,1,0:T(8,128)(2,1)} %pad_maximum_fusion.9), channel_id=1, source_target_pairs={{0,8},{8,0},{2,10},{10,2},{4,12},{12,4},{6,14},{14,6},{16,24},{24,... | collective-permute-start | bytes 786440 | tf_op jit(solution)/shard_map/ppermute | solution.py:21
  93.8 7.1 %copy-start.23 = (bf16[4,16,1024]{2,1,0:T(8,128)(2,1)}, bf16[4,16,1024]{2,1,0:T(8,128)(2,1)S(1)}, u32[]{:S(2)}) copy-start(bf16[4,16,1024]{2,1,0:T(8,128)(2,1)S(1)} %get-tuple-element.670) | copy-start | bytes 393220
  93.8 29.4 %copy-start.21 = (bf16[4,16,1024]{2,1,0:T(8,128)(2,1)}, bf16[4,16,1024]{2,1,0:T(8,128)(2,1)S(1)}, u32[]{:S(2)}) copy-start(bf16[4,16,1024]{2,1,0:T(8,128)(2,1)S(1)} %get-tuple-element.669) | copy-start | bytes 393220
  95.0 40.9 %collective-permute-start.13 = (bf16[8,16,1024]{2,1,0:T(8,128)(2,1)}, bf16[8,16,1024]{2,1,0:T(8,128)(2,1)}, u32[]{:S(2)}, u32[]{:S(2)}) collective-permute-start(bf16[8,16,1024]{2,1,0:T(8,128)(2,1)} %pad_maximum_fusion.10), channel_id=1, source_target_pairs={{0,16},{16,0},{2,18},{18,2},{4,20},{20,4},{6,22},{22,6},{8,24},{24... | collective-permute-start | bytes 786440 | tf_op jit(solution)/shard_map/ppermute | solution.py:21
  122.2 4.5 %copy-start.14 = (bf16[128,8,64]{0,2,1:T(8,128)(2,1)S(1)}, bf16[128,8,64]{0,2,1:T(8,128)(2,1)}, u32[]{:S(2)}) copy-start(bf16[128,8,64]{0,2,1:T(8,128)(2,1)} %copy-done.13) | copy-start | bytes 393220
  126.7 5.9 %copy-start.18 = (bf16[2,32,1024]{2,1,0:T(8,128)(2,1)S(1)}, bf16[2,32,1024]{2,1,0:T(8,128)(2,1)}, u32[]{:S(2)}) copy-start(bf16[2,32,1024]{2,1,0:T(8,128)(2,1)} %copy-done.17) | copy-start | bytes 393220
  126.7 6.0 %copy-start.20 = (bf16[2,32,1024]{2,1,0:T(8,128)(2,1)S(1)}, bf16[2,32,1024]{2,1,0:T(8,128)(2,1)}, u32[]{:S(2)}) copy-start(bf16[2,32,1024]{2,1,0:T(8,128)(2,1)} %copy-done.19) | copy-start | bytes 393220
  127.8 4.8 %copy-start.9 = (bf16[1,128,1024]{1,2,0:T(8,128)(2,1)}, bf16[1,128,1024]{1,2,0:T(8,128)(2,1)S(1)}, u32[]{:S(2)}) copy-start(bf16[1,128,1024]{1,2,0:T(8,128)(2,1)S(1)} %get-tuple-element.656) | copy-start | bytes 786436
  128.8 7.2 %copy-start.22 = (bf16[4,16,1024]{2,1,0:T(8,128)(2,1)S(1)}, bf16[4,16,1024]{2,1,0:T(8,128)(2,1)}, u32[]{:S(2)}) copy-start(bf16[4,16,1024]{2,1,0:T(8,128)(2,1)} %copy-done.21) | copy-start | bytes 393220
  128.8 7.2 %copy-start.24 = (bf16[4,16,1024]{2,1,0:T(8,128)(2,1)S(1)}, bf16[4,16,1024]{2,1,0:T(8,128)(2,1)}, u32[]{:S(2)}) copy-start(bf16[4,16,1024]{2,1,0:T(8,128)(2,1)} %copy-done.23) | copy-start | bytes 393220
  128.8 67.2 %collective-permute-start.2 = (bf16[2,128,1024]{1,2,0:T(8,128)(2,1)}, bf16[2,128,1024]{1,2,0:T(8,128)(2,1)}, u32[]{:S(2)}, u32[]{:S(2)}) collective-permute-start(bf16[2,128,1024]{1,2,0:T(8,128)(2,1)} %pad_maximum_fusion.4), channel_id=1, source_target_pairs={{0,4},{4,0},{2,6},{6,2},{8,12},{12,8},{10,14},{14,10},{16,20},{20,... | collective-permute-start | bytes 1572872 | tf_op jit(solution)/shard_map/ppermute | solution.py:21
  131.7 5.3 %copy-start.7 = (bf16[2,64,1024]{2,1,0:T(8,128)(2,1)}, bf16[2,64,1024]{2,1,0:T(8,128)(2,1)S(1)}, u32[]{:S(2)}) copy-start(bf16[2,64,1024]{2,1,0:T(8,128)(2,1)S(1)} %get-tuple-element.657) | copy-start | bytes 786436
  131.7 5.3 %copy-start.8 = (bf16[2,64,1024]{2,1,0:T(8,128)(2,1)}, bf16[2,64,1024]{2,1,0:T(8,128)(2,1)S(1)}, u32[]{:S(2)}) copy-start(bf16[2,64,1024]{2,1,0:T(8,128)(2,1)S(1)} %get-tuple-element.658) | copy-start | bytes 786436
  132.6 94.1 %collective-permute-start.5 = (bf16[4,64,1024]{2,1,0:T(8,128)(2,1)}, bf16[4,64,1024]{2,1,0:T(8,128)(2,1)}, u32[]{:S(2)}, u32[]{:S(2)}) collective-permute-start(bf16[4,64,1024]{2,1,0:T(8,128)(2,1)} %pad_maximum_fusion.5), channel_id=1, source_target_pairs={{0,8},{8,0},{2,10},{10,2},{4,12},{12,4},{6,14},{14,6},{16,24},{24,... | collective-permute-start | bytes 1572872 | tf_op jit(solution)/shard_map/ppermute | solution.py:21
  133.7 4.2 %copy-start.6 = (bf16[4,32,1024]{2,1,0:T(8,128)(2,1)}, bf16[4,32,1024]{2,1,0:T(8,128)(2,1)S(1)}, u32[]{:S(2)}) copy-start(bf16[4,32,1024]{2,1,0:T(8,128)(2,1)S(1)} %get-tuple-element.660) | copy-start | bytes 786436
  134.6 6.9 %copy-start.37 = (f32[8,16,64]{2,1,0:T(8,128)S(1)}, f32[8,16,64]{2,1,0:T(8,128)}, u32[]{:S(2)}) copy-start(f32[8,16,64]{2,1,0:T(8,128)} %custom-call.8) | copy-start | bytes 98308
  134.6 6.9 %copy-start.60 = (f32[8,16]{1,0:T(8,128)S(1)}, f32[8,16]{1,0:T(8,128)}, u32[]{:S(2)}) copy-start(f32[8,16]{1,0:T(8,128)} %custom-call.9) | copy-start | bytes 1540
  134.6 6.9 %copy-start.66 = (s32[16]{0:T(128)S(1)}, s32[16]{0:T(128)}, u32[]{:S(2)}) copy-start(s32[16]{0:T(128)} %iota_add_fusion.2) | copy-start | bytes 196
  134.6 116.8 %collective-permute-start.9 = (bf16[8,32,1024]{2,1,0:T(8,128)(2,1)}, bf16[8,32,1024]{2,1,0:T(8,128)(2,1)}, u32[]{:S(2)}, u32[]{:S(2)}) collective-permute-start(bf16[8,32,1024]{2,1,0:T(8,128)(2,1)} %pad_maximum_fusion.6), channel_id=1, source_target_pairs={{0,16},{16,0},{2,18},{18,2},{4,20},{20,4},{6,22},{22,6},{8,24},{24... | collective-permute-start | bytes 1572872 | tf_op jit(solution)/shard_map/ppermute | solution.py:21
  170.0 25.9 %copy-start.10 = (bf16[1,128,1024]{1,2,0:T(8,128)(2,1)S(1)}, bf16[1,128,1024]{1,2,0:T(8,128)(2,1)}, u32[]{:S(2)}) copy-start(bf16[1,128,1024]{1,2,0:T(8,128)(2,1)} %copy-done.9) | copy-start | bytes 786436
  267.0 4.5 %copy-start.38 = (f32[256,8]{0,1:T(8,128)S(1)}, f32[256,8]{0,1:T(8,128)}, u32[]{:S(2)}) copy-start(f32[256,8]{0,1:T(8,128)} %mul.481) | copy-start | bytes 24580
  267.0 4.5 %copy-start.39 = (f32[256,8]{0,1:T(8,128)S(1)}, f32[256,8]{0,1:T(8,128)}, u32[]{:S(2)}) copy-start(f32[256,8]{0,1:T(8,128)} %copy.219) | copy-start | bytes 24580
  267.0 4.5 %copy-start.40 = (f32[256,8]{0,1:T(8,128)S(1)}, f32[256,8]{0,1:T(8,128)}, u32[]{:S(2)}) copy-start(f32[256,8]{0,1:T(8,128)} %copy.205) | copy-start | bytes 24580
  267.0 4.5 %copy-start.41 = (f32[256,8]{0,1:T(8,128)S(1)}, f32[256,8]{0,1:T(8,128)}, u32[]{:S(2)}) copy-start(f32[256,8]{0,1:T(8,128)} %mul.499) | copy-start | bytes 24580
  267.0 4.5 %copy-start.42 = (f32[256,8]{0,1:T(8,128)S(1)}, f32[256,8]{0,1:T(8,128)}, u32[]{:S(2)}) copy-start(f32[256,8]{0,1:T(8,128)} %mul.517) | copy-start | bytes 24580
  273.4 21.7 %copy-start.5 = (bf16[256,512]{1,0:T(8,128)(2,1)S(1)}, bf16[256,512]{1,0:T(8,128)(2,1)}, u32[]{:S(2)}) copy-start(bf16[256,512]{1,0:T(8,128)(2,1)} %param.22) | copy-start | bytes 786436
  274.9 56.3 %reduce-scatter.5.cloned.1.call-start = ((), (), s32[]{:S(2)}) async-start(), calls=%async_computation.3 | async-start | bytes 786432 | tf_op jit(solution)/shard_map/reduce_scatter | solution.py:146
  311.6 19.6 %copy-start.4 = (f32[256,512]{1,0:T(8,128)S(1)}, f32[256,512]{1,0:T(8,128)}, u32[]{:S(2)}) copy-start(f32[256,512]{1,0:T(8,128)} %reduce-scatter.3.cloned.1.call-done) | copy-start | bytes 1572868
  (24 other events, 63.0 us)
Sparse Core Ops, SparseCore 0:
  275.0 20.0 reduce-scatter.2
  316.6 14.5 reduce-scatter.4
where the time goes:
time: 346 us; the launch traced here: 340 us
  matrix products  108 us (31%)
  local copies, waits for them, and re-layouts  86.4 us (25%)
  other arithmetic  59.7 us (17%)
  waiting for transfers between devices  37.6 us (11%)
  starting transfers between devices  20.3 us (6%)
  between operations  14.5 us (4%)
  blocking collectives  12.5 us (4%)
    dot_general x48, matrix products, attend(): jnp.dot(query, key_block.T, preferred_element_type=jnp.float32) * scale  50.6 us
    dot_general x48, matrix products, attend(): output = jnp.dot(weights, value_block, preferred_element_type=jnp.float32)  49.1 us
    mul x25, local copies, waits for them, and re-layouts, shards(): outputs.transpose(1, 0, 2)[:, None] * chosen[None, :, :, None]  23 us
    ppermute x18, starting transfers between devices, from_partner(): return lax.ppermute(block, axis, route)  20.3 us
    reduce_scatter x1, waiting for transfers between devices, shards(): lax.psum_scatter(partial_value, 'tp', scatter_dimension=1, tiled=True)  20 us
    another operation x15, local copies, waits for them, and re-layouts, pick_rows(): shaped = array.reshape(count, rate, array.shape[1], array.shape[2])  15.1 us
    reduce_scatter x1, waiting for transfers between devices, shards(): lax.psum_scatter(jnp.dot(act, down_weight, preferred_element_type=jnp.flo...  14.7 us
    reduce_sum x5, other arithmetic, pick_rows(): jnp.sum(shaped * choose[None, :, :, None].astype(array.dtype), axis=1)  12.7 us
  transfers between devices with their start and end apart: 20, of which 6 were waited for; matrix products, arithmetic and copies ran while one was open for 61% of the time, Pallas kernels for 0%

commit v1 on v0

v1 whole, which is shorter than its diff:
```python
import functools
import math

import jax
import jax.numpy as jnp
from jax import lax
from jax.experimental import pallas as pl
from jax.experimental.pallas import tpu as pltpu
from jax.sharding import PartitionSpec as P

BRANCHES = 6
LANES = 128
NEAR = 4
GROUP = LANES // NEAR
PEAK_FLOPS = 1153.5e12
MIB = 1024 * 1024
CHUNKS = 2

masked_score = -1e30


def part_rows(rows, branches):
    first, at = 0, {}
    for branch in branches:
        at[branch] = first
        first += rows // 2**branch
    return at, first


def far_sets(seq_count, rows):
    top_bits = min(seq_count.bit_length() - 1, BRANCHES)
    sets = {}
    for branch in range(2, BRANCHES):
        sets.setdefault(2 ** min(branch + 1, top_bits) // NEAR, []).append(branch)
    return sorted(sets.items())


def set_rows(sets, rows, each):
    first, at = 0, []
    for _, branches in sets:
        at.append(first)
        first += each * sum(rows // 2**branch for branch in branches)
    return at, first


def first_set(sets, step):
    return min(number for number, (span, _) in enumerate(sets) if span > step)


def even(count):
    return -(-count // 16) * 16


def mask_select(rows, branch, offset):
    rate = 2**branch
    count = rows // rate
    row = lax.broadcasted_iota(jnp.int32, (count, rows), 0)
    col = lax.broadcasted_iota(jnp.int32, (count, rows), 1)
    return jnp.where(col == row * rate + (offset & (rate - 1)), 1.0, 0.0)


def selection(rows, branches, offset_ref, head):
    select = [mask_select(rows, branch, offset_ref[branch, head]) for branch in branches]
    return jnp.concatenate(select, axis=0).astype(jnp.bfloat16)


def far_picks(sets, rows, dim, low, offset_ref, blocks, members):
    each = LANES // dim
    far_branches = range(2, BRANCHES)
    starts, _ = part_rows(rows, far_branches)
    picked = []
    for (key, value), member in zip(blocks, members):
        for head in range(each):
            lanes = slice(head * dim, (head + 1) * dim)
            select = selection(rows, far_branches, offset_ref, member * each + head)
            pairs = jnp.concatenate([key[:, lanes], value[:, lanes]], axis=1)
            picked.append(jnp.dot(select, pairs, preferred_element_type=jnp.float32))
    outs = []
    for number in range(len(blocks)):
        parts = []
        for _, branches in sets:
            for branch in branches:
                first, last = starts[branch], starts[branch] + rows // 2**branch
                parts += [picked[number * each + head][first:last] for head in range(each)]
        outs.append(jnp.concatenate(parts, axis=0).astype(jnp.bfloat16))
    return outs


def split_kernel(sets, scale, dim, offset_ref, index_ref, source_ref, *out_refs):
    wide_refs, own_ref, core_ref, chip_ref = out_refs[:2], *out_refs[2:]
    rows = source_ref.shape[0] // 3
    low = index_ref[0] % NEAR
    all_lanes = [
        pl.ds(pl.multiple_of((low ^ side) * LANES, LANES), LANES) for side in range(NEAR)
    ]
    blocks = [
        (source_ref[rows : 2 * rows, lanes], source_ref[2 * rows :, lanes]) for lanes in all_lanes[2:]
    ]
    picks = far_picks(sets, rows, dim, low, offset_ref, blocks, [low ^ 2, low ^ 3])
    for pick, wide_ref in zip(picks, wide_refs):
        wide_ref[...] = pick
    for side, lanes in enumerate(all_lanes):
        ref, first = ((own_ref, 0), (core_ref, 0), (chip_ref, 0), (core_ref, 3 * rows))[side]
        ref[first : first + rows] = source_ref[:rows, lanes] * jnp.asarray(scale, jnp.bfloat16)
        ref[first + rows : first + 3 * rows] = source_ref[rows:, lanes]


def turn_kernel(at, index_ref, *refs):
    in_refs, chip_ref, core_ref, out_refs, relay_ref = refs[:NEAR], *refs[NEAR : NEAR + 2], refs[NEAR + 2 : -1], refs[-1]
    half = chip_ref.shape[0]
    relay_ref[:half] = chip_ref[...]
    relay_ref[half:] = core_ref[half:]
    low = index_ref[0] % NEAR
    for side in range(NEAR):
        for first, out_ref in zip(at, out_refs):
            out_ref[low ^ side] = in_refs[side][first:, :]


def attend(jobs, batch):
    dim = jobs[0][0].shape[1]
    lane = lax.broadcasted_iota(jnp.int32, (1, LANES), 1)
    keys = [pairs[:, :dim] for _, pairs, _, _ in jobs]
    values = [jnp.where(lane < dim, jnp.ones_like(pairs), pairs) for _, pairs, _, _ in jobs]
    pieces = []
    for number, (query, _, _, _) in enumerate(jobs):
        block = min(128, query.shape[0])
        pieces += [(start, number, block) for start in range(0, query.shape[0], block)]
    pieces.sort(key=lambda piece: piece[0])
    done = {}
    for at in range(0, len(pieces), batch):
        now = pieces[at : at + batch]
        scores = []
        for start, number, block in now:
            query, _, before, _ = jobs[number]
            scores.append(
                lax.dot_general(
                    query[start : start + block],
                    keys[number][: before + start + block],
                    (((1,), (1,)), ((), ())),
                    preferred_element_type=jnp.float32,
                )
            )
        masked = []
        for (start, number, block), score in zip(now, scores):
            _, _, before, columns = jobs[number]
            end = before + start + block
            if before == 0 and block == 128:
                row = lax.broadcasted_iota(jnp.int32, (block, block), 0)
                col = lax.broadcasted_iota(jnp.int32, (block, block), 1)
                last = jnp.where(col <= row, score[:, start:], masked_score)
                masked.append(jnp.concatenate([score[:, :start], last], axis=1) if start else last)
            else:
                row = lax.broadcasted_iota(jnp.int32, (block, end), 0)
                allowed = columns[:, :end] <= row + (before + start)
                masked.append(jnp.where(allowed, score, masked_score))
        tops = [jnp.max(score, axis=1, keepdims=True) for score in masked]
        weights = [jnp.exp(score - top).astype(jnp.bfloat16) for score, top in zip(masked, tops)]
        for piece, weight, top in zip(now, weights, tops):
            start, number, block = piece
            end = jobs[number][2] + start + block
            accum = jnp.dot(weight, values[number][:end], preferred_element_type=jnp.float32)
            done.setdefault(number, []).append((top, accum))
    return [
        tuple(jnp.concatenate(column, axis=0) for column in zip(*done[number]))
        for number in range(len(jobs))
    ]


def top_lanes(top, count, branch):
    length = top.shape[0]
    high = top.astype(jnp.bfloat16).astype(jnp.float32)
    middle = (top - high).astype(jnp.bfloat16).astype(jnp.float32)
    low = top - high - middle
    lane = lax.broadcasted_iota(jnp.int32, (length, LANES), 1)
    row = lax.broadcasted_iota(jnp.int32, (length, LANES), 0)
    lane = lane - ((row >> (count.bit_length() - 1)) * GROUP + 3 * branch)
    parts = jnp.where(lane == 0, high, jnp.where(lane == 1, middle, jnp.where(lane == 2, low, 0.0)))
    return jnp.sum(parts.reshape(NEAR, count, LANES), axis=0)


def nearest(members, rows, dim, low, query, pairs):
    each = LANES // dim
    for side, (query_in, key_in, value_in) in members:
        core = (low ^ side) % 2
        query[core] = query_in
        for head in range(each):
            lanes = slice(head * dim, (head + 1) * dim)
            pairs[head, core] = jnp.concatenate([key_in[:, lanes], value_in[:, lanes]], axis=1)
    return [
        (
            query[:, :, head * dim : (head + 1) * dim].reshape(2 * rows, dim),
            pairs[head].reshape(2 * rows, LANES),
            0,
            None,
        )
        for head in range(each)
    ]


def nearest_out(top, accum):
    lane = lax.broadcasted_iota(jnp.int32, (1, LANES), 1)
    return jnp.where(lane == 0, top, accum).reshape(2, top.shape[0] // 2, LANES)


def raw_blocks(ref, rows, first=0):
    return tuple(ref[first + part * rows : first + (part + 1) * rows] for part in range(3))


def own_chip_kernel(sets, rows, dim, offset_ref, index_ref, own_ref, pair_ref, *refs):
    near_ref, pick_refs, query, pairs = refs[0], refs[1:3], *refs[3:]
    low = index_ref[0] % NEAR
    members = [(side, raw_blocks(ref, rows)) for side, ref in enumerate((own_ref, pair_ref))]
    blocks = [block[1:] for _, block in members]
    for pick, pick_ref in zip(far_picks(sets, rows, dim, low, offset_ref, blocks, [low, low]), pick_refs):
        pick_ref[...] = pick
    jobs = nearest(members, rows, dim, low, query, pairs)
    for head, (top, accum) in enumerate(attend(jobs, 4)):
        near_ref[head] = nearest_out(top, accum)


def local_kernel(rows, dim, offset_ref, index_ref, *refs):
    own_ref, core_ref, chip_ref, own_chip_ref, residual_ref, refs = *refs[:5], refs[5:]
    near_ref, far_ref, top_ref, picked_ref, residual_out = refs[:5]
    query, pairs, tight_pairs, tight_query = refs[5:]
    residual_out[...] = residual_ref[...]
    blocks = [raw_blocks(ref, rows) for ref in (own_ref, core_ref, chip_ref)]
    blocks.append(raw_blocks(chip_ref, rows, 3 * rows))
    each = LANES // dim
    low = index_ref[0] % NEAR
    chip = low // 2
    count = rows // 2
    left = lax.broadcasted_iota(jnp.int32, (1, LANES), 1) < dim
    selects = [
        selection(rows, range(1, BRANCHES), offset_ref, low * each + head) for head in range(each)
    ]
    for side in range(NEAR):
        query_in, key_in, value_in = blocks[side]
        both = [jnp.dot(select, query_in, preferred_element_type=jnp.float32) for select in selects]
        picked = jnp.where(left, both[0], both[1])
        tight_query[low ^ side] = picked[:count].astype(jnp.bfloat16)
        rest = picked[count:]
        rest = [rest, jnp.zeros((picked_ref.shape[1] - rest.shape[0], LANES), jnp.float32)]
        picked_ref[low ^ side] = jnp.concatenate(rest, axis=0).astype(jnp.bfloat16)
        for head in range(each):
            lanes = slice(head * dim, (head + 1) * dim)
            block = jnp.concatenate([key_in[:, lanes], value_in[:, lanes]], axis=1)
            block = jnp.dot(selects[head][:count], block, preferred_element_type=jnp.float32)
            tight_pairs[head, low ^ side] = block.astype(jnp.bfloat16)
    members = [(side, blocks[side]) for side in range(2, NEAR)]
    jobs = nearest(members, rows, dim, low, query, pairs)
    for head in range(each):
        near_ref[head, pl.ds(chip * 2, 2)] = own_chip_ref[head]
        jobs.append(
            (
                tight_query[:, :, head * dim : (head + 1) * dim].reshape(NEAR * count, dim),
                tight_pairs[head].reshape(NEAR * count, LANES),
                0,
                None,
            )
        )
    results = attend(jobs, 4)
    for head in range(each):
        near_ref[head, pl.ds((chip ^ 1) * 2, 2)] = nearest_out(*results[head])
        top, accum = results[each + head]
        far_ref[head] = accum.reshape(NEAR, count, LANES)
        top_ref[head] = top_lanes(top, count, 1)


def far_work(sets, rows, dim, index_ref, far_refs, query_ref, far, tops):
    each = LANES // dim
    group = index_ref[0] // NEAR
    starts, _ = part_rows(rows, range(1, BRANCHES))
    query_at, _ = part_rows(rows, range(2, BRANCHES))
    at, _ = set_rows(sets, rows, each)
    jobs, slots = [], []
    for number, (span, branches) in enumerate(sets):
        place = group % span
        first = at[number]
        for branch in branches:
            count = rows // 2**branch
            length = NEAR * count
            col = lax.broadcasted_iota(jnp.int32, (1, span * length), 1)
            step = span - 1 - (col >> (length.bit_length() - 1))
            columns = jnp.where((step == 0) | ((place ^ step) < place), col, 1 << 30)
            queries = query_ref[:, query_at[branch] : query_at[branch] + even(count), :]
            blocks = []
            for far_step in reversed(range(span)):
                skip = first - at[first_set(sets, far_step)]
                blocks.append(far_refs[far_step][:, skip : skip + each * count, :])
            if count % 16:
                queries = queries.astype(jnp.float32)[:, :count]
                blocks = [block.astype(jnp.float32) for block in blocks]
            for head in range(each):
                pairs = [block[:, head * count : (head + 1) * count].reshape(length, LANES) for block in blocks]
                pairs = jnp.concatenate(pairs, axis=0).astype(jnp.bfloat16)
                query = queries[:, :, head * dim : (head + 1) * dim].reshape(length, dim)
                jobs.append((query.astype(jnp.bfloat16), pairs, (span - 1) * length, columns))
                slots.append((branch, head, count))
            first += each * count
    for (branch, head, count), (top, accum) in zip(slots, attend(jobs, 2 * len(jobs))):
        into = slice(starts[branch], starts[branch] + count)
        far[head, :, into, :] = accum.reshape(NEAR, count, LANES)
        tops[head, into, :] = top_lanes(top, count, branch)


def hold_kernel(block_ref, ahead_ref, out_ref):
    out_ref[...] = block_ref[...]


def finish_kernel(sets, rows, dim, offset_ref, index_ref, *refs):
    steps = max(span for span, _ in sets)
    far_refs, refs = refs[:steps], refs[steps:]
    query_ref, near_ref, tight_ref, tight_top_ref, refs = *refs[:4], refs[4:]
    out_refs, far, tops, mixed_ref = refs[:NEAR], *refs[NEAR:]
    each = LANES // dim
    low = index_ref[0] % NEAR
    starts, used = part_rows(rows, range(1, BRANCHES))
    tight = rows // 2
    for head in range(each):
        far[head, :, :tight, :] = tight_ref[head]
        far[head, :, used:, :] = jnp.zeros((NEAR, rows - used, LANES), jnp.float32)
        tops[head, :tight, :] = tight_top_ref[head]
        tops[head, used:, :] = jnp.zeros((rows - used, LANES), jnp.float32)
    far_work(sets, rows, dim, index_ref, far_refs, query_ref, far, tops)

    lane = lax.broadcasted_iota(jnp.int32, (1, LANES), 1)
    inside = lane % GROUP
    column = lax.broadcasted_iota(jnp.int32, (1, rows), 1)
    row = lax.broadcasted_iota(jnp.int32, (rows, 1), 0)
    row_wide = lax.broadcasted_iota(jnp.int32, (rows, rows), 0)
    column_wide = lax.broadcasted_iota(jnp.int32, (rows, rows), 1)
    row_lane = lax.broadcasted_iota(jnp.int32, (rows, LANES), 0)

    def along(start_of, value_of, fill):
        result = jnp.full(start_of.shape, fill, jnp.int32)
        for branch in range(1, BRANCHES):
            result = jnp.where(start_of >= starts[branch], value_of(branch), result)
        return result

    masks = jnp.zeros((1, LANES), jnp.int32)
    for branch in range(1, BRANCHES):
        masks = jnp.where(inside == 3 * branch, 2**branch - 1, masks)
    own_lane = along(row, lambda branch: 3 * branch, 0)

    def turned(array, lanes):
        return pltpu.roll(array, lanes % LANES, 1)

    heads = range(each)
    spreads, gathers, covered = [], [], []
    for head in heads:
        offsets = {
            branch: offset_ref[branch, low * each + head] & (2**branch - 1)
            for branch in range(1, BRANCHES)
        }
        chosen = jnp.where(inside == 0, 0, 1)
        for branch in range(1, BRANCHES):
            chosen = jnp.where(inside == 3 * branch, offsets[branch], chosen)

        def position_of(slot):
            rate = along(slot, lambda branch: 2**branch, 0)
            inner = slot - along(slot, lambda branch: starts[branch], 0)
            return inner * rate + along(slot, lambda branch: offsets[branch], 0)

        spreads.append(jnp.where(row_wide == position_of(column), 1.0, 0.0).astype(jnp.bfloat16))
        gathers.append(jnp.where(column_wide == position_of(row), 1.0, 0.0).astype(jnp.bfloat16))
        covered.append((row_lane & masks) == chosen)
    stats = [
        jnp.dot(spreads[head], tops[head].astype(jnp.bfloat16), preferred_element_type=jnp.float32)
        for head in heads
    ]
    stats = [block + turned(block, -1) + turned(block, -2) for block in stats]
    for member in range(NEAR):
        stats = [
            jnp.where(lane == GROUP * member, near_ref[head, member][:, 0:1], stats[head]) for head in heads
        ]
    stats = [jnp.where(covered[head], stats[head], masked_score) for head in heads]
    peaks = stats
    for step in (3, 6, 12):
        peaks = [jnp.maximum(peak, turned(peak, -step)) for peak in peaks]
    peaks = [jnp.where(inside == 0, peak, masked_score) for peak in peaks]
    for step in (3, 6, 12):
        peaks = [jnp.maximum(peak, turned(peak, step)) for peak in peaks]
    weight = [
        jnp.where(block > 0.5 * masked_score, jnp.exp(block - peak), 0.0)
        for block, peak in zip(stats, peaks)
    ]
    weights = [
        jnp.dot(gathers[head], weight[head].astype(jnp.bfloat16), preferred_element_type=jnp.float32)
        for head in heads
    ]
    scaled = [[] for _ in heads]
    for member in range(NEAR):
        for head in heads:
            picked = jnp.where(lane == own_lane + GROUP * member, weights[head], 0.0)
            block = far[head, member] * jnp.sum(picked, axis=1, keepdims=True)
            rest = block - block.astype(jnp.bfloat16).astype(jnp.float32)
            scaled[head].append(jnp.where(lane == 0, rest, block).astype(jnp.bfloat16))
    added = [
        jnp.dot(spreads[head], jnp.concatenate(scaled[head], axis=1), preferred_element_type=jnp.float32)
        for head in heads
    ]
    halves = [[] for _ in heads]
    for member in range(NEAR):
        for head in heads:
            block = added[head][:, member * LANES : (member + 1) * LANES]
            own = weight[head][:, GROUP * member : GROUP * member + 1]
            total = block + own * near_ref[head, member]
            below = total[:, 1:2] + block[:, 0:1]
            halves[head].append(total[:, dim:] * (1.0 / below))
    for member in range(NEAR):
        pair = [mixed[member] for mixed in halves]
        mixed_ref[member] = jnp.concatenate(pair, axis=1).astype(jnp.bfloat16)
    for side in range(NEAR):
        out_refs[side][...] = mixed_ref[low ^ side]


def lay_out(low, block_refs, part, mix_ref):
    for side, ref in enumerate(block_refs):
        lanes = pl.ds(pl.multiple_of((low ^ side) * LANES, LANES), LANES)
        mix_ref[:, lanes] = ref[part, :]


def own_kernel(index_ref, residual_ref, other_residual_ref, weight_ref, *refs):
    block_refs, out_ref, mix_ref = refs[:NEAR], refs[NEAR], refs[NEAR + 1]
    rows, half = residual_ref.shape
    mine = pl.ds(pl.multiple_of(index_ref[1] * half, LANES), half)
    theirs = pl.ds(pl.multiple_of((1 - index_ref[1]) * half, LANES), half)
    lay_out(index_ref[0] % NEAR, block_refs, slice(0, rows), mix_ref)
    out_ref[...] = jnp.dot(mix_ref[...], weight_ref[...], preferred_element_type=jnp.float32)
    out_ref[:, mine] += residual_ref[...].astype(jnp.float32)
    out_ref[:, theirs] += other_residual_ref[...].astype(jnp.float32)


def block_kernel(part, index_ref, own_ref, *refs):
    block_refs, refs = refs[:NEAR], refs[NEAR:]
    first_weight_ref, second_weight_ref, gain_ref, gate_ref, up_ref, down_ref = refs[:6]
    theirs_ref, mine_ref, hidden_ref, act_ref, mix_ref = refs[6:]
    half = theirs_ref.shape[1]
    mine = pl.ds(pl.multiple_of(index_ref[1] * half, LANES), half)
    theirs = pl.ds(pl.multiple_of((1 - index_ref[1]) * half, LANES), half)
    count = first_weight_ref.shape[0]
    core = index_ref[0] % 2
    lay_out(index_ref[0] % NEAR, block_refs, part, mix_ref)
    hidden = own_ref[part, :]
    for place, weight_ref in ((core, first_weight_ref), (1 - core, second_weight_ref)):
        lanes = pl.ds(pl.multiple_of(place * count, LANES), count)
        hidden += jnp.dot(mix_ref[:, lanes], weight_ref[...], preferred_element_type=jnp.float32)
    hidden_ref[...] = hidden
    inverse = lax.rsqrt(jnp.mean(hidden * hidden, axis=1, keepdims=True) + 1e-05)
    normed = (hidden * inverse * gain_ref[...]).astype(jnp.bfloat16)
    step = 256
    for first in range(0, act_ref.shape[1], step):
        gate = jnp.dot(normed, gate_ref[:, first : first + step], preferred_element_type=jnp.float32)
        up = jnp.dot(normed, up_ref[:, first : first + step], preferred_element_type=jnp.float32)
        act_ref[:, first : first + step] = (gate / (1.0 + jnp.exp(-gate)) * up).astype(jnp.bfloat16)
    act = act_ref[...]
    theirs_ref[...] = jnp.dot(act, down_ref[:, theirs], preferred_element_type=jnp.float32).astype(
        jnp.bfloat16
    )
    mine_ref[...] = hidden_ref[:, mine] + jnp.dot(
        act, down_ref[:, mine], preferred_element_type=jnp.float32
    )


def add_kernel(*refs):
    count = (len(refs) - 1) // 2
    out_ref = refs[-1]
    for number in range(count):
        mine, theirs = refs[number], refs[count + number]
        step = mine.shape[0]
        out_ref[number * step : (number + 1) * step, :] = (
            mine[...] + theirs[...].astype(jnp.float32)
        ).astype(out_ref.dtype)


def call(kernel, out_shape, smem, operands, micros, scratch=(), vmem=8):
    specs = [
        pl.BlockSpec(memory_space=pltpu.SMEM if number < smem else pltpu.VMEM)
        for number in range(len(operands))
    ]
    return pl.pallas_call(
        kernel,
        out_shape=out_shape,
        in_specs=specs,
        out_specs=jax.tree.map(lambda _: pl.BlockSpec(memory_space=pltpu.VMEM), out_shape),
        scratch_shapes=list(scratch),
        compiler_params=pltpu.CompilerParams(vmem_limit_bytes=vmem * MIB),
        cost_estimate=pl.CostEstimate(
            flops=int(micros * PEAK_FLOPS / 1e6), bytes_accessed=0, transcendentals=0
        ),
    )(*operands)


def shards(
    residual_in,
    queries,
    keys,
    values,
    head_offset,
    out_weight,
    norm_gain,
    gate_weight,
    up_weight,
    down_weight,
):
    rows, cols = queries.shape
    heads = head_offset.shape[1]
    dim = cols // heads
    each = heads // NEAR
    seq_count = lax.axis_size("seq")
    scale = 1.0 / math.sqrt(dim)
    sets = far_sets(seq_count, rows)
    index = jnp.stack([lax.axis_index("seq"), lax.axis_index("tp")]).astype(jnp.int32)
    bf16 = jnp.bfloat16

    def shape(*sizes, dtype=bf16):
        return jax.ShapeDtypeStruct(sizes, dtype)

    def across(block, distance):
        if distance == 0:
            return block
        return lax.ppermute(block, "seq", [(i, i ^ distance) for i in range(seq_count)])

    swap = [(0, 1), (1, 0)]
    half = out_weight.shape[0] // 2
    part = lax.dynamic_slice_in_dim(out_weight, lax.axis_index("seq") % 2 * half, half)
    part = lax.ppermute(part, "tp", swap)
    other_weights = (part, across(part, 1))

    source = jnp.concatenate([queries, keys, values], axis=0)
    _, tall = part_rows(rows, range(2, BRANCHES))
    first, second, own, core, chip = call(
        functools.partial(split_kernel, sets, scale, dim),
        [shape(each * tall, LANES)] * 2 + [shape(part * rows, LANES) for part in (3, 6, 3)],
        2,
        (head_offset, index, source),
        1.0,
        vmem=12,
    )
    wide = [across(first, 2), across(second, 3)]
    core = across(core, 1)
    own_chip, *picks = call(
        functools.partial(own_chip_kernel, sets, rows, dim),
        [shape(each, 2, rows, LANES, dtype=jnp.float32)] + [shape(each * tall, LANES)] * 2,
        2,
        (head_offset, index, own, core),
        2.0,
        [pltpu.VMEM((2, rows, LANES), bf16), pltpu.VMEM((each, 2, rows, LANES), bf16)],
        vmem=12,
    )
    at, all_rows = set_rows(sets, rows, each)
    *turned, relay = call(
        functools.partial(turn_kernel, at),
        [shape(NEAR, all_rows - first, LANES) for first in at] + [shape(6 * rows, LANES)],
        1,
        (index, *picks, *wide, chip, core),
        0.3,
    )
    chip = across(relay, 2)
    far = [
        across(turned[first_set(sets, step)], NEAR * step)
        for step in range(max(span for span, _ in sets))
    ]

    near, tight_done, tight_top, picked_queries, residual = call(
        functools.partial(local_kernel, rows, dim),
        [
            shape(each, NEAR, rows, LANES, dtype=jnp.float32),
            shape(each, NEAR, rows // 2, LANES, dtype=jnp.float32),
            shape(each, rows // 2, LANES, dtype=jnp.float32),
            shape(NEAR, even(tall), LANES),
            shape(rows, cols),
        ],
        2,
        (head_offset, index, own, core, chip, own_chip, residual_in),
        4.0,
        [
            pltpu.VMEM((2, rows, LANES), bf16),
            pltpu.VMEM((each, 2, rows, LANES), bf16),
            pltpu.VMEM((each, NEAR, rows // 2, LANES), bf16),
            pltpu.VMEM((NEAR, rows // 2, LANES), bf16),
        ],
        vmem=12,
    )
    mixes = call(
        functools.partial(finish_kernel, sets, rows, dim),
        [shape(rows, LANES)] * NEAR,
        2,
        (head_offset, index, *far, picked_queries, near, tight_done, tight_top),
        6.0,
        [
            pltpu.VMEM((each, NEAR, rows, LANES), jnp.float32),
            pltpu.VMEM((each, rows, LANES), jnp.float32),
            pltpu.VMEM((NEAR, rows, LANES), bf16),
        ],
        vmem=16,
    )
    mixes = [across(block, step) for step, block in enumerate(mixes)]
    held = call(hold_kernel, shape(rows, LANES), 0, (mixes[0], other_weights[1]), 0.2)
    other_mixes = [lax.ppermute(block, "tp", swap) for block in (held, *mixes[1:])]

    other_residual = lax.ppermute(residual, "tp", swap)
    width = norm_gain.shape[0]
    mine, theirs = [], []
    own = call(
        own_kernel,
        shape(rows, width, dtype=jnp.float32),
        1,
        (index, residual_in, other_residual, out_weight, *mixes),
        1.2,
        [pltpu.VMEM((rows, cols), bf16)],
    )
    step = rows // CHUNKS
    for number in range(CHUNKS):
        part = slice(number * step, (number + 1) * step)
        send, keep = call(
            functools.partial(block_kernel, part),
            [shape(step, cols), shape(step, cols, dtype=jnp.float32)],
            1,
            (
                index,
                own,
                *other_mixes,
                *other_weights,
                norm_gain.reshape(1, width),
                gate_weight,
                up_weight,
                down_weight,
            ),
            2.0,
            [
                pltpu.VMEM((step, width), jnp.float32),
                pltpu.VMEM((step, gate_weight.shape[1]), bf16),
                pltpu.VMEM((step, cols), bf16),
            ],
        )
        mine.append(keep)
        theirs.append(lax.ppermute(send, "tp", swap))
    return call(add_kernel, shape(rows, cols), 0, (*mine, *theirs), 0.8)


def solution(mesh):
    placed = (
        P("seq", "tp"),
        P("seq", "tp"),
        P("seq", "tp"),
        P("seq", "tp"),
        P(None, "tp"),
        P("tp", None),
        P(),
        P(None, "tp"),
        P(None, "tp"),
        P("tp", None),
    )
    return jax.shard_map(
        shards, mesh=mesh, in_specs=placed, out_specs=P("seq", "tp"), check_vma=False
    )
```

time: 346 us -> 54.7 us (0.16); the launches traced: 340 us -> 54.6 us
  matrix products: 108 us -> 0 us
  local copies, waits for them, and re-layouts: 86.4 us -> 0.07 us
  other arithmetic: 59.7 us -> 1.23 us
  waiting for transfers between devices: 37.6 us -> 14.8 us
  Pallas kernels: 0 us -> 17 us
  between operations: 14.5 us -> 0.17 us
  blocking collectives: 12.5 us -> 0 us
    dot_general x99 -> x0, matrix products: 108 us -> none  [the longest x48 50.6 us: attend(): jnp.dot(query, key_block.T, preferred_element_type=jnp.float32) * scale]
    reduce_scatter x2 -> x0, waiting for transfers between devices: 34.8 us -> none  [the longest x1 20 us: shards(): lax.psum_scatter(partial_value, 'tp', scatter_dimension=1, tiled=True)]
    reduce_sum x54 -> x0, other arithmetic: 23.5 us -> none  [the longest x5 12.7 us: pick_rows(): jnp.sum(shaped * choose[None, :, :, None].astype(array.dtype), axis=1)]
    mul x25 -> x0, local copies, waits for them, and re-layouts: 23 us -> none  [shards(): outputs.transpose(1, 0, 2)[:, None] * chosen[None, :, :, None]]
    pallas_call x0 -> x10, Pallas kernels: none -> 17 us  [call(): pl.pallas_call(kernel, out_shape=out_shape, in_specs=specs, out_specs=jax...]
    another operation x15 -> x0, local copies, waits for them, and re-layouts: 15.1 us -> none  [pick_rows(): shaped = array.reshape(count, rate, array.shape[1], array.shape[2])]
    slice x16 -> x0, local copies, waits for them, and re-layouts: 14.9 us -> none  [the longest x11 8.81 us: shards(): whole[:, cols:].reshape(group * count, heads_here, head_dim)]
    select_n x20 -> x0, other arithmetic: 13 us -> none  [the longest x18 11.6 us: place_bit(): first = jnp.where(upper, partner, blocks)]
  transfers between devices with their start and end apart: 20 -> 19, of which waited for: 6 -> 9; matrix products, arithmetic and copies ran while one was open for 61% -> 0% of each run, Pallas kernels for 0% -> 24%
where the time goes in v1:
time: 54.7 us; the launch traced here: 54.6 us
  starting transfers between devices  21.3 us (39%)
  Pallas kernels  17 us (31%)
  waiting for transfers between devices  14.8 us (27%)
  other arithmetic  1.23 us (2%)
    pallas_call x10, Pallas kernels, call(): pl.pallas_call(kernel, out_shape=out_shape, in_specs=specs, out_specs=jax...  17 us
    ppermute x11, starting transfers between devices, across(): lax.ppermute(block, 'seq', [(i, i ^ distance) for i in range(seq_count)])  10.6 us
    ppermute x4, starting transfers between devices, shards(): lax.ppermute(block, 'tp', swap)  5.25 us
    ppermute x2, waiting for transfers between devices, shards(): theirs.append(lax.ppermute(send, 'tp', swap))  4.42 us
    ppermute x1, waiting for transfers between devices, shards(): part = lax.ppermute(part, 'tp', swap)  4.24 us
    ppermute x11, waiting for transfers between devices, across(): lax.ppermute(block, 'seq', [(i, i ^ distance) for i in range(seq_count)])  3.82 us
    ppermute x4, waiting for transfers between devices, shards(): lax.ppermute(block, 'tp', swap)  2.33 us
    ppermute x2, starting transfers between devices, shards(): theirs.append(lax.ppermute(send, 'tp', swap))  2.15 us
  transfers between devices with their start and end apart: 19, of which 9 were waited for; matrix products, arithmetic and copies ran while one was open for 0% of the time, Pallas kernels for 24%

profile of v1, /device:TPU:0, one launch (start us, length us, event | category | flops | bytes accessed | tf_op | source)
XLA Modules:
  0.0 54.6 jit_solution(14911768995813743769)
XLA Ops:
  0.0 0.0 copy-start.6
  0.0 0.1 pad_add_fusion.index_ref
  0.1 1.2 %pad_maximum_fusion.source_ref = bf16[768,512]{1,0:T(8,128)(2,1)S(1)} fusion(bf16[256,512]{1,0:T(8,128)(2,1)} %param.13, bf16[256,512]{1,0:T(8,128)(2,1)} %param.12, bf16[256,512]{1,0:T(8,128)(2,1)} %param.11), kind=kLoop, calls=%fused_computation | loop fusion | flops 2359296 | bytes 1572864 | tf_op jit(solution)/shard_map/concatenate | solution.py:530
  1.2 0.0 copy-done.6
  1.2 0.0 copy-start.3
  1.3 1.0 %shard_map.100 = (bf16[240,128]{1,0:T(8,128)(2,1)S(1)}, bf16[240,128]{1,0:T(8,128)(2,1)S(1)}, bf16[768,128]{1,0:T(8,128)(2,1)S(1)}, bf16[1536,128]{1,0:T(8,128)(2,1)S(1)}, bf16[768,128]{1,0:T(8,128)(2,1)S(1)}) custom-call(s32[6,8]{1,0:T(8,128)S(1)} %copy-done.6, s32[2]{0:T(128)S(1)} %pad_add_fusion.index_ref, bf16[768,512]{1,0:T(8,128)(2,1)S(1)} %pad_maximum_fusion.source_ref), custom_call_target="tpu_custom_call" | custom-call | flops 1153500032 | tf_op jit(solution)/shard_map/pallas_call | solution.py:481
  2.3 0.5 collective-permute-start
  2.8 2.6 %collective-permute-start.1 = (bf16[240,128]{1,0:T(8,128)(2,1)S(1)}, bf16[240,128]{1,0:T(8,128)(2,1)S(1)}, u32[]{:S(2)}, u32[]{:S(2)}) collective-permute-start(bf16[240,128]{1,0:T(8,128)(2,1)S(1)} %get-tuple-element.33), channel_id=1, source_target_pairs={{0,4},{2,6},{4,0},{6,2},{8,12},{10,14},{12,8},{14,10},{16,20},{18,... | collective-permute-start | bytes 184328 | tf_op jit(solution)/shard_map/ppermute | solution.py:522
  5.4 0.1 collective-permute-start.2
  5.4 0.0 copy-done.3
  5.5 1.8 %collective-permute-start.11 = (bf16[256,1024]{1,0:T(8,128)(2,1)S(1)}, bf16[256,1024]{1,0:T(8,128)(2,1)S(1)}, u32[]{:S(2)}, u32[]{:S(2)}) collective-permute-start(bf16[256,1024]{1,0:T(8,128)(2,1)S(1)} %constant_dynamic-slice_fusion), channel_id=1, source_target_pairs={{0,1},{1,0},{2,3},{3,2},{4,5},{5,4},{6,7},{7,6},{8,9},{9,8},{10,11... | collective-permute-start | bytes 1572872 | tf_op jit(solution)/shard_map/ppermute | solution.py:527
  7.2 0.0 collective-permute-done.pair_ref.refs_5_.refs_1_
  7.2 0.0 copy-start.5
  7.3 1.7 %shard_map.101 = (f32[2,2,256,128]{3,2,1,0:T(8,128)S(1)}, bf16[240,128]{1,0:T(8,128)(2,1)S(1)}, bf16[240,128]{1,0:T(8,128)(2,1)S(1)}) custom-call(s32[6,8]{1,0:T(8,128)S(1)} %copy-done.6, s32[2]{0:T(128)S(1)} %pad_add_fusion.index_ref, bf16[768,128]{1,0:T(8,128)(2,1)S(1)} %get-tuple-element.29.own_ref.refs_0_, ...), custom_call_target="tpu_custom_call" | custom-call | flops 2307000064 | tf_op jit(solution)/shard_map/pallas_call | solution.py:481
  8.9 0.0 collective-permute-done.1.refs_2_
  8.9 0.4 collective-permute-done.2.refs_3_
  9.3 0.6 %shard_map.102 = (bf16[4,240,128]{2,1,0:T(8,128)(2,1)S(1)}, bf16[4,112,128]{2,1,0:T(8,128)(2,1)S(1)}, bf16[1536,128]{1,0:T(8,128)(2,1)S(1)}) custom-call(s32[2]{0:T(128)S(1)} %pad_add_fusion.index_ref, bf16[240,128]{1,0:T(8,128)(2,1)S(1)} %get-tuple-element.31.refs_0_, bf16[240,128]{1,0:T(8,128)(2,1)S(1)} %get-tuple-element.32.refs_1_, ...), custom_call_target="tpu_custom_call" | custom-call | flops 346049984 | tf_op jit(solution)/shard_map/pallas_call | solution.py:481
  10.0 1.3 %collective-permute-start.3 = (bf16[1536,128]{1,0:T(8,128)(2,1)S(1)}, bf16[1536,128]{1,0:T(8,128)(2,1)S(1)}, u32[]{:S(2)}, u32[]{:S(2)}) collective-permute-start(bf16[1536,128]{1,0:T(8,128)(2,1)S(1)} %get-tuple-element.36), channel_id=1, source_target_pairs={{0,4},{2,6},{4,0},{6,2},{8,12},{10,14},{12,8},{14,10},{16,20},{18,... | collective-permute-start | bytes 1179656 | tf_op jit(solution)/shard_map/ppermute | solution.py:522
  11.3 2.6 %collective-permute-start.6 = (bf16[4,112,128]{2,1,0:T(8,128)(2,1)S(1)}, bf16[4,112,128]{2,1,0:T(8,128)(2,1)S(1)}, u32[]{:S(2)}, u32[]{:S(2)}) collective-permute-start(bf16[4,112,128]{2,1,0:T(8,128)(2,1)S(1)} %get-tuple-element.40), channel_id=1, source_target_pairs={{0,16},{2,18},{4,20},{6,22},{8,24},{10,26},{12,28},{14,30},{16,0},... | collective-permute-start | bytes 344072 | tf_op jit(solution)/shard_map/ppermute | solution.py:522
  13.9 1.3 %collective-permute-start.7 = (bf16[4,112,128]{2,1,0:T(8,128)(2,1)S(1)}, bf16[4,112,128]{2,1,0:T(8,128)(2,1)S(1)}, u32[]{:S(2)}, u32[]{:S(2)}) collective-permute-start(bf16[4,112,128]{2,1,0:T(8,128)(2,1)S(1)} %get-tuple-element.40), channel_id=1, source_target_pairs={{0,24},{2,26},{4,28},{6,30},{8,16},{10,18},{12,20},{14,22},{16,8},... | collective-permute-start | bytes 344072 | tf_op jit(solution)/shard_map/ppermute | solution.py:522
  15.2 0.2 collective-permute-start.5
  15.4 4.2 %collective-permute-done.11.refs_4_ = bf16[256,1024]{1,0:T(8,128)(2,1)S(1)} collective-permute-done((bf16[256,1024]{1,0:T(8,128)(2,1)S(1)}, bf16[256,1024]{1,0:T(8,128)(2,1)S(1)}, u32[]{:S(2)}, u32[]{:S(2)}) %collective-permute-start.11) | collective-permute-done | bytes 524320 | tf_op jit(solution)/shard_map/ppermute | solution.py:527
  19.7 0.0 collective-permute-start.12
  19.7 1.8 %collective-permute-done.3.refs_2_ = bf16[1536,128]{1,0:T(8,128)(2,1)S(1)} collective-permute-done((bf16[1536,128]{1,0:T(8,128)(2,1)S(1)}, bf16[1536,128]{1,0:T(8,128)(2,1)S(1)}, u32[]{:S(2)}, u32[]{:S(2)}) %collective-permute-start.3) | collective-permute-done | bytes 393248 | tf_op jit(solution)/shard_map/ppermute | solution.py:522
  21.5 0.0 copy-done.5
  21.5 3.4 %shard_map.103 = (f32[2,4,256,128]{3,2,1,0:T(8,128)S(1)}, f32[2,4,128,128]{3,2,1,0:T(8,128)S(1)}, f32[2,128,128]{2,1,0:T(8,128)S(1)}, bf16[4,128,128]{2,1,0:T(8,128)(2,1)S(1)}, bf16[256,512]{1,0:T(8,128)(2,1)S(1)}) custom-call(s32[6,8]{1,0:T(8,128)S(1)} %copy-done.6, s32[2]{0:T(128)S(1)} %pad_add_fusion.index_ref, ...), custom_call_target="tpu_custom_call" | custom-call | flops 4614000128 | tf_op jit(solution)/shard_map/pallas_call | solution.py:481
  24.9 1.5 %collective-permute-start.4 = (bf16[256,512]{1,0:T(8,128)(2,1)S(1)}, bf16[256,512]{1,0:T(8,128)(2,1)S(1)}, u32[]{:S(2)}, u32[]{:S(2)}) collective-permute-start(bf16[256,512]{1,0:T(8,128)(2,1)S(1)} %get-tuple-element.38), channel_id=1, source_target_pairs={{0,1},{1,0},{2,3},{3,2},{4,5},{5,4},{6,7},{7,6},{8,9},{9,8},{10,11... | collective-permute-start | bytes 786440 | tf_op jit(solution)/shard_map/ppermute | solution.py:602
  26.4 0.0 collective-permute-done.6.refs_2_
  26.4 0.0 collective-permute-done.7.refs_3_
  26.4 0.2 collective-permute-done.5.refs_1_
  26.6 0.0 copy-start.2
  26.6 4.5 %shard_map.104 = (bf16[256,128]{1,0:T(8,128)(2,1)S(1)}, bf16[256,128]{1,0:T(8,128)(2,1)S(1)}, bf16[256,128]{1,0:T(8,128)(2,1)S(1)}, bf16[256,128]{1,0:T(8,128)(2,1)S(1)}) custom-call(s32[6,8]{1,0:T(8,128)S(1)} %copy-done.6, s32[2]{0:T(128)S(1)} %pad_add_fusion.index_ref, bf16[4,240,128]{2,1,0:T(8,128)(2,1)S(1)} %get-tuple-element.39.refs_0_, ...), custom_call_target="tpu_custom_call" | custom-call | flops 6920999936 | tf_op jit(solution)/shard_map/pallas_call | solution.py:481
  31.1 0.1 collective-permute-start.8
  31.2 1.3 %collective-permute-start.9 = (bf16[256,128]{1,0:T(8,128)(2,1)S(1)}, bf16[256,128]{1,0:T(8,128)(2,1)S(1)}, u32[]{:S(2)}, u32[]{:S(2)}) collective-permute-start(bf16[256,128]{1,0:T(8,128)(2,1)S(1)} %get-tuple-element.47), channel_id=1, source_target_pairs={{0,4},{2,6},{4,0},{6,2},{8,12},{10,14},{12,8},{14,10},{16,20},{18,... | collective-permute-start | bytes 196616 | tf_op jit(solution)/shard_map/ppermute | solution.py:522
  32.5 0.6 %collective-permute-start.10 = (bf16[256,128]{1,0:T(8,128)(2,1)S(1)}, bf16[256,128]{1,0:T(8,128)(2,1)S(1)}, u32[]{:S(2)}, u32[]{:S(2)}) collective-permute-start(bf16[256,128]{1,0:T(8,128)(2,1)S(1)} %get-tuple-element.48), channel_id=1, source_target_pairs={{0,6},{2,4},{4,2},{6,0},{8,14},{10,12},{12,10},{14,8},{16,22},{18,... | collective-permute-start | bytes 196616 | tf_op jit(solution)/shard_map/ppermute | solution.py:522
  33.1 0.0 collective-permute-done.8.refs_1_
  33.1 1.5 %collective-permute-start.14 = (bf16[256,128]{1,0:T(8,128)(2,1)S(1)}, bf16[256,128]{1,0:T(8,128)(2,1)S(1)}, u32[]{:S(2)}, u32[]{:S(2)}) collective-permute-start(bf16[256,128]{1,0:T(8,128)(2,1)S(1)} %collective-permute-done.8.refs_1_), channel_id=1, source_target_pairs={{0,1},{1,0},{2,3},{3,2},{4,5},{5,4},{6,7},{7,6},{8,9},{9,8},{10,11... | collective-permute-start | bytes 196616 | tf_op jit(solution)/shard_map/ppermute | solution.py:600
  34.6 1.4 %collective-permute-done.9.refs_2_ = bf16[256,128]{1,0:T(8,128)(2,1)S(1)} collective-permute-done((bf16[256,128]{1,0:T(8,128)(2,1)S(1)}, bf16[256,128]{1,0:T(8,128)(2,1)S(1)}, u32[]{:S(2)}, u32[]{:S(2)}) %collective-permute-start.9) | collective-permute-done | bytes 65568 | tf_op jit(solution)/shard_map/ppermute | solution.py:522
  36.0 1.7 %collective-permute-start.15 = (bf16[256,128]{1,0:T(8,128)(2,1)S(1)}, bf16[256,128]{1,0:T(8,128)(2,1)S(1)}, u32[]{:S(2)}, u32[]{:S(2)}) collective-permute-start(bf16[256,128]{1,0:T(8,128)(2,1)S(1)} %collective-permute-done.9.refs_2_), channel_id=1, source_target_pairs={{0,1},{1,0},{2,3},{3,2},{4,5},{5,4},{6,7},{7,6},{8,9},{9,8},{10,11... | collective-permute-start | bytes 196616 | tf_op jit(solution)/shard_map/ppermute | solution.py:600
  37.6 0.0 collective-permute-done.10.refs_3_
  37.7 0.5 collective-permute-start.16
  38.1 0.0 collective-permute-done.12.ahead_ref.refs_5_
  38.2 0.0 copy-start
  38.2 0.0 copy-start.1
  38.2 0.0 copy-start.4
  38.2 1.6 %collective-permute-start.13 = (bf16[256,128]{1,0:T(8,128)(2,1)S(1)}, bf16[256,128]{1,0:T(8,128)(2,1)S(1)}, u32[]{:S(2)}, u32[]{:S(2)}) collective-permute-start(bf16[256,128]{1,0:T(8,128)(2,1)S(1)} %shard_map.106), channel_id=1, source_target_pairs={{0,1},{1,0},{2,3},{3,2},{4,5},{5,4},{6,7},{7,6},{8,9},{9,8},{10,11... | collective-permute-start | bytes 196616 | tf_op jit(solution)/shard_map/ppermute | solution.py:600
  39.8 0.0 collective-permute-done.4.other_residual_ref
  39.8 1.1 %shard_map.105.own_ref = f32[256,1024]{1,0:T(8,128)S(1)} custom-call(s32[2]{0:T(128)S(1)} %pad_add_fusion.index_ref, bf16[256,512]{1,0:T(8,128)(2,1)S(1)} %copy-done.5, bf16[256,512]{1,0:T(8,128)(2,1)S(1)} %collective-permute-done.4.other_residual_ref, bf16[512,1024]{1,0:T(8,128)(2,1)S(1)} %copy-done.3, ...), custom_call_target="tpu_custom_call" | custom-call | flops 1384199936 | tf_op jit(solution)/shard_map/pallas_call | solution.py:481
  40.9 0.0 collective-permute-done.14.refs_1_
  40.9 0.0 collective-permute-done.15.refs_2_
  40.9 1.6 %collective-permute-done.16.refs_3_ = bf16[256,128]{1,0:T(8,128)(2,1)S(1)} collective-permute-done((bf16[256,128]{1,0:T(8,128)(2,1)S(1)}, bf16[256,128]{1,0:T(8,128)(2,1)S(1)}, u32[]{:S(2)}, u32[]{:S(2)}) %collective-permute-start.16) | collective-permute-done | bytes 65568 | tf_op jit(solution)/shard_map/ppermute | solution.py:600
  42.6 0.7 %collective-permute-done.13.refs_0_ = bf16[256,128]{1,0:T(8,128)(2,1)S(1)} collective-permute-done((bf16[256,128]{1,0:T(8,128)(2,1)S(1)}, bf16[256,128]{1,0:T(8,128)(2,1)S(1)}, u32[]{:S(2)}, u32[]{:S(2)}) %collective-permute-start.13) | collective-permute-done | bytes 65568 | tf_op jit(solution)/shard_map/ppermute | solution.py:600
  43.3 0.0 copy-done.2
  43.3 0.0 copy-done
  43.3 0.0 copy-done.1
  43.3 0.0 copy-done.4
  43.3 2.0 %shard_map.108 = (bf16[128,512]{1,0:T(8,128)(2,1)S(1)}, f32[128,512]{1,0:T(8,128)S(1)}) custom-call(s32[2]{0:T(128)S(1)} %pad_add_fusion.index_ref, f32[256,1024]{1,0:T(8,128)S(1)} %shard_map.105.own_ref, bf16[256,128]{1,0:T(8,128)(2,1)S(1)} %collective-permute-done.13.refs_0_, bf16[256,128]{1,0:T(8,128)(2,1)S(1)} %collective-permute-done.14.refs_1_, ...), custom_call_target="tpu_custom_call" | custom-call | flops 2307000064 | tf_op jit(solution)/shard_map/pallas_call | solution.py:481
  45.3 1.5 %collective-permute-start.18 = (bf16[128,512]{1,0:T(8,128)(2,1)S(1)}, bf16[128,512]{1,0:T(8,128)(2,1)S(1)}, u32[]{:S(2)}, u32[]{:S(2)}) collective-permute-start(bf16[128,512]{1,0:T(8,128)(2,1)S(1)} %get-tuple-element.52), channel_id=1, source_target_pairs={{0,1},{1,0},{2,3},{3,2},{4,5},{5,4},{6,7},{7,6},{8,9},{9,8},{10,11... | collective-permute-start | bytes 393224 | tf_op jit(solution)/shard_map/ppermute | solution.py:638
  46.8 2.0 %shard_map.107 = (bf16[128,512]{1,0:T(8,128)(2,1)S(1)}, f32[128,512]{1,0:T(8,128)S(1)}) custom-call(s32[2]{0:T(128)S(1)} %pad_add_fusion.index_ref, f32[256,1024]{1,0:T(8,128)S(1)} %shard_map.105.own_ref, bf16[256,128]{1,0:T(8,128)(2,1)S(1)} %collective-permute-done.13.refs_0_, bf16[256,128]{1,0:T(8,128)(2,1)S(1)} %collective-permute-done.14.refs_1_, ...), custom_call_target="tpu_custom_call" | custom-call | flops 2307000064 | tf_op jit(solution)/shard_map/pallas_call | solution.py:481
  48.8 0.6 %collective-permute-start.17 = (bf16[128,512]{1,0:T(8,128)(2,1)S(1)}, bf16[128,512]{1,0:T(8,128)(2,1)S(1)}, u32[]{:S(2)}, u32[]{:S(2)}) collective-permute-start(bf16[128,512]{1,0:T(8,128)(2,1)S(1)} %get-tuple-element.51), channel_id=1, source_target_pairs={{0,1},{1,0},{2,3},{3,2},{4,5},{5,4},{6,7},{7,6},{8,9},{9,8},{10,11... | collective-permute-start | bytes 393224 | tf_op jit(solution)/shard_map/ppermute | solution.py:638
  49.4 0.9 %collective-permute-done.18.refs_3_ = bf16[128,512]{1,0:T(8,128)(2,1)S(1)} collective-permute-done((bf16[128,512]{1,0:T(8,128)(2,1)S(1)}, bf16[128,512]{1,0:T(8,128)(2,1)S(1)}, u32[]{:S(2)}, u32[]{:S(2)}) %collective-permute-start.18) | collective-permute-done | bytes 131104 | tf_op jit(solution)/shard_map/ppermute | solution.py:638
  50.3 3.5 %collective-permute-done.17.refs_2_ = bf16[128,512]{1,0:T(8,128)(2,1)S(1)} collective-permute-done((bf16[128,512]{1,0:T(8,128)(2,1)S(1)}, bf16[128,512]{1,0:T(8,128)(2,1)S(1)}, u32[]{:S(2)}, u32[]{:S(2)}) %collective-permute-start.17) | collective-permute-done | bytes 131104 | tf_op jit(solution)/shard_map/ppermute | solution.py:638
  53.8 0.8 %shard_map.109 = bf16[256,512]{1,0:T(8,128)(2,1)} custom-call(f32[128,512]{1,0:T(8,128)S(1)} %get-tuple-element.49.refs_0_, f32[128,512]{1,0:T(8,128)S(1)} %get-tuple-element.50.refs_1_, bf16[128,512]{1,0:T(8,128)(2,1)S(1)} %collective-permute-done.17.refs_2_, bf16[128,512]{1,0:T(8,128)(2,1)S(1)} %collective-permute-done.18.refs_3_), custom_call_target="tpu_custom_call" | custom-call | flops 922800000 | tf_op jit(solution)/shard_map/pallas_call | solution.py:481
  (2 shorter events, 0.0 us)
Async XLA Ops:
  0.0 1.2 %copy-start.6 = (s32[6,8]{1,0:T(8,128)S(1)}, s32[6,8]{1,0:T(8,128)}, u32[]{:S(2)}) copy-start(s32[6,8]{1,0:T(8,128)} %offset_ref.7) | copy-start | bytes 580
  1.2 4.2 %copy-start.3 = (bf16[512,1024]{1,0:T(8,128)(2,1)S(1)}, bf16[512,1024]{1,0:T(8,128)(2,1)}, u32[]{:S(2)}) copy-start(bf16[512,1024]{1,0:T(8,128)(2,1)} %weight_ref.1) | copy-start | bytes 3145732
  2.3 5.0 %collective-permute-start = (bf16[1536,128]{1,0:T(8,128)(2,1)S(1)}, bf16[1536,128]{1,0:T(8,128)(2,1)S(1)}, u32[]{:S(2)}, u32[]{:S(2)}) collective-permute-start(bf16[1536,128]{1,0:T(8,128)(2,1)S(1)} %get-tuple-element.30), channel_id=1, source_target_pairs={{0,2},{2,0},{4,6},{6,4},{8,10},{10,8},{12,14},{14,12},{16,18},{18,... | collective-permute-start | bytes 1179656 | tf_op jit(solution)/shard_map/ppermute | solution.py:522
  2.8 6.1 %collective-permute-start.1 = (bf16[240,128]{1,0:T(8,128)(2,1)S(1)}, bf16[240,128]{1,0:T(8,128)(2,1)S(1)}, u32[]{:S(2)}, u32[]{:S(2)}) collective-permute-start(bf16[240,128]{1,0:T(8,128)(2,1)S(1)} %get-tuple-element.33), channel_id=1, source_target_pairs={{0,4},{2,6},{4,0},{6,2},{8,12},{10,14},{12,8},{14,10},{16,20},{18,... | collective-permute-start | bytes 184328 | tf_op jit(solution)/shard_map/ppermute | solution.py:522
  5.4 4.0 %collective-permute-start.2 = (bf16[240,128]{1,0:T(8,128)(2,1)S(1)}, bf16[240,128]{1,0:T(8,128)(2,1)S(1)}, u32[]{:S(2)}, u32[]{:S(2)}) collective-permute-start(bf16[240,128]{1,0:T(8,128)(2,1)S(1)} %get-tuple-element.34), channel_id=1, source_target_pairs={{0,6},{2,4},{4,2},{6,0},{8,14},{10,12},{12,10},{14,8},{16,22},{18,... | collective-permute-start | bytes 184328 | tf_op jit(solution)/shard_map/ppermute | solution.py:522
  5.5 14.2 %collective-permute-start.11 = (bf16[256,1024]{1,0:T(8,128)(2,1)S(1)}, bf16[256,1024]{1,0:T(8,128)(2,1)S(1)}, u32[]{:S(2)}, u32[]{:S(2)}) collective-permute-start(bf16[256,1024]{1,0:T(8,128)(2,1)S(1)} %constant_dynamic-slice_fusion), channel_id=1, source_target_pairs={{0,1},{1,0},{2,3},{3,2},{4,5},{5,4},{6,7},{7,6},{8,9},{9,8},{10,11... | collective-permute-start | bytes 1572872 | tf_op jit(solution)/shard_map/ppermute | solution.py:527
  7.2 14.3 %copy-start.5 = (bf16[256,512]{1,0:T(8,128)(2,1)S(1)}, bf16[256,512]{1,0:T(8,128)(2,1)}, u32[]{:S(2)}) copy-start(bf16[256,512]{1,0:T(8,128)(2,1)} %residual_ref.1) | copy-start | bytes 786436
  10.0 11.5 %collective-permute-start.3 = (bf16[1536,128]{1,0:T(8,128)(2,1)S(1)}, bf16[1536,128]{1,0:T(8,128)(2,1)S(1)}, u32[]{:S(2)}, u32[]{:S(2)}) collective-permute-start(bf16[1536,128]{1,0:T(8,128)(2,1)S(1)} %get-tuple-element.36), channel_id=1, source_target_pairs={{0,4},{2,6},{4,0},{6,2},{8,12},{10,14},{12,8},{14,10},{16,20},{18,... | collective-permute-start | bytes 1179656 | tf_op jit(solution)/shard_map/ppermute | solution.py:522
  11.3 15.2 %collective-permute-start.6 = (bf16[4,112,128]{2,1,0:T(8,128)(2,1)S(1)}, bf16[4,112,128]{2,1,0:T(8,128)(2,1)S(1)}, u32[]{:S(2)}, u32[]{:S(2)}) collective-permute-start(bf16[4,112,128]{2,1,0:T(8,128)(2,1)S(1)} %get-tuple-element.40), channel_id=1, source_target_pairs={{0,16},{2,18},{4,20},{6,22},{8,24},{10,26},{12,28},{14,30},{16,0},... | collective-permute-start | bytes 344072 | tf_op jit(solution)/shard_map/ppermute | solution.py:522
  13.9 12.6 %collective-permute-start.7 = (bf16[4,112,128]{2,1,0:T(8,128)(2,1)S(1)}, bf16[4,112,128]{2,1,0:T(8,128)(2,1)S(1)}, u32[]{:S(2)}, u32[]{:S(2)}) collective-permute-start(bf16[4,112,128]{2,1,0:T(8,128)(2,1)S(1)} %get-tuple-element.40), channel_id=1, source_target_pairs={{0,24},{2,26},{4,28},{6,30},{8,16},{10,18},{12,20},{14,22},{16,8},... | collective-permute-start | bytes 344072 | tf_op jit(solution)/shard_map/ppermute | solution.py:522
  15.2 11.4 %collective-permute-start.5 = (bf16[4,240,128]{2,1,0:T(8,128)(2,1)S(1)}, bf16[4,240,128]{2,1,0:T(8,128)(2,1)S(1)}, u32[]{:S(2)}, u32[]{:S(2)}) collective-permute-start(bf16[4,240,128]{2,1,0:T(8,128)(2,1)S(1)} %get-tuple-element.39.refs_0_), channel_id=1, source_target_pairs={{0,8},{2,10},{4,12},{6,14},{8,0},{10,2},{12,4},{14,6},{16,24},{18,... | collective-permute-start | bytes 737288 | tf_op jit(solution)/shard_map/ppermute | solution.py:522
  19.7 18.5 %collective-permute-start.12 = (bf16[256,1024]{1,0:T(8,128)(2,1)S(1)}, bf16[256,1024]{1,0:T(8,128)(2,1)S(1)}, u32[]{:S(2)}, u32[]{:S(2)}) collective-permute-start(bf16[256,1024]{1,0:T(8,128)(2,1)S(1)} %collective-permute-done.11.refs_4_), channel_id=1, source_target_pairs={{0,2},{2,0},{4,6},{6,4},{8,10},{10,8},{12,14},{14,12},{16,18},{18,... | collective-permute-start | bytes 1572872 | tf_op jit(solution)/shard_map/ppermute | solution.py:522
  24.9 14.9 %collective-permute-start.4 = (bf16[256,512]{1,0:T(8,128)(2,1)S(1)}, bf16[256,512]{1,0:T(8,128)(2,1)S(1)}, u32[]{:S(2)}, u32[]{:S(2)}) collective-permute-start(bf16[256,512]{1,0:T(8,128)(2,1)S(1)} %get-tuple-element.38), channel_id=1, source_target_pairs={{0,1},{1,0},{2,3},{3,2},{4,5},{5,4},{6,7},{7,6},{8,9},{9,8},{10,11... | collective-permute-start | bytes 786440 | tf_op jit(solution)/shard_map/ppermute | solution.py:602
  26.6 16.6 %copy-start.2 = (bf16[1024,1024]{1,0:T(8,128)(2,1)S(1)}, bf16[1024,1024]{1,0:T(8,128)(2,1)}, u32[]{:S(2)}) copy-start(bf16[1024,1024]{1,0:T(8,128)(2,1)} %refs_9_.3) | copy-start | bytes 6291460
  31.1 1.9 %collective-permute-start.8 = (bf16[256,128]{1,0:T(8,128)(2,1)S(1)}, bf16[256,128]{1,0:T(8,128)(2,1)S(1)}, u32[]{:S(2)}, u32[]{:S(2)}) collective-permute-start(bf16[256,128]{1,0:T(8,128)(2,1)S(1)} %get-tuple-element.46), channel_id=1, source_target_pairs={{0,2},{2,0},{4,6},{6,4},{8,10},{10,8},{12,14},{14,12},{16,18},{18,... | collective-permute-start | bytes 196616 | tf_op jit(solution)/shard_map/ppermute | solution.py:522
  31.2 4.8 %collective-permute-start.9 = (bf16[256,128]{1,0:T(8,128)(2,1)S(1)}, bf16[256,128]{1,0:T(8,128)(2,1)S(1)}, u32[]{:S(2)}, u32[]{:S(2)}) collective-permute-start(bf16[256,128]{1,0:T(8,128)(2,1)S(1)} %get-tuple-element.47), channel_id=1, source_target_pairs={{0,4},{2,6},{4,0},{6,2},{8,12},{10,14},{12,8},{14,10},{16,20},{18,... | collective-permute-start | bytes 196616 | tf_op jit(solution)/shard_map/ppermute | solution.py:522
  32.5 5.2 %collective-permute-start.10 = (bf16[256,128]{1,0:T(8,128)(2,1)S(1)}, bf16[256,128]{1,0:T(8,128)(2,1)S(1)}, u32[]{:S(2)}, u32[]{:S(2)}) collective-permute-start(bf16[256,128]{1,0:T(8,128)(2,1)S(1)} %get-tuple-element.48), channel_id=1, source_target_pairs={{0,6},{2,4},{4,2},{6,0},{8,14},{10,12},{12,10},{14,8},{16,22},{18,... | collective-permute-start | bytes 196616 | tf_op jit(solution)/shard_map/ppermute | solution.py:522
  33.1 7.8 %collective-permute-start.14 = (bf16[256,128]{1,0:T(8,128)(2,1)S(1)}, bf16[256,128]{1,0:T(8,128)(2,1)S(1)}, u32[]{:S(2)}, u32[]{:S(2)}) collective-permute-start(bf16[256,128]{1,0:T(8,128)(2,1)S(1)} %collective-permute-done.8.refs_1_), channel_id=1, source_target_pairs={{0,1},{1,0},{2,3},{3,2},{4,5},{5,4},{6,7},{7,6},{8,9},{9,8},{10,11... | collective-permute-start | bytes 196616 | tf_op jit(solution)/shard_map/ppermute | solution.py:600
  36.0 4.9 %collective-permute-start.15 = (bf16[256,128]{1,0:T(8,128)(2,1)S(1)}, bf16[256,128]{1,0:T(8,128)(2,1)S(1)}, u32[]{:S(2)}, u32[]{:S(2)}) collective-permute-start(bf16[256,128]{1,0:T(8,128)(2,1)S(1)} %collective-permute-done.9.refs_2_), channel_id=1, source_target_pairs={{0,1},{1,0},{2,3},{3,2},{4,5},{5,4},{6,7},{7,6},{8,9},{9,8},{10,11... | collective-permute-start | bytes 196616 | tf_op jit(solution)/shard_map/ppermute | solution.py:600
  37.7 4.9 %collective-permute-start.16 = (bf16[256,128]{1,0:T(8,128)(2,1)S(1)}, bf16[256,128]{1,0:T(8,128)(2,1)S(1)}, u32[]{:S(2)}, u32[]{:S(2)}) collective-permute-start(bf16[256,128]{1,0:T(8,128)(2,1)S(1)} %collective-permute-done.10.refs_3_), channel_id=1, source_target_pairs={{0,1},{1,0},{2,3},{3,2},{4,5},{5,4},{6,7},{7,6},{8,9},{9,8},{10,11... | collective-permute-start | bytes 196616 | tf_op jit(solution)/shard_map/ppermute | solution.py:600
  38.2 5.1 %copy-start = (bf16[1024,1024]{1,0:T(8,128)(2,1)S(1)}, bf16[1024,1024]{1,0:T(8,128)(2,1)}, u32[]{:S(2)}) copy-start(bf16[1024,1024]{1,0:T(8,128)(2,1)} %refs_7_.3) | copy-start | bytes 6291460
  38.2 5.1 %copy-start.1 = (bf16[1024,1024]{1,0:T(8,128)(2,1)S(1)}, bf16[1024,1024]{1,0:T(8,128)(2,1)}, u32[]{:S(2)}) copy-start(bf16[1024,1024]{1,0:T(8,128)(2,1)} %refs_8_.3) | copy-start | bytes 6291460
  38.2 5.1 %copy-start.4 = (f32[1024]{0:T(1024)S(1)}, f32[1024]{0:T(1024)}, u32[]{:S(2)}) copy-start(f32[1024]{0:T(1024)} %param.16) | copy-start | bytes 12292
  38.2 5.1 %collective-permute-start.13 = (bf16[256,128]{1,0:T(8,128)(2,1)S(1)}, bf16[256,128]{1,0:T(8,128)(2,1)S(1)}, u32[]{:S(2)}, u32[]{:S(2)}) collective-permute-start(bf16[256,128]{1,0:T(8,128)(2,1)S(1)} %shard_map.106), channel_id=1, source_target_pairs={{0,1},{1,0},{2,3},{3,2},{4,5},{5,4},{6,7},{7,6},{8,9},{9,8},{10,11... | collective-permute-start | bytes 196616 | tf_op jit(solution)/shard_map/ppermute | solution.py:600
  45.3 5.0 %collective-permute-start.18 = (bf16[128,512]{1,0:T(8,128)(2,1)S(1)}, bf16[128,512]{1,0:T(8,128)(2,1)S(1)}, u32[]{:S(2)}, u32[]{:S(2)}) collective-permute-start(bf16[128,512]{1,0:T(8,128)(2,1)S(1)} %get-tuple-element.52), channel_id=1, source_target_pairs={{0,1},{1,0},{2,3},{3,2},{4,5},{5,4},{6,7},{7,6},{8,9},{9,8},{10,11... | collective-permute-start | bytes 393224 | tf_op jit(solution)/shard_map/ppermute | solution.py:638
  48.8 5.0 %collective-permute-start.17 = (bf16[128,512]{1,0:T(8,128)(2,1)S(1)}, bf16[128,512]{1,0:T(8,128)(2,1)S(1)}, u32[]{:S(2)}, u32[]{:S(2)}) collective-permute-start(bf16[128,512]{1,0:T(8,128)(2,1)S(1)} %get-tuple-element.51), channel_id=1, source_target_pairs={{0,1},{1,0},{2,3},{3,2},{4,5},{5,4},{6,7},{7,6},{8,9},{9,8},{10,11... | collective-permute-start | bytes 393224 | tf_op jit(solution)/shard_map/ppermute | solution.py:638

commit v2 on v1

--- a/solution.py
+++ b/solution.py
@@ -64,17 +64,16 @@
     return jnp.concatenate(select, axis=0).astype(jnp.bfloat16)
 
 
-def far_picks(sets, rows, dim, low, offset_ref, blocks, members):
+def far_picks(sets, rows, dim, blocks, selects):
     each = LANES // dim
     far_branches = range(2, BRANCHES)
     starts, _ = part_rows(rows, far_branches)
     picked = []
-    for (key, value), member in zip(blocks, members):
+    for (key, value), mine in zip(blocks, selects):
         for head in range(each):
             lanes = slice(head * dim, (head + 1) * dim)
-            select = selection(rows, far_branches, offset_ref, member * each + head)
             pairs = jnp.concatenate([key[:, lanes], value[:, lanes]], axis=1)
-            picked.append(jnp.dot(select, pairs, preferred_element_type=jnp.float32))
+            picked.append(jnp.dot(mine[head], pairs, preferred_element_type=jnp.float32))
     outs = []
     for number in range(len(blocks)):
         parts = []
@@ -96,7 +95,12 @@
     blocks = [
         (source_ref[rows : 2 * rows, lanes], source_ref[2 * rows :, lanes]) for lanes in all_lanes[2:]
     ]
-    picks = far_picks(sets, rows, dim, low, offset_ref, blocks, [low ^ 2, low ^ 3])
+    each = LANES // dim
+    selects = [
+        [selection(rows, range(2, BRANCHES), offset_ref, (low ^ side) * each + head) for head in range(each)]
+        for side in (2, 3)
+    ]
+    picks = far_picks(sets, rows, dim, blocks, selects)
     for pick, wide_ref in zip(picks, wide_refs):
         wide_ref[...] = pick
     for side, lanes in enumerate(all_lanes):
@@ -106,10 +110,7 @@
 
 
 def turn_kernel(at, index_ref, *refs):
-    in_refs, chip_ref, core_ref, out_refs, relay_ref = refs[:NEAR], *refs[NEAR : NEAR + 2], refs[NEAR + 2 : -1], refs[-1]
-    half = chip_ref.shape[0]
-    relay_ref[:half] = chip_ref[...]
-    relay_ref[half:] = core_ref[half:]
+    in_refs, out_refs = refs[:NEAR], refs[NEAR + 1 : -1]
     low = index_ref[0] % NEAR
     for side in range(NEAR):
         for first, out_ref in zip(at, out_refs):
@@ -206,46 +207,80 @@
     return tuple(ref[first + part * rows : first + (part + 1) * rows] for part in range(3))
 
 
-def own_chip_kernel(sets, rows, dim, offset_ref, index_ref, own_ref, pair_ref, *refs):
-    near_ref, pick_refs, query, pairs = refs[0], refs[1:3], *refs[3:]
+def local_picks(rows, dim, block, select_ref):
+    query, key, value = block
+    each = LANES // dim
+    left = lax.broadcasted_iota(jnp.int32, (1, LANES), 1) < dim
+    both = [jnp.dot(select_ref[head], query, preferred_element_type=jnp.float32) for head in range(each)]
+    pairs = []
+    for head in range(each):
+        lanes = slice(head * dim, (head + 1) * dim)
+        pair = jnp.concatenate([key[:, lanes], value[:, lanes]], axis=1)
+        pair = jnp.dot(select_ref[head, : rows // 2], pair, preferred_element_type=jnp.float32)
+        pairs.append(pair.astype(jnp.bfloat16))
+    return jnp.where(left, both[0], both[1]).astype(jnp.bfloat16), pairs
+
+
+def own_chip_kernel(sets, rows, dim, offset_ref, index_ref, own_ref, pair_ref, chip_ref, *refs):
+    near_ref, pick_refs, relay_ref = refs[0], refs[1:3], refs[3]
+    select_ref, spread_ref, picked_ref, tight_ref, query, pairs = refs[4:]
+    half = chip_ref.shape[0]
+    relay_ref[:half] = chip_ref[...]
+    relay_ref[half:] = pair_ref[half:]
+    each = LANES // dim
     low = index_ref[0] % NEAR
+    starts, used = part_rows(rows, range(1, BRANCHES))
+    column = lax.broadcasted_iota(jnp.int32, (1, rows), 1)
+    row_wide = lax.broadcasted_iota(jnp.int32, (rows, rows), 0)
+    for head in range(each):
+        select = [mask_select(rows, b, offset_ref[b, low * each + head]) for b in range(1, BRANCHES)]
+        select.append(jnp.zeros((rows - used, rows), jnp.float32))
+        select_ref[head] = jnp.concatenate(select, axis=0).astype(jnp.bfloat16)
+        target = jnp.full((1, rows), -1, jnp.int32)
+        for branch in range(1, BRANCHES):
+            rate = 2**branch
+            offset = offset_ref[branch, low * each + head] & (rate - 1)
+            target = jnp.where(
+                column >= starts[branch], (column - starts[branch]) * rate + offset, target
+            )
+        spread_ref[head] = jnp.where(row_wide == target, 1.0, 0.0).astype(jnp.bfloat16)
     members = [(side, raw_blocks(ref, rows)) for side, ref in enumerate((own_ref, pair_ref))]
+    selects = [select_ref[head, rows // 2 : used] for head in range(each)]
     blocks = [block[1:] for _, block in members]
-    for pick, pick_ref in zip(far_picks(sets, rows, dim, low, offset_ref, blocks, [low, low]), pick_refs):
+    for pick, pick_ref in zip(far_picks(sets, rows, dim, blocks, [selects, selects]), pick_refs):
         pick_ref[...] = pick
+    for side, block in members:
+        picked, tight = local_picks(rows, dim, block, select_ref)
+        core = (low ^ side) % 2
+        picked_ref[core] = picked
+        for head in range(each):
+            tight_ref[head, core] = tight[head]
     jobs = nearest(members, rows, dim, low, query, pairs)
     for head, (top, accum) in enumerate(attend(jobs, 4)):
         near_ref[head] = nearest_out(top, accum)
 
 
-def local_kernel(rows, dim, offset_ref, index_ref, *refs):
-    own_ref, core_ref, chip_ref, own_chip_ref, residual_ref, refs = *refs[:5], refs[5:]
-    near_ref, far_ref, top_ref, picked_ref, residual_out = refs[:5]
-    query, pairs, tight_pairs, tight_query = refs[5:]
+def local_kernel(rows, dim, index_ref, *refs):
+    chip_ref, own_chip_ref, select_ref, own_picked_ref, own_tight_ref, residual_ref = refs[:6]
+    near_ref, far_ref, top_ref, picked_ref, residual_out = refs[6:11]
+    query, pairs, tight_pairs, tight_query = refs[11:]
     residual_out[...] = residual_ref[...]
-    blocks = [raw_blocks(ref, rows) for ref in (own_ref, core_ref, chip_ref)]
-    blocks.append(raw_blocks(chip_ref, rows, 3 * rows))
     each = LANES // dim
     low = index_ref[0] % NEAR
     chip = low // 2
     count = rows // 2
-    left = lax.broadcasted_iota(jnp.int32, (1, LANES), 1) < dim
-    selects = [
-        selection(rows, range(1, BRANCHES), offset_ref, low * each + head) for head in range(each)
-    ]
-    for side in range(NEAR):
-        query_in, key_in, value_in = blocks[side]
-        both = [jnp.dot(select, query_in, preferred_element_type=jnp.float32) for select in selects]
-        picked = jnp.where(left, both[0], both[1])
-        tight_query[low ^ side] = picked[:count].astype(jnp.bfloat16)
-        rest = picked[count:]
-        rest = [rest, jnp.zeros((picked_ref.shape[1] - rest.shape[0], LANES), jnp.float32)]
-        picked_ref[low ^ side] = jnp.concatenate(rest, axis=0).astype(jnp.bfloat16)
+    blocks = {side: raw_blocks(chip_ref, rows, 3 * rows * (side - 2)) for side in (2, 3)}
+    for core in range(2):
+        tight_query[chip * 2 + core] = own_picked_ref[core, :count]
+        picked_ref[chip * 2 + core] = own_picked_ref[core, count:]
         for head in range(each):
-            lanes = slice(head * dim, (head + 1) * dim)
-            block = jnp.concatenate([key_in[:, lanes], value_in[:, lanes]], axis=1)
-            block = jnp.dot(selects[head][:count], block, preferred_element_type=jnp.float32)
-            tight_pairs[head, low ^ side] = block.astype(jnp.bfloat16)
+            tight_pairs[head, chip * 2 + core] = own_tight_ref[head, core]
+    for side in (2, 3):
+        picked, tight = local_picks(rows, dim, blocks[side], select_ref)
+        tight_query[low ^ side] = picked[:count]
+        picked_ref[low ^ side] = picked[count:]
+        for head in range(each):
+            tight_pairs[head, low ^ side] = tight[head]
     members = [(side, blocks[side]) for side in range(2, NEAR)]
     jobs = nearest(members, rows, dim, low, query, pairs)
     for head in range(each):
@@ -303,14 +338,10 @@
         tops[head, into, :] = top_lanes(top, count, branch)
 
 
-def hold_kernel(block_ref, ahead_ref, out_ref):
-    out_ref[...] = block_ref[...]
-
-
 def finish_kernel(sets, rows, dim, offset_ref, index_ref, *refs):
     steps = max(span for span, _ in sets)
     far_refs, refs = refs[:steps], refs[steps:]
-    query_ref, near_ref, tight_ref, tight_top_ref, refs = *refs[:4], refs[4:]
+    query_ref, near_ref, tight_ref, tight_top_ref, select_ref, spread_ref, refs = *refs[:6], refs[6:]
     out_refs, far, tops, mixed_ref = refs[:NEAR], *refs[NEAR:]
     each = LANES // dim
     low = index_ref[0] % NEAR
@@ -325,10 +356,7 @@
 
     lane = lax.broadcasted_iota(jnp.int32, (1, LANES), 1)
     inside = lane % GROUP
-    column = lax.broadcasted_iota(jnp.int32, (1, rows), 1)
     row = lax.broadcasted_iota(jnp.int32, (rows, 1), 0)
-    row_wide = lax.broadcasted_iota(jnp.int32, (rows, rows), 0)
-    column_wide = lax.broadcasted_iota(jnp.int32, (rows, rows), 1)
     row_lane = lax.broadcasted_iota(jnp.int32, (rows, LANES), 0)
 
     def along(start_of, value_of, fill):
@@ -346,7 +374,7 @@
         return pltpu.roll(array, lanes % LANES, 1)
 
     heads = range(each)
-    spreads, gathers, covered = [], [], []
+    covered = []
     for head in heads:
         offsets = {
             branch: offset_ref[branch, low * each + head] & (2**branch - 1)
@@ -355,17 +383,9 @@
         chosen = jnp.where(inside == 0, 0, 1)
         for branch in range(1, BRANCHES):
             chosen = jnp.where(inside == 3 * branch, offsets[branch], chosen)
-
-        def position_of(slot):
-            rate = along(slot, lambda branch: 2**branch, 0)
-            inner = slot - along(slot, lambda branch: starts[branch], 0)
-            return inner * rate + along(slot, lambda branch: offsets[branch], 0)
-
-        spreads.append(jnp.where(row_wide == position_of(column), 1.0, 0.0).astype(jnp.bfloat16))
-        gathers.append(jnp.where(column_wide == position_of(row), 1.0, 0.0).astype(jnp.bfloat16))
         covered.append((row_lane & masks) == chosen)
     stats = [
-        jnp.dot(spreads[head], tops[head].astype(jnp.bfloat16), preferred_element_type=jnp.float32)
+        jnp.dot(spread_ref[head], tops[head].astype(jnp.bfloat16), preferred_element_type=jnp.float32)
         for head in heads
     ]
     stats = [block + turned(block, -1) + turned(block, -2) for block in stats]
@@ -384,26 +404,33 @@
         jnp.where(block > 0.5 * masked_score, jnp.exp(block - peak), 0.0)
         for block, peak in zip(stats, peaks)
     ]
+    weight = [block.astype(jnp.bfloat16) for block in weight]
     weights = [
-        jnp.dot(gathers[head], weight[head].astype(jnp.bfloat16), preferred_element_type=jnp.float32)
-        for head in heads
-    ]
+        jnp.dot(select_ref[head], weight[head], preferred_element_type=jnp.float32) for head in heads
+    ]
+    from_lane = lax.broadcasted_iota(jnp.int32, (LANES, NEAR * LANES), 0)
+    to_member = lax.broadcasted_iota(jnp.int32, (LANES, NEAR * LANES), 1) >> (LANES.bit_length() - 1)
+    group = GROUP.bit_length() - 1
+    any_lane = jnp.where(from_lane >> group == to_member, 1.0, 0.0).astype(jnp.bfloat16)
+    first_lane = jnp.where(from_lane == to_member << group, 1.0, 0.0).astype(jnp.bfloat16)
+    weights = [jnp.where(inside == own_lane, block, 0.0).astype(jnp.bfloat16) for block in weights]
+    weights = [jnp.dot(block, any_lane, preferred_element_type=jnp.float32) for block in weights]
+    owns = [jnp.dot(block, first_lane, preferred_element_type=jnp.float32) for block in weight]
     scaled = [[] for _ in heads]
     for member in range(NEAR):
         for head in heads:
-            picked = jnp.where(lane == own_lane + GROUP * member, weights[head], 0.0)
-            block = far[head, member] * jnp.sum(picked, axis=1, keepdims=True)
+            block = far[head, member] * weights[head][:, member * LANES : (member + 1) * LANES]
             rest = block - block.astype(jnp.bfloat16).astype(jnp.float32)
             scaled[head].append(jnp.where(lane == 0, rest, block).astype(jnp.bfloat16))
     added = [
-        jnp.dot(spreads[head], jnp.concatenate(scaled[head], axis=1), preferred_element_type=jnp.float32)
+        jnp.dot(spread_ref[head], jnp.concatenate(scaled[head], axis=1), preferred_element_type=jnp.float32)
         for head in heads
     ]
     halves = [[] for _ in heads]
     for member in range(NEAR):
         for head in heads:
             block = added[head][:, member * LANES : (member + 1) * LANES]
-            own = weight[head][:, GROUP * member : GROUP * member + 1]
+            own = owns[head][:, member * LANES : (member + 1) * LANES]
             total = block + own * near_ref[head, member]
             below = total[:, 1:2] + block[:, 0:1]
             halves[head].append(total[:, dim:] * (1.0 / below))
@@ -473,16 +500,22 @@
         ).astype(out_ref.dtype)
 
 
-def call(kernel, out_shape, smem, operands, micros, scratch=(), vmem=8):
+def call(kernel, out_shape, smem, operands, micros, scratch=(), vmem=8, passed=False):
     specs = [
         pl.BlockSpec(memory_space=pltpu.SMEM if number < smem else pltpu.VMEM)
         for number in range(len(operands))
     ]
+    out_specs = jax.tree.map(lambda _: pl.BlockSpec(memory_space=pltpu.VMEM), out_shape)
+    aliases = {}
+    if passed:
+        specs[-1] = out_specs[-1] = pl.BlockSpec(memory_space=pl.ANY)
+        aliases = {len(specs) - 1: len(out_specs) - 1}
     return pl.pallas_call(
         kernel,
         out_shape=out_shape,
         in_specs=specs,
-        out_specs=jax.tree.map(lambda _: pl.BlockSpec(memory_space=pltpu.VMEM), out_shape),
+        out_specs=out_specs,
+        input_output_aliases=aliases,
         scratch_shapes=list(scratch),
         compiler_params=pltpu.CompilerParams(vmem_limit_bytes=vmem * MIB),
         cost_estimate=pl.CostEstimate(
@@ -539,12 +572,15 @@
     )
     wide = [across(first, 2), across(second, 3)]
     core = across(core, 1)
-    own_chip, *picks = call(
+    own_chip, first, second, relay, selects, spreads, own_picked, own_tight = call(
         functools.partial(own_chip_kernel, sets, rows, dim),
-        [shape(each, 2, rows, LANES, dtype=jnp.float32)] + [shape(each * tall, LANES)] * 2,
+        [shape(each, 2, rows, LANES, dtype=jnp.float32)] + [shape(each * tall, LANES)] * 2
+        + [shape(6 * rows, LANES)]
+        + [shape(each, rows, rows)] * 2
+        + [shape(2, rows, LANES), shape(each, 2, rows // 2, LANES)],
         2,
-        (head_offset, index, own, core),
-        2.0,
+        (head_offset, index, own, core, chip),
+        2.4,
         [pltpu.VMEM((2, rows, LANES), bf16), pltpu.VMEM((each, 2, rows, LANES), bf16)],
         vmem=12,
     )
@@ -553,8 +589,9 @@
         functools.partial(turn_kernel, at),
         [shape(NEAR, all_rows - first, LANES) for first in at] + [shape(6 * rows, LANES)],
         1,
-        (index, *picks, *wide, chip, core),
+        (index, first, second, *wide, relay),
         0.3,
+        passed=True,
     )
     chip = across(relay, 2)
     far = [
@@ -568,12 +605,12 @@
             shape(each, NEAR, rows, LANES, dtype=jnp.float32),
             shape(each, NEAR, rows // 2, LANES, dtype=jnp.float32),
             shape(each, rows // 2, LANES, dtype=jnp.float32),
-            shape(NEAR, even(tall), LANES),
+            shape(NEAR, rows // 2, LANES),
             shape(rows, cols),
         ],
-        2,
-        (head_offset, index, own, core, chip, own_chip, residual_in),
-        4.0,
+        1,
+        (index, chip, own_chip, selects, own_picked, own_tight, residual_in),
+        3.4,
         [
             pltpu.VMEM((2, rows, LANES), bf16),
             pltpu.VMEM((each, 2, rows, LANES), bf16),
@@ -586,7 +623,7 @@
         functools.partial(finish_kernel, sets, rows, dim),
         [shape(rows, LANES)] * NEAR,
         2,
-        (head_offset, index, *far, picked_queries, near, tight_done, tight_top),
+        (head_offset, index, *far, picked_queries, near, tight_done, tight_top, selects, spreads),
         6.0,
         [
             pltpu.VMEM((each, NEAR, rows, LANES), jnp.float32),
@@ -596,8 +633,7 @@
         vmem=16,
     )
     mixes = [across(block, step) for step, block in enumerate(mixes)]
-    held = call(hold_kernel, shape(rows, LANES), 0, (mixes[0], other_weights[1]), 0.2)
-    other_mixes = [lax.ppermute(block, "tp", swap) for block in (held, *mixes[1:])]
+    other_mixes = [lax.ppermute(block, "tp", swap) for block in mixes]
 
     other_residual = lax.ppermute(residual, "tp", swap)
     width = norm_gain.shape[0]

time: 54.7 us -> 53.8 us (0.984)
  starting transfers between devices: 21.3 us -> 20.6 us
    ppermute x4, starting transfers between devices: 5.25 us -> 4.05 us  [shards(): other_mixes = [lax.ppermute(block, 'tp', swap) for block in mixes]]
    pallas_call x10 -> x9, Pallas kernels: 17 us -> 16.7 us  [call(): pl.pallas_call(kernel, out_shape=out_shape, in_specs=specs, out_specs=out...]
  transfers between devices with their start and end apart: 19 -> 19, of which waited for: 9 -> 10; matrix products, arithmetic and copies ran while one was open for 0% -> 0% of each run, Pallas kernels for 24% -> 24%
where the time goes in v2:
time: 53.8 us; the launch traced here: 53.6 us
  starting transfers between devices  20.6 us (38%)
  Pallas kernels  16.7 us (31%)
  waiting for transfers between devices  14.9 us (28%)
  other arithmetic  1.23 us (2%)
    pallas_call x9, Pallas kernels, call(): pl.pallas_call(kernel, out_shape=out_shape, in_specs=specs, out_specs=out...  16.7 us
    ppermute x11, starting transfers between devices, across(): lax.ppermute(block, 'seq', [(i, i ^ distance) for i in range(seq_count)])  11.1 us
    ppermute x11, waiting for transfers between devices, across(): lax.ppermute(block, 'seq', [(i, i ^ distance) for i in range(seq_count)])  4.1 us
    ppermute x1, waiting for transfers between devices, shards(): part = lax.ppermute(part, 'tp', swap)  4.09 us
    ppermute x4, starting transfers between devices, shards(): other_mixes = [lax.ppermute(block, 'tp', swap) for block in mixes]  4.05 us
    ppermute x2, waiting for transfers between devices, shards(): theirs.append(lax.ppermute(send, 'tp', swap))  4 us
    ppermute x4, waiting for transfers between devices, shards(): other_mixes = [lax.ppermute(block, 'tp', swap) for block in mixes]  2.7 us
    ppermute x2, starting transfers between devices, shards(): theirs.append(lax.ppermute(send, 'tp', swap))  2.15 us
  transfers between devices with their start and end apart: 19, of which 10 were waited for; matrix products, arithmetic and copies ran while one was open for 0% of the time, Pallas kernels for 24%

profile of v2, /device:TPU:0, one launch (start us, length us, event | category | flops | bytes accessed | tf_op | source)
XLA Modules:
  0.0 53.6 jit_solution(14239772914860405701)
XLA Ops:
  0.0 0.0 copy-start.6
  0.0 0.1 pad_add_fusion.index_ref
  0.1 1.2 %pad_maximum_fusion.source_ref = bf16[768,512]{1,0:T(8,128)(2,1)S(1)} fusion(bf16[256,512]{1,0:T(8,128)(2,1)} %param.13, bf16[256,512]{1,0:T(8,128)(2,1)} %param.12, bf16[256,512]{1,0:T(8,128)(2,1)} %param.11), kind=kLoop, calls=%fused_computation | loop fusion | flops 2359296 | bytes 1572864 | tf_op jit(solution)/shard_map/concatenate | solution.py:563
  1.2 0.0 copy-done.6
  1.2 0.0 copy-start.3
  1.3 1.0 %shard_map.100 = (bf16[240,128]{1,0:T(8,128)(2,1)S(1)}, bf16[240,128]{1,0:T(8,128)(2,1)S(1)}, bf16[768,128]{1,0:T(8,128)(2,1)S(1)}, bf16[1536,128]{1,0:T(8,128)(2,1)S(1)}, bf16[768,128]{1,0:T(8,128)(2,1)S(1)}) custom-call(s32[6,8]{1,0:T(8,128)S(1)} %copy-done.6, s32[2]{0:T(128)S(1)} %pad_add_fusion.index_ref, bf16[768,512]{1,0:T(8,128)(2,1)S(1)} %pad_maximum_fusion.source_ref), custom_call_target="tpu_custom_call" | custom-call | flops 1153500032 | tf_op jit(solution)/shard_map/pallas_call | solution.py:513
  2.3 0.5 collective-permute-start
  2.8 2.6 %collective-permute-start.1 = (bf16[240,128]{1,0:T(8,128)(2,1)S(1)}, bf16[240,128]{1,0:T(8,128)(2,1)S(1)}, u32[]{:S(2)}, u32[]{:S(2)}) collective-permute-start(bf16[240,128]{1,0:T(8,128)(2,1)S(1)} %get-tuple-element.39), channel_id=1, source_target_pairs={{0,4},{2,6},{4,0},{6,2},{8,12},{10,14},{12,8},{14,10},{16,20},{18,... | collective-permute-start | bytes 184328 | tf_op jit(solution)/shard_map/ppermute | solution.py:555
  5.4 0.1 collective-permute-start.2
  5.4 0.0 copy-done.3
  5.5 1.8 %collective-permute-start.15 = (bf16[256,1024]{1,0:T(8,128)(2,1)S(1)}, bf16[256,1024]{1,0:T(8,128)(2,1)S(1)}, u32[]{:S(2)}, u32[]{:S(2)}) collective-permute-start(bf16[256,1024]{1,0:T(8,128)(2,1)S(1)} %constant_dynamic-slice_fusion), channel_id=1, source_target_pairs={{0,1},{1,0},{2,3},{3,2},{4,5},{5,4},{6,7},{7,6},{8,9},{9,8},{10,11... | collective-permute-start | bytes 1572872 | tf_op jit(solution)/shard_map/ppermute | solution.py:560
  7.2 0.0 collective-permute-done.pair_ref
  7.2 0.0 copy-start.5
  7.3 2.0 %shard_map.101 = (f32[2,2,256,128]{3,2,1,0:T(8,128)S(1)}, bf16[240,128]{1,0:T(8,128)(2,1)S(1)}, bf16[240,128]{1,0:T(8,128)(2,1)S(1)}, bf16[1536,128]{1,0:T(8,128...) custom-call(s32[6,8]{1,0:T(8,128)S(1)} %copy-done.6, ...), custom_call_target="tpu_custom_call" | custom-call | flops 2768399872 | tf_op jit(solution)/shard_map/pallas_call | solution.py:513
  9.2 0.0 collective-permute-done.1.refs_2_
  9.2 0.1 collective-permute-done.2.refs_3_
  9.3 0.6 %shard_map.102 = (bf16[4,240,128]{2,1,0:T(8,128)(2,1)S(1)}, bf16[4,112,128]{2,1,0:T(8,128)(2,1)S(1)}, bf16[1536,128]{1,0:T(8,128)(2,1)S(1)}) custom-call(s32[2]{0:T(128)S(1)} %pad_add_fusion.index_ref, bf16[240,128]{1,0:T(8,128)(2,1)S(1)} %get-tuple-element.37.refs_0_, ...), custom_call_target="tpu_custom_call", output_to_operand_aliasing={{2}: (5, {})} | custom-call | flops 346049984 | tf_op jit(solution)/shard_map/pallas_call | solution.py:513
  9.9 1.5 %collective-permute-start.3 = (bf16[1536,128]{1,0:T(8,128)(2,1)S(1)}, bf16[1536,128]{1,0:T(8,128)(2,1)S(1)}, u32[]{:S(2)}, u32[]{:S(2)}) collective-permute-start(bf16[1536,128]{1,0:T(8,128)(2,1)S(1)} %get-tuple-element.42), channel_id=1, source_target_pairs={{0,4},{2,6},{4,0},{6,2},{8,12},{10,14},{12,8},{14,10},{16,20},{18,... | collective-permute-start | bytes 1179656 | tf_op jit(solution)/shard_map/ppermute | solution.py:555
  11.4 2.6 %collective-permute-start.6 = (bf16[4,112,128]{2,1,0:T(8,128)(2,1)S(1)}, bf16[4,112,128]{2,1,0:T(8,128)(2,1)S(1)}, u32[]{:S(2)}, u32[]{:S(2)}) collective-permute-start(bf16[4,112,128]{2,1,0:T(8,128)(2,1)S(1)} %get-tuple-element.49), channel_id=1, source_target_pairs={{0,16},{2,18},{4,20},{6,22},{8,24},{10,26},{12,28},{14,30},{16,0},... | collective-permute-start | bytes 344072 | tf_op jit(solution)/shard_map/ppermute | solution.py:555
  14.0 1.4 %collective-permute-start.7 = (bf16[4,112,128]{2,1,0:T(8,128)(2,1)S(1)}, bf16[4,112,128]{2,1,0:T(8,128)(2,1)S(1)}, u32[]{:S(2)}, u32[]{:S(2)}) collective-permute-start(bf16[4,112,128]{2,1,0:T(8,128)(2,1)S(1)} %get-tuple-element.49), channel_id=1, source_target_pairs={{0,24},{2,26},{4,28},{6,30},{8,16},{10,18},{12,20},{14,22},{16,8},... | collective-permute-start | bytes 344072 | tf_op jit(solution)/shard_map/ppermute | solution.py:555
  15.4 0.2 collective-permute-start.5
  15.6 4.1 %collective-permute-done.15.refs_4_ = bf16[256,1024]{1,0:T(8,128)(2,1)S(1)} collective-permute-done((bf16[256,1024]{1,0:T(8,128)(2,1)S(1)}, bf16[256,1024]{1,0:T(8,128)(2,1)S(1)}, u32[]{:S(2)}, u32[]{:S(2)}) %collective-permute-start.15) | collective-permute-done | bytes 524320 | tf_op jit(solution)/shard_map/ppermute | solution.py:560
  19.7 0.0 collective-permute-start.16
  19.7 1.8 %collective-permute-done.3.refs_0_ = bf16[1536,128]{1,0:T(8,128)(2,1)S(1)} collective-permute-done((bf16[1536,128]{1,0:T(8,128)(2,1)S(1)}, bf16[1536,128]{1,0:T(8,128)(2,1)S(1)}, u32[]{:S(2)}, u32[]{:S(2)}) %collective-permute-start.3) | collective-permute-done | bytes 393248 | tf_op jit(solution)/shard_map/ppermute | solution.py:555
  21.5 0.0 copy-done.5
  21.5 3.1 %shard_map.103 = (f32[2,4,256,128]{3,2,1,0:T(8,128)S(1)}, f32[2,4,128,128]{3,2,1,0:T(8,128)S(1)}, f32[2,128,128]{2,1,0:T(8,128)S(1)}, bf16[4,128,128]{2,1,0:T(8,128)(2,1)S(1)}, bf16[256,512]{1,0:T(8,128)(2,1)S(1)}) custom-call(s32[2]{0:T(128)S(1)} %pad_add_fusion.index_ref, bf16[1536,128]{1,0:T(8,128)(2,1)S(1)} %collective-permute-done.3.refs_0_, ...), custom_call_target="tpu_custom_call" | custom-call | flops 3921900032 | tf_op jit(solution)/shard_map/pallas_call | solution.py:513
  24.6 1.6 %collective-permute-start.4 = (bf16[256,512]{1,0:T(8,128)(2,1)S(1)}, bf16[256,512]{1,0:T(8,128)(2,1)S(1)}, u32[]{:S(2)}, u32[]{:S(2)}) collective-permute-start(bf16[256,512]{1,0:T(8,128)(2,1)S(1)} %get-tuple-element.47), channel_id=1, source_target_pairs={{0,1},{1,0},{2,3},{3,2},{4,5},{5,4},{6,7},{7,6},{8,9},{9,8},{10,11... | collective-permute-start | bytes 786440 | tf_op jit(solution)/shard_map/ppermute | solution.py:638
  26.2 0.0 collective-permute-done.6.refs_2_
  26.2 0.0 collective-permute-done.7.refs_3_
  26.2 0.4 collective-permute-done.5.refs_1_
  26.6 0.0 copy-start.2
  26.6 4.2 %shard_map.104 = (bf16[256,128]{1,0:T(8,128)(2,1)S(1)}, bf16[256,128]{1,0:T(8,128)(2,1)S(1)}, bf16[256,128]{1,0:T(8,128)(2,1)S(1)}, bf16[256,128]{1,0:T(8,128)(2,1)S(1)}) custom-call(s32[6,8]{1,0:T(8,128)S(1)} %copy-done.6, s32[2]{0:T(128)S(1)} %pad_add_fusion.index_ref, bf16[4,240,128]{2,1,0:T(8,128)(2,1)S(1)} %get-tuple-element.48.refs_0_, ...), custom_call_target="tpu_custom_call" | custom-call | flops 6920999936 | tf_op jit(solution)/shard_map/pallas_call | solution.py:513
  30.8 0.1 collective-permute-start.10
  31.0 1.0 %collective-permute-start.8 = (bf16[256,128]{1,0:T(8,128)(2,1)S(1)}, bf16[256,128]{1,0:T(8,128)(2,1)S(1)}, u32[]{:S(2)}, u32[]{:S(2)}) collective-permute-start(bf16[256,128]{1,0:T(8,128)(2,1)S(1)} %get-tuple-element.56), channel_id=1, source_target_pairs={{0,2},{2,0},{4,6},{6,4},{8,10},{10,8},{12,14},{14,12},{16,18},{18,... | collective-permute-start | bytes 196616 | tf_op jit(solution)/shard_map/ppermute | solution.py:555
  32.0 1.1 %collective-permute-start.9 = (bf16[256,128]{1,0:T(8,128)(2,1)S(1)}, bf16[256,128]{1,0:T(8,128)(2,1)S(1)}, u32[]{:S(2)}, u32[]{:S(2)}) collective-permute-start(bf16[256,128]{1,0:T(8,128)(2,1)S(1)} %get-tuple-element.57), channel_id=1, source_target_pairs={{0,4},{2,6},{4,0},{6,2},{8,12},{10,14},{12,8},{14,10},{16,20},{18,... | collective-permute-start | bytes 196616 | tf_op jit(solution)/shard_map/ppermute | solution.py:555
  33.1 1.8 %collective-permute-done.10.refs_3_ = bf16[256,128]{1,0:T(8,128)(2,1)S(1)} collective-permute-done((bf16[256,128]{1,0:T(8,128)(2,1)S(1)}, bf16[256,128]{1,0:T(8,128)(2,1)S(1)}, u32[]{:S(2)}, u32[]{:S(2)}) %collective-permute-start.10) | collective-permute-done | bytes 65568 | tf_op jit(solution)/shard_map/ppermute | solution.py:555
  34.8 0.0 copy-start
  34.8 0.0 copy-start.1
  34.8 0.0 copy-start.4
  34.8 1.3 %collective-permute-start.11 = (bf16[256,128]{1,0:T(8,128)(2,1)S(1)}, bf16[256,128]{1,0:T(8,128)(2,1)S(1)}, u32[]{:S(2)}, u32[]{:S(2)}) collective-permute-start(bf16[256,128]{1,0:T(8,128)(2,1)S(1)} %get-tuple-element.55.refs_0_), channel_id=1, source_target_pairs={{0,1},{1,0},{2,3},{3,2},{4,5},{5,4},{6,7},{7,6},{8,9},{9,8},{10,11... | collective-permute-start | bytes 196616 | tf_op jit(solution)/shard_map/ppermute | solution.py:636
  36.1 0.0 collective-permute-done.8.refs_1_
  36.1 0.8 %collective-permute-start.12 = (bf16[256,128]{1,0:T(8,128)(2,1)S(1)}, bf16[256,128]{1,0:T(8,128)(2,1)S(1)}, u32[]{:S(2)}, u32[]{:S(2)}) collective-permute-start(bf16[256,128]{1,0:T(8,128)(2,1)S(1)} %collective-permute-done.8.refs_1_), channel_id=1, source_target_pairs={{0,1},{1,0},{2,3},{3,2},{4,5},{5,4},{6,7},{7,6},{8,9},{9,8},{10,11... | collective-permute-start | bytes 196616 | tf_op jit(solution)/shard_map/ppermute | solution.py:636
  36.8 0.0 collective-permute-done.9.refs_2_
  36.8 1.3 %collective-permute-start.13 = (bf16[256,128]{1,0:T(8,128)(2,1)S(1)}, bf16[256,128]{1,0:T(8,128)(2,1)S(1)}, u32[]{:S(2)}, u32[]{:S(2)}) collective-permute-start(bf16[256,128]{1,0:T(8,128)(2,1)S(1)} %collective-permute-done.9.refs_2_), channel_id=1, source_target_pairs={{0,1},{1,0},{2,3},{3,2},{4,5},{5,4},{6,7},{7,6},{8,9},{9,8},{10,11... | collective-permute-start | bytes 196616 | tf_op jit(solution)/shard_map/ppermute | solution.py:636
  38.1 0.0 collective-permute-done.4.other_residual_ref
  38.1 0.8 %collective-permute-start.14 = (bf16[256,128]{1,0:T(8,128)(2,1)S(1)}, bf16[256,128]{1,0:T(8,128)(2,1)S(1)}, u32[]{:S(2)}, u32[]{:S(2)}) collective-permute-start(bf16[256,128]{1,0:T(8,128)(2,1)S(1)} %collective-permute-done.10.refs_3_), channel_id=1, source_target_pairs={{0,1},{1,0},{2,3},{3,2},{4,5},{5,4},{6,7},{7,6},{8,9},{9,8},{10,11... | collective-permute-start | bytes 196616 | tf_op jit(solution)/shard_map/ppermute | solution.py:636
  38.9 1.1 %shard_map.105.own_ref = f32[256,1024]{1,0:T(8,128)S(1)} custom-call(s32[2]{0:T(128)S(1)} %pad_add_fusion.index_ref, bf16[256,512]{1,0:T(8,128)(2,1)S(1)} %copy-done.5, bf16[256,512]{1,0:T(8,128)(2,1)S(1)} %collective-permute-done.4.other_residual_ref, bf16[512,1024]{1,0:T(8,128)(2,1)S(1)} %copy-done.3, bf16[256,128]{1,0:T(8,128)(2,1)S(1)} %get-tuple-element.55.refs_0_, ...), custom_call_target="tpu_custom_call" | custom-call | flops 1384199936 | tf_op jit(solution)/shard_map/pallas_call | solution.py:513
  40.0 0.0 collective-permute-done.11.refs_0_
  40.0 1.2 %collective-permute-done.12.refs_1_ = bf16[256,128]{1,0:T(8,128)(2,1)S(1)} collective-permute-done((bf16[256,128]{1,0:T(8,128)(2,1)S(1)}, bf16[256,128]{1,0:T(8,128)(2,1)S(1)}, u32[]{:S(2)}, u32[]{:S(2)}) %collective-permute-start.12) | collective-permute-done | bytes 65568 | tf_op jit(solution)/shard_map/ppermute | solution.py:636
  41.2 0.8 %collective-permute-done.13.refs_2_ = bf16[256,128]{1,0:T(8,128)(2,1)S(1)} collective-permute-done((bf16[256,128]{1,0:T(8,128)(2,1)S(1)}, bf16[256,128]{1,0:T(8,128)(2,1)S(1)}, u32[]{:S(2)}, u32[]{:S(2)}) %collective-permute-start.13) | collective-permute-done | bytes 65568 | tf_op jit(solution)/shard_map/ppermute | solution.py:636
  42.0 0.7 %collective-permute-done.14.refs_3_ = bf16[256,128]{1,0:T(8,128)(2,1)S(1)} collective-permute-done((bf16[256,128]{1,0:T(8,128)(2,1)S(1)}, bf16[256,128]{1,0:T(8,128)(2,1)S(1)}, u32[]{:S(2)}, u32[]{:S(2)}) %collective-permute-start.14) | collective-permute-done | bytes 65568 | tf_op jit(solution)/shard_map/ppermute | solution.py:636
  42.7 0.0 collective-permute-done.16.refs_5_
  42.7 0.0 copy-done.2
  42.7 0.0 copy-done
  42.7 0.0 copy-done.1
  42.7 0.0 copy-done.4
  42.7 2.0 %shard_map.107 = (bf16[128,512]{1,0:T(8,128)(2,1)S(1)}, f32[128,512]{1,0:T(8,128)S(1)}) custom-call(s32[2]{0:T(128)S(1)} %pad_add_fusion.index_ref, f32[256,1024]{1,0:T(8,128)S(1)} %shard_map.105.own_ref, bf16[256,128]{1,0:T(8,128)(2,1)S(1)} %collective-permute-done.11.refs_0_, bf16[256,128]{1,0:T(8,128)(2,1)S(1)} %collective-permute-done.12.refs_1_, ...), custom_call_target="tpu_custom_call" | custom-call | flops 2307000064 | tf_op jit(solution)/shard_map/pallas_call | solution.py:513
  44.7 1.1 %collective-permute-start.18 = (bf16[128,512]{1,0:T(8,128)(2,1)S(1)}, bf16[128,512]{1,0:T(8,128)(2,1)S(1)}, u32[]{:S(2)}, u32[]{:S(2)}) collective-permute-start(bf16[128,512]{1,0:T(8,128)(2,1)S(1)} %get-tuple-element.62), channel_id=1, source_target_pairs={{0,1},{1,0},{2,3},{3,2},{4,5},{5,4},{6,7},{7,6},{8,9},{9,8},{10,11... | collective-permute-start | bytes 393224 | tf_op jit(solution)/shard_map/ppermute | solution.py:674
  45.8 2.0 %shard_map.106 = (bf16[128,512]{1,0:T(8,128)(2,1)S(1)}, f32[128,512]{1,0:T(8,128)S(1)}) custom-call(s32[2]{0:T(128)S(1)} %pad_add_fusion.index_ref, f32[256,1024]{1,0:T(8,128)S(1)} %shard_map.105.own_ref, bf16[256,128]{1,0:T(8,128)(2,1)S(1)} %collective-permute-done.11.refs_0_, bf16[256,128]{1,0:T(8,128)(2,1)S(1)} %collective-permute-done.12.refs_1_, ...), custom_call_target="tpu_custom_call" | custom-call | flops 2307000064 | tf_op jit(solution)/shard_map/pallas_call | solution.py:513
  47.8 1.0 %collective-permute-start.17 = (bf16[128,512]{1,0:T(8,128)(2,1)S(1)}, bf16[128,512]{1,0:T(8,128)(2,1)S(1)}, u32[]{:S(2)}, u32[]{:S(2)}) collective-permute-start(bf16[128,512]{1,0:T(8,128)(2,1)S(1)} %get-tuple-element.61), channel_id=1, source_target_pairs={{0,1},{1,0},{2,3},{3,2},{4,5},{5,4},{6,7},{7,6},{8,9},{9,8},{10,11... | collective-permute-start | bytes 393224 | tf_op jit(solution)/shard_map/ppermute | solution.py:674
  48.9 1.8 %collective-permute-done.18.refs_3_ = bf16[128,512]{1,0:T(8,128)(2,1)S(1)} collective-permute-done((bf16[128,512]{1,0:T(8,128)(2,1)S(1)}, bf16[128,512]{1,0:T(8,128)(2,1)S(1)}, u32[]{:S(2)}, u32[]{:S(2)}) %collective-permute-start.18) | collective-permute-done | bytes 131104 | tf_op jit(solution)/shard_map/ppermute | solution.py:674
  50.7 2.2 %collective-permute-done.17.refs_2_ = bf16[128,512]{1,0:T(8,128)(2,1)S(1)} collective-permute-done((bf16[128,512]{1,0:T(8,128)(2,1)S(1)}, bf16[128,512]{1,0:T(8,128)(2,1)S(1)}, u32[]{:S(2)}, u32[]{:S(2)}) %collective-permute-start.17) | collective-permute-done | bytes 131104 | tf_op jit(solution)/shard_map/ppermute | solution.py:674
  52.9 0.8 %shard_map.108 = bf16[256,512]{1,0:T(8,128)(2,1)} custom-call(f32[128,512]{1,0:T(8,128)S(1)} %get-tuple-element.59.refs_0_, f32[128,512]{1,0:T(8,128)S(1)} %get-tuple-element.60.refs_1_, bf16[128,512]{1,0:T(8,128)(2,1)S(1)} %collective-permute-done.17.refs_2_, bf16[128,512]{1,0:T(8,128)(2,1)S(1)} %collective-permute-done.18.refs_3_), custom_call_target="tpu_custom_call" | custom-call | flops 922800000 | tf_op jit(solution)/shard_map/pallas_call | solution.py:513
  (1 shorter events, 0.0 us)
Async XLA Ops:
  0.0 1.2 %copy-start.6 = (s32[6,8]{1,0:T(8,128)S(1)}, s32[6,8]{1,0:T(8,128)}, u32[]{:S(2)}) copy-start(s32[6,8]{1,0:T(8,128)} %offset_ref.5) | copy-start | bytes 580
  1.2 4.2 %copy-start.3 = (bf16[512,1024]{1,0:T(8,128)(2,1)S(1)}, bf16[512,1024]{1,0:T(8,128)(2,1)}, u32[]{:S(2)}) copy-start(bf16[512,1024]{1,0:T(8,128)(2,1)} %weight_ref.1) | copy-start | bytes 3145732
  2.3 5.0 %collective-permute-start = (bf16[1536,128]{1,0:T(8,128)(2,1)S(1)}, bf16[1536,128]{1,0:T(8,128)(2,1)S(1)}, u32[]{:S(2)}, u32[]{:S(2)}) collective-permute-start(bf16[1536,128]{1,0:T(8,128)(2,1)S(1)} %get-tuple-element.35), channel_id=1, source_target_pairs={{0,2},{2,0},{4,6},{6,4},{8,10},{10,8},{12,14},{14,12},{16,18},{18,... | collective-permute-start | bytes 1179656 | tf_op jit(solution)/shard_map/ppermute | solution.py:555
  2.8 6.4 %collective-permute-start.1 = (bf16[240,128]{1,0:T(8,128)(2,1)S(1)}, bf16[240,128]{1,0:T(8,128)(2,1)S(1)}, u32[]{:S(2)}, u32[]{:S(2)}) collective-permute-start(bf16[240,128]{1,0:T(8,128)(2,1)S(1)} %get-tuple-element.39), channel_id=1, source_target_pairs={{0,4},{2,6},{4,0},{6,2},{8,12},{10,14},{12,8},{14,10},{16,20},{18,... | collective-permute-start | bytes 184328 | tf_op jit(solution)/shard_map/ppermute | solution.py:555
  5.4 4.0 %collective-permute-start.2 = (bf16[240,128]{1,0:T(8,128)(2,1)S(1)}, bf16[240,128]{1,0:T(8,128)(2,1)S(1)}, u32[]{:S(2)}, u32[]{:S(2)}) collective-permute-start(bf16[240,128]{1,0:T(8,128)(2,1)S(1)} %get-tuple-element.40), channel_id=1, source_target_pairs={{0,6},{2,4},{4,2},{6,0},{8,14},{10,12},{12,10},{14,8},{16,22},{18,... | collective-permute-start | bytes 184328 | tf_op jit(solution)/shard_map/ppermute | solution.py:555
  5.5 14.2 %collective-permute-start.15 = (bf16[256,1024]{1,0:T(8,128)(2,1)S(1)}, bf16[256,1024]{1,0:T(8,128)(2,1)S(1)}, u32[]{:S(2)}, u32[]{:S(2)}) collective-permute-start(bf16[256,1024]{1,0:T(8,128)(2,1)S(1)} %constant_dynamic-slice_fusion), channel_id=1, source_target_pairs={{0,1},{1,0},{2,3},{3,2},{4,5},{5,4},{6,7},{7,6},{8,9},{9,8},{10,11... | collective-permute-start | bytes 1572872 | tf_op jit(solution)/shard_map/ppermute | solution.py:560
  7.2 14.2 %copy-start.5 = (bf16[256,512]{1,0:T(8,128)(2,1)S(1)}, bf16[256,512]{1,0:T(8,128)(2,1)}, u32[]{:S(2)}) copy-start(bf16[256,512]{1,0:T(8,128)(2,1)} %residual_ref.1) | copy-start | bytes 786436
  9.9 11.5 %collective-permute-start.3 = (bf16[1536,128]{1,0:T(8,128)(2,1)S(1)}, bf16[1536,128]{1,0:T(8,128)(2,1)S(1)}, u32[]{:S(2)}, u32[]{:S(2)}) collective-permute-start(bf16[1536,128]{1,0:T(8,128)(2,1)S(1)} %get-tuple-element.42), channel_id=1, source_target_pairs={{0,4},{2,6},{4,0},{6,2},{8,12},{10,14},{12,8},{14,10},{16,20},{18,... | collective-permute-start | bytes 1179656 | tf_op jit(solution)/shard_map/ppermute | solution.py:555
  11.4 14.7 %collective-permute-start.6 = (bf16[4,112,128]{2,1,0:T(8,128)(2,1)S(1)}, bf16[4,112,128]{2,1,0:T(8,128)(2,1)S(1)}, u32[]{:S(2)}, u32[]{:S(2)}) collective-permute-start(bf16[4,112,128]{2,1,0:T(8,128)(2,1)S(1)} %get-tuple-element.49), channel_id=1, source_target_pairs={{0,16},{2,18},{4,20},{6,22},{8,24},{10,26},{12,28},{14,30},{16,0},... | collective-permute-start | bytes 344072 | tf_op jit(solution)/shard_map/ppermute | solution.py:555
  14.0 12.2 %collective-permute-start.7 = (bf16[4,112,128]{2,1,0:T(8,128)(2,1)S(1)}, bf16[4,112,128]{2,1,0:T(8,128)(2,1)S(1)}, u32[]{:S(2)}, u32[]{:S(2)}) collective-permute-start(bf16[4,112,128]{2,1,0:T(8,128)(2,1)S(1)} %get-tuple-element.49), channel_id=1, source_target_pairs={{0,24},{2,26},{4,28},{6,30},{8,16},{10,18},{12,20},{14,22},{16,8},... | collective-permute-start | bytes 344072 | tf_op jit(solution)/shard_map/ppermute | solution.py:555
  15.4 11.2 %collective-permute-start.5 = (bf16[4,240,128]{2,1,0:T(8,128)(2,1)S(1)}, bf16[4,240,128]{2,1,0:T(8,128)(2,1)S(1)}, u32[]{:S(2)}, u32[]{:S(2)}) collective-permute-start(bf16[4,240,128]{2,1,0:T(8,128)(2,1)S(1)} %get-tuple-element.48.refs_0_), channel_id=1, source_target_pairs={{0,8},{2,10},{4,12},{6,14},{8,0},{10,2},{12,4},{14,6},{16,24},{18,... | collective-permute-start | bytes 737288 | tf_op jit(solution)/shard_map/ppermute | solution.py:555
  19.7 23.0 %collective-permute-start.16 = (bf16[256,1024]{1,0:T(8,128)(2,1)S(1)}, bf16[256,1024]{1,0:T(8,128)(2,1)S(1)}, u32[]{:S(2)}, u32[]{:S(2)}) collective-permute-start(bf16[256,1024]{1,0:T(8,128)(2,1)S(1)} %collective-permute-done.15.refs_4_), channel_id=1, source_target_pairs={{0,2},{2,0},{4,6},{6,4},{8,10},{10,8},{12,14},{14,12},{16,18},{18,... | collective-permute-start | bytes 1572872 | tf_op jit(solution)/shard_map/ppermute | solution.py:555
  24.6 13.5 %collective-permute-start.4 = (bf16[256,512]{1,0:T(8,128)(2,1)S(1)}, bf16[256,512]{1,0:T(8,128)(2,1)S(1)}, u32[]{:S(2)}, u32[]{:S(2)}) collective-permute-start(bf16[256,512]{1,0:T(8,128)(2,1)S(1)} %get-tuple-element.47), channel_id=1, source_target_pairs={{0,1},{1,0},{2,3},{3,2},{4,5},{5,4},{6,7},{7,6},{8,9},{9,8},{10,11... | collective-permute-start | bytes 786440 | tf_op jit(solution)/shard_map/ppermute | solution.py:638
  26.6 16.1 %copy-start.2 = (bf16[1024,1024]{1,0:T(8,128)(2,1)S(1)}, bf16[1024,1024]{1,0:T(8,128)(2,1)}, u32[]{:S(2)}) copy-start(bf16[1024,1024]{1,0:T(8,128)(2,1)} %refs_9_.3) | copy-start | bytes 6291460
  30.8 4.0 %collective-permute-start.10 = (bf16[256,128]{1,0:T(8,128)(2,1)S(1)}, bf16[256,128]{1,0:T(8,128)(2,1)S(1)}, u32[]{:S(2)}, u32[]{:S(2)}) collective-permute-start(bf16[256,128]{1,0:T(8,128)(2,1)S(1)} %get-tuple-element.58), channel_id=1, source_target_pairs={{0,6},{2,4},{4,2},{6,0},{8,14},{10,12},{12,10},{14,8},{16,22},{18,... | collective-permute-start | bytes 196616 | tf_op jit(solution)/shard_map/ppermute | solution.py:555
  31.0 5.1 %collective-permute-start.8 = (bf16[256,128]{1,0:T(8,128)(2,1)S(1)}, bf16[256,128]{1,0:T(8,128)(2,1)S(1)}, u32[]{:S(2)}, u32[]{:S(2)}) collective-permute-start(bf16[256,128]{1,0:T(8,128)(2,1)S(1)} %get-tuple-element.56), channel_id=1, source_target_pairs={{0,2},{2,0},{4,6},{6,4},{8,10},{10,8},{12,14},{14,12},{16,18},{18,... | collective-permute-start | bytes 196616 | tf_op jit(solution)/shard_map/ppermute | solution.py:555
  32.0 4.9 %collective-permute-start.9 = (bf16[256,128]{1,0:T(8,128)(2,1)S(1)}, bf16[256,128]{1,0:T(8,128)(2,1)S(1)}, u32[]{:S(2)}, u32[]{:S(2)}) collective-permute-start(bf16[256,128]{1,0:T(8,128)(2,1)S(1)} %get-tuple-element.57), channel_id=1, source_target_pairs={{0,4},{2,6},{4,0},{6,2},{8,12},{10,14},{12,8},{14,10},{16,20},{18,... | collective-permute-start | bytes 196616 | tf_op jit(solution)/shard_map/ppermute | solution.py:555
  34.8 7.9 %copy-start = (bf16[1024,1024]{1,0:T(8,128)(2,1)S(1)}, bf16[1024,1024]{1,0:T(8,128)(2,1)}, u32[]{:S(2)}) copy-start(bf16[1024,1024]{1,0:T(8,128)(2,1)} %refs_7_.3) | copy-start | bytes 6291460
  34.8 7.9 %copy-start.1 = (bf16[1024,1024]{1,0:T(8,128)(2,1)S(1)}, bf16[1024,1024]{1,0:T(8,128)(2,1)}, u32[]{:S(2)}) copy-start(bf16[1024,1024]{1,0:T(8,128)(2,1)} %refs_8_.3) | copy-start | bytes 6291460
  34.8 7.9 %copy-start.4 = (f32[1024]{0:T(1024)S(1)}, f32[1024]{0:T(1024)}, u32[]{:S(2)}) copy-start(f32[1024]{0:T(1024)} %param.16) | copy-start | bytes 12292
  34.8 5.2 %collective-permute-start.11 = (bf16[256,128]{1,0:T(8,128)(2,1)S(1)}, bf16[256,128]{1,0:T(8,128)(2,1)S(1)}, u32[]{:S(2)}, u32[]{:S(2)}) collective-permute-start(bf16[256,128]{1,0:T(8,128)(2,1)S(1)} %get-tuple-element.55.refs_0_), channel_id=1, source_target_pairs={{0,1},{1,0},{2,3},{3,2},{4,5},{5,4},{6,7},{7,6},{8,9},{9,8},{10,11... | collective-permute-start | bytes 196616 | tf_op jit(solution)/shard_map/ppermute | solution.py:636
  36.1 5.1 %collective-permute-start.12 = (bf16[256,128]{1,0:T(8,128)(2,1)S(1)}, bf16[256,128]{1,0:T(8,128)(2,1)S(1)}, u32[]{:S(2)}, u32[]{:S(2)}) collective-permute-start(bf16[256,128]{1,0:T(8,128)(2,1)S(1)} %collective-permute-done.8.refs_1_), channel_id=1, source_target_pairs={{0,1},{1,0},{2,3},{3,2},{4,5},{5,4},{6,7},{7,6},{8,9},{9,8},{10,11... | collective-permute-start | bytes 196616 | tf_op jit(solution)/shard_map/ppermute | solution.py:636
  36.8 5.2 %collective-permute-start.13 = (bf16[256,128]{1,0:T(8,128)(2,1)S(1)}, bf16[256,128]{1,0:T(8,128)(2,1)S(1)}, u32[]{:S(2)}, u32[]{:S(2)}) collective-permute-start(bf16[256,128]{1,0:T(8,128)(2,1)S(1)} %collective-permute-done.9.refs_2_), channel_id=1, source_target_pairs={{0,1},{1,0},{2,3},{3,2},{4,5},{5,4},{6,7},{7,6},{8,9},{9,8},{10,11... | collective-permute-start | bytes 196616 | tf_op jit(solution)/shard_map/ppermute | solution.py:636
  38.1 4.6 %collective-permute-start.14 = (bf16[256,128]{1,0:T(8,128)(2,1)S(1)}, bf16[256,128]{1,0:T(8,128)(2,1)S(1)}, u32[]{:S(2)}, u32[]{:S(2)}) collective-permute-start(bf16[256,128]{1,0:T(8,128)(2,1)S(1)} %collective-permute-done.10.refs_3_), channel_id=1, source_target_pairs={{0,1},{1,0},{2,3},{3,2},{4,5},{5,4},{6,7},{7,6},{8,9},{9,8},{10,11... | collective-permute-start | bytes 196616 | tf_op jit(solution)/shard_map/ppermute | solution.py:636
  44.7 6.0 %collective-permute-start.18 = (bf16[128,512]{1,0:T(8,128)(2,1)S(1)}, bf16[128,512]{1,0:T(8,128)(2,1)S(1)}, u32[]{:S(2)}, u32[]{:S(2)}) collective-permute-start(bf16[128,512]{1,0:T(8,128)(2,1)S(1)} %get-tuple-element.62), channel_id=1, source_target_pairs={{0,1},{1,0},{2,3},{3,2},{4,5},{5,4},{6,7},{7,6},{8,9},{9,8},{10,11... | collective-permute-start | bytes 393224 | tf_op jit(solution)/shard_map/ppermute | solution.py:674
  47.8 5.0 %collective-permute-start.17 = (bf16[128,512]{1,0:T(8,128)(2,1)S(1)}, bf16[128,512]{1,0:T(8,128)(2,1)S(1)}, u32[]{:S(2)}, u32[]{:S(2)}) collective-permute-start(bf16[128,512]{1,0:T(8,128)(2,1)S(1)} %get-tuple-element.61), channel_id=1, source_target_pairs={{0,1},{1,0},{2,3},{3,2},{4,5},{5,4},{6,7},{7,6},{8,9},{9,8},{10,11... | collective-permute-start | bytes 393224 | tf_op jit(solution)/shard_map/ppermute | solution.py:674

commit v3 on v2

--- a/solution.py
+++ b/solution.py
@@ -338,6 +338,10 @@
         tops[head, into, :] = top_lanes(top, count, branch)
 
 
+def hold_kernel(block_ref, ahead_ref, out_ref):
+    out_ref[...] = block_ref[...]
+
+
 def finish_kernel(sets, rows, dim, offset_ref, index_ref, *refs):
     steps = max(span for span, _ in sets)
     far_refs, refs = refs[:steps], refs[steps:]
@@ -632,7 +636,9 @@
         ],
         vmem=16,
     )
-    mixes = [across(block, step) for step, block in enumerate(mixes)]
+    mixes = [mixes[0], across(mixes[1], 1), across(mixes[2], 2), mixes[3]]
+    held = call(hold_kernel, shape(rows, LANES), 0, (mixes[3], mixes[1]), 0.2)
+    mixes[3] = across(held, 3)
     other_mixes = [lax.ppermute(block, "tp", swap) for block in mixes]
 
     other_residual = lax.ppermute(residual, "tp", swap)

time: 53.8 us -> 54.3 us (level)
    ppermute x4, starting transfers between devices: 4.05 us -> 4.94 us  [shards(): other_mixes = [lax.ppermute(block, 'tp', swap) for block in mixes]]
    pallas_call x9 -> x10, Pallas kernels: 16.7 us -> 16.7 us  [call(): pl.pallas_call(kernel, out_shape=out_shape, in_specs=specs, out_specs=out...]
  transfers between devices with their start and end apart: 19 -> 19, of which waited for: 10 -> 11; matrix products, arithmetic and copies ran while one was open for 0% -> 0% of each run, Pallas kernels for 24% -> 24%
where the time goes in v3:
time: 54.3 us; the launch traced here: 54.2 us
  starting transfers between devices  21 us (39%)
  Pallas kernels  16.7 us (31%)
  waiting for transfers between devices  15 us (28%)
  other arithmetic  1.23 us (2%)
    pallas_call x10, Pallas kernels, call(): pl.pallas_call(kernel, out_shape=out_shape, in_specs=specs, out_specs=out...  16.7 us
    ppermute x11, starting transfers between devices, across(): lax.ppermute(block, 'seq', [(i, i ^ distance) for i in range(seq_count)])  10.6 us
    ppermute x4, starting transfers between devices, shards(): other_mixes = [lax.ppermute(block, 'tp', swap) for block in mixes]  4.94 us
    ppermute x2, waiting for transfers between devices, shards(): theirs.append(lax.ppermute(send, 'tp', swap))  4.4 us
    ppermute x1, waiting for transfers between devices, shards(): part = lax.ppermute(part, 'tp', swap)  4.09 us
    ppermute x11, waiting for transfers between devices, across(): lax.ppermute(block, 'seq', [(i, i ^ distance) for i in range(seq_count)])  4 us
    ppermute x4, waiting for transfers between devices, shards(): other_mixes = [lax.ppermute(block, 'tp', swap) for block in mixes]  2.46 us
    ppermute x2, starting transfers between devices, shards(): theirs.append(lax.ppermute(send, 'tp', swap))  2.14 us
  transfers between devices with their start and end apart: 19, of which 11 were waited for; matrix products, arithmetic and copies ran while one was open for 0% of the time, Pallas kernels for 24%

profile of v3, /device:TPU:0, one launch (start us, length us, event | category | flops | bytes accessed | tf_op | source)
XLA Modules:
  0.0 54.2 jit_solution(9552987877335302742)
XLA Ops:
  0.0 0.0 copy-start.6
  0.0 0.1 pad_add_fusion.index_ref
  0.1 1.2 %pad_maximum_fusion.source_ref = bf16[768,512]{1,0:T(8,128)(2,1)S(1)} fusion(bf16[256,512]{1,0:T(8,128)(2,1)} %param.13, bf16[256,512]{1,0:T(8,128)(2,1)} %param.12, bf16[256,512]{1,0:T(8,128)(2,1)} %param.11), kind=kLoop, calls=%fused_computation | loop fusion | flops 2359296 | bytes 1572864 | tf_op jit(solution)/shard_map/concatenate | solution.py:567
  1.2 0.0 copy-done.6
  1.2 0.0 copy-start.3
  1.3 1.0 %shard_map.100 = (bf16[240,128]{1,0:T(8,128)(2,1)S(1)}, bf16[240,128]{1,0:T(8,128)(2,1)S(1)}, bf16[768,128]{1,0:T(8,128)(2,1)S(1)}, bf16[1536,128]{1,0:T(8,128)(2,1)S(1)}, bf16[768,128]{1,0:T(8,128)(2,1)S(1)}) custom-call(s32[6,8]{1,0:T(8,128)S(1)} %copy-done.6, s32[2]{0:T(128)S(1)} %pad_add_fusion.index_ref, bf16[768,512]{1,0:T(8,128)(2,1)S(1)} %pad_maximum_fusion.source_ref), custom_call_target="tpu_custom_call" | custom-call | flops 1153500032 | tf_op jit(solution)/shard_map/pallas_call | solution.py:517
  2.3 0.5 collective-permute-start
  2.8 2.6 %collective-permute-start.1 = (bf16[240,128]{1,0:T(8,128)(2,1)S(1)}, bf16[240,128]{1,0:T(8,128)(2,1)S(1)}, u32[]{:S(2)}, u32[]{:S(2)}) collective-permute-start(bf16[240,128]{1,0:T(8,128)(2,1)S(1)} %get-tuple-element.39), channel_id=1, source_target_pairs={{0,4},{2,6},{4,0},{6,2},{8,12},{10,14},{12,8},{14,10},{16,20},{18,... | collective-permute-start | bytes 184328 | tf_op jit(solution)/shard_map/ppermute | solution.py:559
  5.4 0.1 collective-permute-start.2
  5.4 0.0 copy-done.3
  5.5 1.8 %collective-permute-start.15 = (bf16[256,1024]{1,0:T(8,128)(2,1)S(1)}, bf16[256,1024]{1,0:T(8,128)(2,1)S(1)}, u32[]{:S(2)}, u32[]{:S(2)}) collective-permute-start(bf16[256,1024]{1,0:T(8,128)(2,1)S(1)} %constant_dynamic-slice_fusion), channel_id=1, source_target_pairs={{0,1},{1,0},{2,3},{3,2},{4,5},{5,4},{6,7},{7,6},{8,9},{9,8},{10,11... | collective-permute-start | bytes 1572872 | tf_op jit(solution)/shard_map/ppermute | solution.py:564
  7.2 0.0 collective-permute-done.pair_ref
  7.2 0.0 copy-start.5
  7.3 2.0 %shard_map.101 = (f32[2,2,256,128]{3,2,1,0:T(8,128)S(1)}, bf16[240,128]{1,0:T(8,128)(2,1)S(1)}, bf16[240,128]{1,0:T(8,128)(2,1)S(1)}, bf16[1536,128]{1,0:T(8,128...) custom-call(s32[6,8]{1,0:T(8,128)S(1)} %copy-done.6, ...), custom_call_target="tpu_custom_call" | custom-call | flops 2768399872 | tf_op jit(solution)/shard_map/pallas_call | solution.py:517
  9.2 0.0 collective-permute-done.1.refs_2_
  9.2 0.1 collective-permute-done.2.refs_3_
  9.3 0.6 %shard_map.102 = (bf16[4,240,128]{2,1,0:T(8,128)(2,1)S(1)}, bf16[4,112,128]{2,1,0:T(8,128)(2,1)S(1)}, bf16[1536,128]{1,0:T(8,128)(2,1)S(1)}) custom-call(s32[2]{0:T(128)S(1)} %pad_add_fusion.index_ref, bf16[240,128]{1,0:T(8,128)(2,1)S(1)} %get-tuple-element.37.refs_0_, ...), custom_call_target="tpu_custom_call", output_to_operand_aliasing={{2}: (5, {})} | custom-call | flops 346049984 | tf_op jit(solution)/shard_map/pallas_call | solution.py:517
  9.9 1.5 %collective-permute-start.3 = (bf16[1536,128]{1,0:T(8,128)(2,1)S(1)}, bf16[1536,128]{1,0:T(8,128)(2,1)S(1)}, u32[]{:S(2)}, u32[]{:S(2)}) collective-permute-start(bf16[1536,128]{1,0:T(8,128)(2,1)S(1)} %get-tuple-element.42), channel_id=1, source_target_pairs={{0,4},{2,6},{4,0},{6,2},{8,12},{10,14},{12,8},{14,10},{16,20},{18,... | collective-permute-start | bytes 1179656 | tf_op jit(solution)/shard_map/ppermute | solution.py:559
  11.4 2.6 %collective-permute-start.6 = (bf16[4,112,128]{2,1,0:T(8,128)(2,1)S(1)}, bf16[4,112,128]{2,1,0:T(8,128)(2,1)S(1)}, u32[]{:S(2)}, u32[]{:S(2)}) collective-permute-start(bf16[4,112,128]{2,1,0:T(8,128)(2,1)S(1)} %get-tuple-element.49), channel_id=1, source_target_pairs={{0,16},{2,18},{4,20},{6,22},{8,24},{10,26},{12,28},{14,30},{16,0},... | collective-permute-start | bytes 344072 | tf_op jit(solution)/shard_map/ppermute | solution.py:559
  14.0 1.4 %collective-permute-start.7 = (bf16[4,112,128]{2,1,0:T(8,128)(2,1)S(1)}, bf16[4,112,128]{2,1,0:T(8,128)(2,1)S(1)}, u32[]{:S(2)}, u32[]{:S(2)}) collective-permute-start(bf16[4,112,128]{2,1,0:T(8,128)(2,1)S(1)} %get-tuple-element.49), channel_id=1, source_target_pairs={{0,24},{2,26},{4,28},{6,30},{8,16},{10,18},{12,20},{14,22},{16,8},... | collective-permute-start | bytes 344072 | tf_op jit(solution)/shard_map/ppermute | solution.py:559
  15.4 0.2 collective-permute-start.5
  15.6 4.1 %collective-permute-done.15.refs_4_ = bf16[256,1024]{1,0:T(8,128)(2,1)S(1)} collective-permute-done((bf16[256,1024]{1,0:T(8,128)(2,1)S(1)}, bf16[256,1024]{1,0:T(8,128)(2,1)S(1)}, u32[]{:S(2)}, u32[]{:S(2)}) %collective-permute-start.15) | collective-permute-done | bytes 524320 | tf_op jit(solution)/shard_map/ppermute | solution.py:564
  19.7 0.0 collective-permute-start.16
  19.7 1.8 %collective-permute-done.3.refs_0_ = bf16[1536,128]{1,0:T(8,128)(2,1)S(1)} collective-permute-done((bf16[1536,128]{1,0:T(8,128)(2,1)S(1)}, bf16[1536,128]{1,0:T(8,128)(2,1)S(1)}, u32[]{:S(2)}, u32[]{:S(2)}) %collective-permute-start.3) | collective-permute-done | bytes 393248 | tf_op jit(solution)/shard_map/ppermute | solution.py:559
  21.5 0.0 copy-done.5
  21.5 3.1 %shard_map.103 = (f32[2,4,256,128]{3,2,1,0:T(8,128)S(1)}, f32[2,4,128,128]{3,2,1,0:T(8,128)S(1)}, f32[2,128,128]{2,1,0:T(8,128)S(1)}, bf16[4,128,128]{2,1,0:T(8,128)(2,1)S(1)}, bf16[256,512]{1,0:T(8,128)(2,1)S(1)}) custom-call(s32[2]{0:T(128)S(1)} %pad_add_fusion.index_ref, bf16[1536,128]{1,0:T(8,128)(2,1)S(1)} %collective-permute-done.3.refs_0_, ...), custom_call_target="tpu_custom_call" | custom-call | flops 3921900032 | tf_op jit(solution)/shard_map/pallas_call | solution.py:517
  24.6 1.6 %collective-permute-start.4 = (bf16[256,512]{1,0:T(8,128)(2,1)S(1)}, bf16[256,512]{1,0:T(8,128)(2,1)S(1)}, u32[]{:S(2)}, u32[]{:S(2)}) collective-permute-start(bf16[256,512]{1,0:T(8,128)(2,1)S(1)} %get-tuple-element.47), channel_id=1, source_target_pairs={{0,1},{1,0},{2,3},{3,2},{4,5},{5,4},{6,7},{7,6},{8,9},{9,8},{10,11... | collective-permute-start | bytes 786440 | tf_op jit(solution)/shard_map/ppermute | solution.py:644
  26.2 0.0 collective-permute-done.6.refs_2_
  26.2 0.0 collective-permute-done.7.refs_3_
  26.2 0.4 collective-permute-done.5.refs_1_
  26.6 0.0 copy-start.2
  26.6 4.2 %shard_map.104 = (bf16[256,128]{1,0:T(8,128)(2,1)S(1)}, bf16[256,128]{1,0:T(8,128)(2,1)S(1)}, bf16[256,128]{1,0:T(8,128)(2,1)S(1)}, bf16[256,128]{1,0:T(8,128)(2,1)S(1)}) custom-call(s32[6,8]{1,0:T(8,128)S(1)} %copy-done.6, s32[2]{0:T(128)S(1)} %pad_add_fusion.index_ref, bf16[4,240,128]{2,1,0:T(8,128)(2,1)S(1)} %get-tuple-element.48.refs_0_, ...), custom_call_target="tpu_custom_call" | custom-call | flops 6920999936 | tf_op jit(solution)/shard_map/pallas_call | solution.py:517
  30.8 0.1 collective-permute-start.8
  30.9 1.0 %collective-permute-start.9 = (bf16[256,128]{1,0:T(8,128)(2,1)S(1)}, bf16[256,128]{1,0:T(8,128)(2,1)S(1)}, u32[]{:S(2)}, u32[]{:S(2)}) collective-permute-start(bf16[256,128]{1,0:T(8,128)(2,1)S(1)} %get-tuple-element.57), channel_id=1, source_target_pairs={{0,4},{2,6},{4,0},{6,2},{8,12},{10,14},{12,8},{14,10},{16,20},{18,... | collective-permute-start | bytes 196616 | tf_op jit(solution)/shard_map/ppermute | solution.py:559
  31.9 0.2 collective-permute-done.8.ahead_ref.refs_1_
  32.2 0.7 %collective-permute-start.10 = (bf16[256,128]{1,0:T(8,128)(2,1)S(1)}, bf16[256,128]{1,0:T(8,128)(2,1)S(1)}, u32[]{:S(2)}, u32[]{:S(2)}) collective-permute-start(bf16[256,128]{1,0:T(8,128)(2,1)S(1)} %shard_map.105), channel_id=1, source_target_pairs={{0,6},{2,4},{4,2},{6,0},{8,14},{10,12},{12,10},{14,8},{16,22},{18,... | collective-permute-start | bytes 196616 | tf_op jit(solution)/shard_map/ppermute | solution.py:559
  32.9 0.0 copy-start
  32.9 0.0 copy-start.1
  32.9 0.0 copy-start.4
  32.9 1.4 %collective-permute-start.11 = (bf16[256,128]{1,0:T(8,128)(2,1)S(1)}, bf16[256,128]{1,0:T(8,128)(2,1)S(1)}, u32[]{:S(2)}, u32[]{:S(2)}) collective-permute-start(bf16[256,128]{1,0:T(8,128)(2,1)S(1)} %get-tuple-element.55.refs_0_), channel_id=1, source_target_pairs={{0,1},{1,0},{2,3},{3,2},{4,5},{5,4},{6,7},{7,6},{8,9},{9,8},{10,11... | collective-permute-start | bytes 196616 | tf_op jit(solution)/shard_map/ppermute | solution.py:642
  34.3 1.4 %collective-permute-done.9.refs_2_ = bf16[256,128]{1,0:T(8,128)(2,1)S(1)} collective-permute-done((bf16[256,128]{1,0:T(8,128)(2,1)S(1)}, bf16[256,128]{1,0:T(8,128)(2,1)S(1)}, u32[]{:S(2)}, u32[]{:S(2)}) %collective-permute-start.9) | collective-permute-done | bytes 65568 | tf_op jit(solution)/shard_map/ppermute | solution.py:559
  35.8 1.5 %collective-permute-start.12 = (bf16[256,128]{1,0:T(8,128)(2,1)S(1)}, bf16[256,128]{1,0:T(8,128)(2,1)S(1)}, u32[]{:S(2)}, u32[]{:S(2)}) collective-permute-start(bf16[256,128]{1,0:T(8,128)(2,1)S(1)} %collective-permute-done.8.ahead_ref.refs_1_), channel_id=1, source_target_pairs={{0,1},{1,0},{2,3},{3,2},{4,5},{5,4},{6,7},{7,6},{8,9},{9,8},{10,11... | collective-permute-start | bytes 196616 | tf_op jit(solution)/shard_map/ppermute | solution.py:642
  37.2 0.0 collective-permute-done.10.refs_3_
  37.2 0.7 %collective-permute-start.13 = (bf16[256,128]{1,0:T(8,128)(2,1)S(1)}, bf16[256,128]{1,0:T(8,128)(2,1)S(1)}, u32[]{:S(2)}, u32[]{:S(2)}) collective-permute-start(bf16[256,128]{1,0:T(8,128)(2,1)S(1)} %collective-permute-done.9.refs_2_), channel_id=1, source_target_pairs={{0,1},{1,0},{2,3},{3,2},{4,5},{5,4},{6,7},{7,6},{8,9},{9,8},{10,11... | collective-permute-start | bytes 196616 | tf_op jit(solution)/shard_map/ppermute | solution.py:642
  38.0 0.0 collective-permute-done.4.other_residual_ref
  38.0 1.3 %collective-permute-start.14 = (bf16[256,128]{1,0:T(8,128)(2,1)S(1)}, bf16[256,128]{1,0:T(8,128)(2,1)S(1)}, u32[]{:S(2)}, u32[]{:S(2)}) collective-permute-start(bf16[256,128]{1,0:T(8,128)(2,1)S(1)} %collective-permute-done.10.refs_3_), channel_id=1, source_target_pairs={{0,1},{1,0},{2,3},{3,2},{4,5},{5,4},{6,7},{7,6},{8,9},{9,8},{10,11... | collective-permute-start | bytes 196616 | tf_op jit(solution)/shard_map/ppermute | solution.py:642
  39.3 1.1 %shard_map.106.own_ref = f32[256,1024]{1,0:T(8,128)S(1)} custom-call(s32[2]{0:T(128)S(1)} %pad_add_fusion.index_ref, bf16[256,512]{1,0:T(8,128)(2,1)S(1)} %copy-done.5, bf16[256,512]{1,0:T(8,128)(2,1)S(1)} %collective-permute-done.4.other_residual_ref, bf16[512,1024]{1,0:T(8,128)(2,1)S(1)} %copy-done.3, bf16[256,128]{1,0:T(8,128)(2,1)S(1)} %get-tuple-element.55.refs_0_, ...), custom_call_target="tpu_custom_call" | custom-call | flops 1384199936 | tf_op jit(solution)/shard_map/pallas_call | solution.py:517
  40.4 0.0 collective-permute-done.11.refs_0_
  40.4 0.1 collective-permute-done.12.refs_1_
  40.5 1.6 %collective-permute-done.13.refs_2_ = bf16[256,128]{1,0:T(8,128)(2,1)S(1)} collective-permute-done((bf16[256,128]{1,0:T(8,128)(2,1)S(1)}, bf16[256,128]{1,0:T(8,128)(2,1)S(1)}, u32[]{:S(2)}, u32[]{:S(2)}) %collective-permute-start.13) | collective-permute-done | bytes 65568 | tf_op jit(solution)/shard_map/ppermute | solution.py:642
  42.1 0.7 %collective-permute-done.14.refs_3_ = bf16[256,128]{1,0:T(8,128)(2,1)S(1)} collective-permute-done((bf16[256,128]{1,0:T(8,128)(2,1)S(1)}, bf16[256,128]{1,0:T(8,128)(2,1)S(1)}, u32[]{:S(2)}, u32[]{:S(2)}) %collective-permute-start.14) | collective-permute-done | bytes 65568 | tf_op jit(solution)/shard_map/ppermute | solution.py:642
  42.8 0.0 collective-permute-done.16.refs_5_
  42.8 0.0 copy-done.2
  42.8 0.0 copy-done
  42.9 0.0 copy-done.1
  42.9 0.0 copy-done.4
  42.9 2.0 %shard_map.108 = (bf16[128,512]{1,0:T(8,128)(2,1)S(1)}, f32[128,512]{1,0:T(8,128)S(1)}) custom-call(s32[2]{0:T(128)S(1)} %pad_add_fusion.index_ref, f32[256,1024]{1,0:T(8,128)S(1)} %shard_map.106.own_ref, bf16[256,128]{1,0:T(8,128)(2,1)S(1)} %collective-permute-done.11.refs_0_, bf16[256,128]{1,0:T(8,128)(2,1)S(1)} %collective-permute-done.12.refs_1_, ...), custom_call_target="tpu_custom_call" | custom-call | flops 2307000064 | tf_op jit(solution)/shard_map/pallas_call | solution.py:517
  44.9 1.5 %collective-permute-start.18 = (bf16[128,512]{1,0:T(8,128)(2,1)S(1)}, bf16[128,512]{1,0:T(8,128)(2,1)S(1)}, u32[]{:S(2)}, u32[]{:S(2)}) collective-permute-start(bf16[128,512]{1,0:T(8,128)(2,1)S(1)} %get-tuple-element.62), channel_id=1, source_target_pairs={{0,1},{1,0},{2,3},{3,2},{4,5},{5,4},{6,7},{7,6},{8,9},{9,8},{10,11... | collective-permute-start | bytes 393224 | tf_op jit(solution)/shard_map/ppermute | solution.py:680
  46.4 2.0 %shard_map.107 = (bf16[128,512]{1,0:T(8,128)(2,1)S(1)}, f32[128,512]{1,0:T(8,128)S(1)}) custom-call(s32[2]{0:T(128)S(1)} %pad_add_fusion.index_ref, f32[256,1024]{1,0:T(8,128)S(1)} %shard_map.106.own_ref, bf16[256,128]{1,0:T(8,128)(2,1)S(1)} %collective-permute-done.11.refs_0_, bf16[256,128]{1,0:T(8,128)(2,1)S(1)} %collective-permute-done.12.refs_1_, ...), custom_call_target="tpu_custom_call" | custom-call | flops 2307000064 | tf_op jit(solution)/shard_map/pallas_call | solution.py:517
  48.4 0.6 %collective-permute-start.17 = (bf16[128,512]{1,0:T(8,128)(2,1)S(1)}, bf16[128,512]{1,0:T(8,128)(2,1)S(1)}, u32[]{:S(2)}, u32[]{:S(2)}) collective-permute-start(bf16[128,512]{1,0:T(8,128)(2,1)S(1)} %get-tuple-element.61), channel_id=1, source_target_pairs={{0,1},{1,0},{2,3},{3,2},{4,5},{5,4},{6,7},{7,6},{8,9},{9,8},{10,11... | collective-permute-start | bytes 393224 | tf_op jit(solution)/shard_map/ppermute | solution.py:680
  49.0 0.9 %collective-permute-done.18.refs_3_ = bf16[128,512]{1,0:T(8,128)(2,1)S(1)} collective-permute-done((bf16[128,512]{1,0:T(8,128)(2,1)S(1)}, bf16[128,512]{1,0:T(8,128)(2,1)S(1)}, u32[]{:S(2)}, u32[]{:S(2)}) %collective-permute-start.18) | collective-permute-done | bytes 131104 | tf_op jit(solution)/shard_map/ppermute | solution.py:680
  49.9 3.5 %collective-permute-done.17.refs_2_ = bf16[128,512]{1,0:T(8,128)(2,1)S(1)} collective-permute-done((bf16[128,512]{1,0:T(8,128)(2,1)S(1)}, bf16[128,512]{1,0:T(8,128)(2,1)S(1)}, u32[]{:S(2)}, u32[]{:S(2)}) %collective-permute-start.17) | collective-permute-done | bytes 131104 | tf_op jit(solution)/shard_map/ppermute | solution.py:680
  53.4 0.8 %shard_map.109 = bf16[256,512]{1,0:T(8,128)(2,1)} custom-call(f32[128,512]{1,0:T(8,128)S(1)} %get-tuple-element.59.refs_0_, f32[128,512]{1,0:T(8,128)S(1)} %get-tuple-element.60.refs_1_, bf16[128,512]{1,0:T(8,128)(2,1)S(1)} %collective-permute-done.17.refs_2_, bf16[128,512]{1,0:T(8,128)(2,1)S(1)} %collective-permute-done.18.refs_3_), custom_call_target="tpu_custom_call" | custom-call | flops 922800000 | tf_op jit(solution)/shard_map/pallas_call | solution.py:517
  (2 shorter events, 0.0 us)
Async XLA Ops:
  0.0 1.2 %copy-start.6 = (s32[6,8]{1,0:T(8,128)S(1)}, s32[6,8]{1,0:T(8,128)}, u32[]{:S(2)}) copy-start(s32[6,8]{1,0:T(8,128)} %offset_ref.5) | copy-start | bytes 580
  1.2 4.2 %copy-start.3 = (bf16[512,1024]{1,0:T(8,128)(2,1)S(1)}, bf16[512,1024]{1,0:T(8,128)(2,1)}, u32[]{:S(2)}) copy-start(bf16[512,1024]{1,0:T(8,128)(2,1)} %weight_ref.1) | copy-start | bytes 3145732
  2.3 5.0 %collective-permute-start = (bf16[1536,128]{1,0:T(8,128)(2,1)S(1)}, bf16[1536,128]{1,0:T(8,128)(2,1)S(1)}, u32[]{:S(2)}, u32[]{:S(2)}) collective-permute-start(bf16[1536,128]{1,0:T(8,128)(2,1)S(1)} %get-tuple-element.35), channel_id=1, source_target_pairs={{0,2},{2,0},{4,6},{6,4},{8,10},{10,8},{12,14},{14,12},{16,18},{18,... | collective-permute-start | bytes 1179656 | tf_op jit(solution)/shard_map/ppermute | solution.py:559
  2.8 6.4 %collective-permute-start.1 = (bf16[240,128]{1,0:T(8,128)(2,1)S(1)}, bf16[240,128]{1,0:T(8,128)(2,1)S(1)}, u32[]{:S(2)}, u32[]{:S(2)}) collective-permute-start(bf16[240,128]{1,0:T(8,128)(2,1)S(1)} %get-tuple-element.39), channel_id=1, source_target_pairs={{0,4},{2,6},{4,0},{6,2},{8,12},{10,14},{12,8},{14,10},{16,20},{18,... | collective-permute-start | bytes 184328 | tf_op jit(solution)/shard_map/ppermute | solution.py:559
  5.4 4.0 %collective-permute-start.2 = (bf16[240,128]{1,0:T(8,128)(2,1)S(1)}, bf16[240,128]{1,0:T(8,128)(2,1)S(1)}, u32[]{:S(2)}, u32[]{:S(2)}) collective-permute-start(bf16[240,128]{1,0:T(8,128)(2,1)S(1)} %get-tuple-element.40), channel_id=1, source_target_pairs={{0,6},{2,4},{4,2},{6,0},{8,14},{10,12},{12,10},{14,8},{16,22},{18,... | collective-permute-start | bytes 184328 | tf_op jit(solution)/shard_map/ppermute | solution.py:559
  5.5 14.2 %collective-permute-start.15 = (bf16[256,1024]{1,0:T(8,128)(2,1)S(1)}, bf16[256,1024]{1,0:T(8,128)(2,1)S(1)}, u32[]{:S(2)}, u32[]{:S(2)}) collective-permute-start(bf16[256,1024]{1,0:T(8,128)(2,1)S(1)} %constant_dynamic-slice_fusion), channel_id=1, source_target_pairs={{0,1},{1,0},{2,3},{3,2},{4,5},{5,4},{6,7},{7,6},{8,9},{9,8},{10,11... | collective-permute-start | bytes 1572872 | tf_op jit(solution)/shard_map/ppermute | solution.py:564
  7.2 14.2 %copy-start.5 = (bf16[256,512]{1,0:T(8,128)(2,1)S(1)}, bf16[256,512]{1,0:T(8,128)(2,1)}, u32[]{:S(2)}) copy-start(bf16[256,512]{1,0:T(8,128)(2,1)} %residual_ref.1) | copy-start | bytes 786436
  9.9 11.5 %collective-permute-start.3 = (bf16[1536,128]{1,0:T(8,128)(2,1)S(1)}, bf16[1536,128]{1,0:T(8,128)(2,1)S(1)}, u32[]{:S(2)}, u32[]{:S(2)}) collective-permute-start(bf16[1536,128]{1,0:T(8,128)(2,1)S(1)} %get-tuple-element.42), channel_id=1, source_target_pairs={{0,4},{2,6},{4,0},{6,2},{8,12},{10,14},{12,8},{14,10},{16,20},{18,... | collective-permute-start | bytes 1179656 | tf_op jit(solution)/shard_map/ppermute | solution.py:559
  11.4 14.7 %collective-permute-start.6 = (bf16[4,112,128]{2,1,0:T(8,128)(2,1)S(1)}, bf16[4,112,128]{2,1,0:T(8,128)(2,1)S(1)}, u32[]{:S(2)}, u32[]{:S(2)}) collective-permute-start(bf16[4,112,128]{2,1,0:T(8,128)(2,1)S(1)} %get-tuple-element.49), channel_id=1, source_target_pairs={{0,16},{2,18},{4,20},{6,22},{8,24},{10,26},{12,28},{14,30},{16,0},... | collective-permute-start | bytes 344072 | tf_op jit(solution)/shard_map/ppermute | solution.py:559
  14.0 12.2 %collective-permute-start.7 = (bf16[4,112,128]{2,1,0:T(8,128)(2,1)S(1)}, bf16[4,112,128]{2,1,0:T(8,128)(2,1)S(1)}, u32[]{:S(2)}, u32[]{:S(2)}) collective-permute-start(bf16[4,112,128]{2,1,0:T(8,128)(2,1)S(1)} %get-tuple-element.49), channel_id=1, source_target_pairs={{0,24},{2,26},{4,28},{6,30},{8,16},{10,18},{12,20},{14,22},{16,8},... | collective-permute-start | bytes 344072 | tf_op jit(solution)/shard_map/ppermute | solution.py:559
  15.4 11.2 %collective-permute-start.5 = (bf16[4,240,128]{2,1,0:T(8,128)(2,1)S(1)}, bf16[4,240,128]{2,1,0:T(8,128)(2,1)S(1)}, u32[]{:S(2)}, u32[]{:S(2)}) collective-permute-start(bf16[4,240,128]{2,1,0:T(8,128)(2,1)S(1)} %get-tuple-element.48.refs_0_), channel_id=1, source_target_pairs={{0,8},{2,10},{4,12},{6,14},{8,0},{10,2},{12,4},{14,6},{16,24},{18,... | collective-permute-start | bytes 737288 | tf_op jit(solution)/shard_map/ppermute | solution.py:559
  19.7 23.2 %collective-permute-start.16 = (bf16[256,1024]{1,0:T(8,128)(2,1)S(1)}, bf16[256,1024]{1,0:T(8,128)(2,1)S(1)}, u32[]{:S(2)}, u32[]{:S(2)}) collective-permute-start(bf16[256,1024]{1,0:T(8,128)(2,1)S(1)} %collective-permute-done.15.refs_4_), channel_id=1, source_target_pairs={{0,2},{2,0},{4,6},{6,4},{8,10},{10,8},{12,14},{14,12},{16,18},{18,... | collective-permute-start | bytes 1572872 | tf_op jit(solution)/shard_map/ppermute | solution.py:559
  24.6 13.4 %collective-permute-start.4 = (bf16[256,512]{1,0:T(8,128)(2,1)S(1)}, bf16[256,512]{1,0:T(8,128)(2,1)S(1)}, u32[]{:S(2)}, u32[]{:S(2)}) collective-permute-start(bf16[256,512]{1,0:T(8,128)(2,1)S(1)} %get-tuple-element.47), channel_id=1, source_target_pairs={{0,1},{1,0},{2,3},{3,2},{4,5},{5,4},{6,7},{7,6},{8,9},{9,8},{10,11... | collective-permute-start | bytes 786440 | tf_op jit(solution)/shard_map/ppermute | solution.py:644
  26.6 16.2 %copy-start.2 = (bf16[1024,1024]{1,0:T(8,128)(2,1)S(1)}, bf16[1024,1024]{1,0:T(8,128)(2,1)}, u32[]{:S(2)}) copy-start(bf16[1024,1024]{1,0:T(8,128)(2,1)} %refs_9_.3) | copy-start | bytes 6291460
  30.8 1.3 %collective-permute-start.8 = (bf16[256,128]{1,0:T(8,128)(2,1)S(1)}, bf16[256,128]{1,0:T(8,128)(2,1)S(1)}, u32[]{:S(2)}, u32[]{:S(2)}) collective-permute-start(bf16[256,128]{1,0:T(8,128)(2,1)S(1)} %get-tuple-element.56), channel_id=1, source_target_pairs={{0,2},{2,0},{4,6},{6,4},{8,10},{10,8},{12,14},{14,12},{16,18},{18,... | collective-permute-start | bytes 196616 | tf_op jit(solution)/shard_map/ppermute | solution.py:559
  30.9 4.8 %collective-permute-start.9 = (bf16[256,128]{1,0:T(8,128)(2,1)S(1)}, bf16[256,128]{1,0:T(8,128)(2,1)S(1)}, u32[]{:S(2)}, u32[]{:S(2)}) collective-permute-start(bf16[256,128]{1,0:T(8,128)(2,1)S(1)} %get-tuple-element.57), channel_id=1, source_target_pairs={{0,4},{2,6},{4,0},{6,2},{8,12},{10,14},{12,8},{14,10},{16,20},{18,... | collective-permute-start | bytes 196616 | tf_op jit(solution)/shard_map/ppermute | solution.py:559
  32.2 5.1 %collective-permute-start.10 = (bf16[256,128]{1,0:T(8,128)(2,1)S(1)}, bf16[256,128]{1,0:T(8,128)(2,1)S(1)}, u32[]{:S(2)}, u32[]{:S(2)}) collective-permute-start(bf16[256,128]{1,0:T(8,128)(2,1)S(1)} %shard_map.105), channel_id=1, source_target_pairs={{0,6},{2,4},{4,2},{6,0},{8,14},{10,12},{12,10},{14,8},{16,22},{18,... | collective-permute-start | bytes 196616 | tf_op jit(solution)/shard_map/ppermute | solution.py:559
  32.9 10.0 %copy-start = (bf16[1024,1024]{1,0:T(8,128)(2,1)S(1)}, bf16[1024,1024]{1,0:T(8,128)(2,1)}, u32[]{:S(2)}) copy-start(bf16[1024,1024]{1,0:T(8,128)(2,1)} %refs_7_.3) | copy-start | bytes 6291460
  32.9 10.0 %copy-start.1 = (bf16[1024,1024]{1,0:T(8,128)(2,1)S(1)}, bf16[1024,1024]{1,0:T(8,128)(2,1)}, u32[]{:S(2)}) copy-start(bf16[1024,1024]{1,0:T(8,128)(2,1)} %refs_8_.3) | copy-start | bytes 6291460
  32.9 10.0 %copy-start.4 = (f32[1024]{0:T(1024)S(1)}, f32[1024]{0:T(1024)}, u32[]{:S(2)}) copy-start(f32[1024]{0:T(1024)} %param.16) | copy-start | bytes 12292
  32.9 7.5 %collective-permute-start.11 = (bf16[256,128]{1,0:T(8,128)(2,1)S(1)}, bf16[256,128]{1,0:T(8,128)(2,1)S(1)}, u32[]{:S(2)}, u32[]{:S(2)}) collective-permute-start(bf16[256,128]{1,0:T(8,128)(2,1)S(1)} %get-tuple-element.55.refs_0_), channel_id=1, source_target_pairs={{0,1},{1,0},{2,3},{3,2},{4,5},{5,4},{6,7},{7,6},{8,9},{9,8},{10,11... | collective-permute-start | bytes 196616 | tf_op jit(solution)/shard_map/ppermute | solution.py:642
  35.8 4.7 %collective-permute-start.12 = (bf16[256,128]{1,0:T(8,128)(2,1)S(1)}, bf16[256,128]{1,0:T(8,128)(2,1)S(1)}, u32[]{:S(2)}, u32[]{:S(2)}) collective-permute-start(bf16[256,128]{1,0:T(8,128)(2,1)S(1)} %collective-permute-done.8.ahead_ref.refs_1_), channel_id=1, source_target_pairs={{0,1},{1,0},{2,3},{3,2},{4,5},{5,4},{6,7},{7,6},{8,9},{9,8},{10,11... | collective-permute-start | bytes 196616 | tf_op jit(solution)/shard_map/ppermute | solution.py:642
  37.2 4.9 %collective-permute-start.13 = (bf16[256,128]{1,0:T(8,128)(2,1)S(1)}, bf16[256,128]{1,0:T(8,128)(2,1)S(1)}, u32[]{:S(2)}, u32[]{:S(2)}) collective-permute-start(bf16[256,128]{1,0:T(8,128)(2,1)S(1)} %collective-permute-done.9.refs_2_), channel_id=1, source_target_pairs={{0,1},{1,0},{2,3},{3,2},{4,5},{5,4},{6,7},{7,6},{8,9},{9,8},{10,11... | collective-permute-start | bytes 196616 | tf_op jit(solution)/shard_map/ppermute | solution.py:642
  38.0 4.9 %collective-permute-start.14 = (bf16[256,128]{1,0:T(8,128)(2,1)S(1)}, bf16[256,128]{1,0:T(8,128)(2,1)S(1)}, u32[]{:S(2)}, u32[]{:S(2)}) collective-permute-start(bf16[256,128]{1,0:T(8,128)(2,1)S(1)} %collective-permute-done.10.refs_3_), channel_id=1, source_target_pairs={{0,1},{1,0},{2,3},{3,2},{4,5},{5,4},{6,7},{7,6},{8,9},{9,8},{10,11... | collective-permute-start | bytes 196616 | tf_op jit(solution)/shard_map/ppermute | solution.py:642
  44.9 5.0 %collective-permute-start.18 = (bf16[128,512]{1,0:T(8,128)(2,1)S(1)}, bf16[128,512]{1,0:T(8,128)(2,1)S(1)}, u32[]{:S(2)}, u32[]{:S(2)}) collective-permute-start(bf16[128,512]{1,0:T(8,128)(2,1)S(1)} %get-tuple-element.62), channel_id=1, source_target_pairs={{0,1},{1,0},{2,3},{3,2},{4,5},{5,4},{6,7},{7,6},{8,9},{9,8},{10,11... | collective-permute-start | bytes 393224 | tf_op jit(solution)/shard_map/ppermute | solution.py:680
  48.4 5.0 %collective-permute-start.17 = (bf16[128,512]{1,0:T(8,128)(2,1)S(1)}, bf16[128,512]{1,0:T(8,128)(2,1)S(1)}, u32[]{:S(2)}, u32[]{:S(2)}) collective-permute-start(bf16[128,512]{1,0:T(8,128)(2,1)S(1)} %get-tuple-element.61), channel_id=1, source_target_pairs={{0,1},{1,0},{2,3},{3,2},{4,5},{5,4},{6,7},{7,6},{8,9},{9,8},{10,11... | collective-permute-start | bytes 393224 | tf_op jit(solution)/shard_map/ppermute | solution.py:680

commit v4 on v3

--- a/solution.py
+++ b/solution.py
@@ -338,8 +338,11 @@
         tops[head, into, :] = top_lanes(top, count, branch)
 
 
-def hold_kernel(block_ref, ahead_ref, out_ref):
+def hold_kernel(block_ref, own_ref, core_ref, out_ref, both_ref):
     out_ref[...] = block_ref[...]
+    rows = own_ref.shape[0]
+    both_ref[:rows] = own_ref[...]
+    both_ref[rows:] = core_ref[...]
 
 
 def finish_kernel(sets, rows, dim, offset_ref, index_ref, *refs):
@@ -451,6 +454,14 @@
         mix_ref[:, lanes] = ref[part, :]
 
 
+def halve_kernel(first_ref, second_ref, *out_refs):
+    step = out_refs[0].shape[0] // 2
+    for number, out_ref in enumerate(out_refs):
+        part = slice(number * step, (number + 1) * step)
+        out_ref[:step] = first_ref[part, :]
+        out_ref[step:] = second_ref[part, :]
+
+
 def own_kernel(index_ref, residual_ref, other_residual_ref, weight_ref, *refs):
     block_refs, out_ref, mix_ref = refs[:NEAR], refs[NEAR], refs[NEAR + 1]
     rows, half = residual_ref.shape
@@ -462,8 +473,8 @@
     out_ref[:, theirs] += other_residual_ref[...].astype(jnp.float32)
 
 
-def block_kernel(part, index_ref, own_ref, *refs):
-    block_refs, refs = refs[:NEAR], refs[NEAR:]
+def block_kernel(part, places, index_ref, own_ref, *refs):
+    block_refs, refs = refs[:2], refs[2:]
     first_weight_ref, second_weight_ref, gain_ref, gate_ref, up_ref, down_ref = refs[:6]
     theirs_ref, mine_ref, hidden_ref, act_ref, mix_ref = refs[6:]
     half = theirs_ref.shape[1]
@@ -471,7 +482,10 @@
     theirs = pl.ds(pl.multiple_of((1 - index_ref[1]) * half, LANES), half)
     count = first_weight_ref.shape[0]
     core = index_ref[0] % 2
-    lay_out(index_ref[0] % NEAR, block_refs, part, mix_ref)
+    rows = mix_ref.shape[0]
+    for side, (place, first) in enumerate(places):
+        lanes = pl.ds(pl.multiple_of((index_ref[0] % NEAR ^ side) * LANES, LANES), LANES)
+        mix_ref[:, lanes] = block_refs[place][first : first + rows, :]
     hidden = own_ref[part, :]
     for place, weight_ref in ((core, first_weight_ref), (1 - core, second_weight_ref)):
         lanes = pl.ds(pl.multiple_of(place * count, LANES), count)
@@ -637,10 +651,18 @@
         vmem=16,
     )
     mixes = [mixes[0], across(mixes[1], 1), across(mixes[2], 2), mixes[3]]
-    held = call(hold_kernel, shape(rows, LANES), 0, (mixes[3], mixes[1]), 0.2)
+    held, both = call(
+        hold_kernel,
+        [shape(rows, LANES), shape(2 * rows, LANES)],
+        0,
+        (mixes[3], mixes[0], mixes[1]),
+        0.2,
+    )
     mixes[3] = across(held, 3)
-    other_mixes = [lax.ppermute(block, "tp", swap) for block in mixes]
-
+    step = rows // CHUNKS
+    parts = call(halve_kernel, [shape(2 * step, LANES)] * CHUNKS, 0, mixes[2:], 0.2)
+    both = lax.ppermute(both, "tp", swap)
+    parts = [lax.ppermute(block, "tp", swap) for block in parts]
     other_residual = lax.ppermute(residual, "tp", swap)
     width = norm_gain.shape[0]
     mine, theirs = [], []
@@ -652,17 +674,18 @@
         1.2,
         [pltpu.VMEM((rows, cols), bf16)],
     )
-    step = rows // CHUNKS
     for number in range(CHUNKS):
         part = slice(number * step, (number + 1) * step)
+        places = [(0, part.start), (0, rows + part.start), (1, 0), (1, step)]
         send, keep = call(
-            functools.partial(block_kernel, part),
+            functools.partial(block_kernel, part, places),
             [shape(step, cols), shape(step, cols, dtype=jnp.float32)],
             1,
             (
                 index,
                 own,
-                *other_mixes,
+                both,
+                parts[number],
                 *other_weights,
                 norm_gain.reshape(1, width),
                 gate_weight,

time: 54.3 us -> 53.1 us (0.978)
  starting transfers between devices: 21 us -> 19.7 us
    ppermute x4 -> x3, starting transfers between devices: 4.94 us -> 3.51 us  [the longest x2 2.11 us: shards(): parts = [lax.ppermute(block, 'tp', swap) for block in parts]]
    ppermute x4 -> x3, waiting for transfers between devices: 2.46 us -> 1.46 us  [the longest x2 1.46 us: shards(): parts = [lax.ppermute(block, 'tp', swap) for block in parts]]
    ppermute x11, waiting for transfers between devices: 4 us -> 4.87 us  [across(): lax.ppermute(block, 'seq', [(i, i ^ distance) for i in range(seq_count)])]
    pallas_call x10 -> x11, Pallas kernels: 16.7 us -> 16.8 us  [call(): pl.pallas_call(kernel, out_shape=out_shape, in_specs=specs, out_specs=out...]
  transfers between devices with their start and end apart: 19 -> 18, of which waited for: 11 -> 10; matrix products, arithmetic and copies ran while one was open for 0% -> 0% of each run, Pallas kernels for 24% -> 28%
where the time goes in v4:
time: 53.1 us; the launch traced here: 53 us
  starting transfers between devices  19.7 us (37%)
  Pallas kernels  16.8 us (32%)
  waiting for transfers between devices  15.1 us (28%)
  other arithmetic  1.23 us (2%)
    pallas_call x11, Pallas kernels, call(): pl.pallas_call(kernel, out_shape=out_shape, in_specs=specs, out_specs=out...  16.8 us
    ppermute x11, starting transfers between devices, across(): lax.ppermute(block, 'seq', [(i, i ^ distance) for i in range(seq_count)])  10.7 us
    ppermute x11, waiting for transfers between devices, across(): lax.ppermute(block, 'seq', [(i, i ^ distance) for i in range(seq_count)])  4.87 us
    ppermute x2, waiting for transfers between devices, shards(): theirs.append(lax.ppermute(send, 'tp', swap))  4.69 us
    ppermute x1, waiting for transfers between devices, shards(): part = lax.ppermute(part, 'tp', swap)  4.05 us
    ppermute x2, starting transfers between devices, shards(): theirs.append(lax.ppermute(send, 'tp', swap))  2.16 us
    ppermute x2, starting transfers between devices, shards(): parts = [lax.ppermute(block, 'tp', swap) for block in parts]  2.11 us
    ppermute x1, starting transfers between devices, shards(): part = lax.ppermute(part, 'tp', swap)  1.76 us
  transfers between devices with their start and end apart: 18, of which 10 were waited for; matrix products, arithmetic and copies ran while one was open for 0% of the time, Pallas kernels for 28%

profile of v4, /device:TPU:0, one launch (start us, length us, event | category | flops | bytes accessed | tf_op | source)
XLA Modules:
  0.0 53.0 jit_solution(18250322946883370345)
XLA Ops:
  0.0 0.0 copy-start.6
  0.0 0.1 pad_add_fusion.index_ref
  0.1 1.2 %pad_maximum_fusion.source_ref = bf16[768,512]{1,0:T(8,128)(2,1)S(1)} fusion(bf16[256,512]{1,0:T(8,128)(2,1)} %param.13, bf16[256,512]{1,0:T(8,128)(2,1)} %param.12, bf16[256,512]{1,0:T(8,128)(2,1)} %param.11), kind=kLoop, calls=%fused_computation | loop fusion | flops 2359296 | bytes 1572864 | tf_op jit(solution)/shard_map/concatenate | solution.py:581
  1.2 0.0 copy-done.6
  1.2 0.0 copy-start.3
  1.3 1.0 %shard_map.100 = (bf16[240,128]{1,0:T(8,128)(2,1)S(1)}, bf16[240,128]{1,0:T(8,128)(2,1)S(1)}, bf16[768,128]{1,0:T(8,128)(2,1)S(1)}, bf16[1536,128]{1,0:T(8,128)(2,1)S(1)}, bf16[768,128]{1,0:T(8,128)(2,1)S(1)}) custom-call(s32[6,8]{1,0:T(8,128)S(1)} %copy-done.6, s32[2]{0:T(128)S(1)} %pad_add_fusion.index_ref, bf16[768,512]{1,0:T(8,128)(2,1)S(1)} %pad_maximum_fusion.source_ref), custom_call_target="tpu_custom_call" | custom-call | flops 1153500032 | tf_op jit(solution)/shard_map/pallas_call | solution.py:531
  2.3 0.5 collective-permute-start
  2.8 2.6 %collective-permute-start.1 = (bf16[240,128]{1,0:T(8,128)(2,1)S(1)}, bf16[240,128]{1,0:T(8,128)(2,1)S(1)}, u32[]{:S(2)}, u32[]{:S(2)}) collective-permute-start(bf16[240,128]{1,0:T(8,128)(2,1)S(1)} %get-tuple-element.43), channel_id=1, source_target_pairs={{0,4},{2,6},{4,0},{6,2},{8,12},{10,14},{12,8},{14,10},{16,20},{18,... | collective-permute-start | bytes 184328 | tf_op jit(solution)/shard_map/ppermute | solution.py:573
  5.4 0.1 collective-permute-start.2
  5.4 0.0 copy-done.3
  5.5 1.8 %collective-permute-start.13 = (bf16[256,1024]{1,0:T(8,128)(2,1)S(1)}, bf16[256,1024]{1,0:T(8,128)(2,1)S(1)}, u32[]{:S(2)}, u32[]{:S(2)}) collective-permute-start(bf16[256,1024]{1,0:T(8,128)(2,1)S(1)} %constant_dynamic-slice_fusion), channel_id=1, source_target_pairs={{0,1},{1,0},{2,3},{3,2},{4,5},{5,4},{6,7},{7,6},{8,9},{9,8},{10,11... | collective-permute-start | bytes 1572872 | tf_op jit(solution)/shard_map/ppermute | solution.py:578
  7.2 0.0 collective-permute-done.pair_ref
  7.2 0.0 copy-start.5
  7.3 2.0 %shard_map.101 = (f32[2,2,256,128]{3,2,1,0:T(8,128)S(1)}, bf16[240,128]{1,0:T(8,128)(2,1)S(1)}, bf16[240,128]{1,0:T(8,128)(2,1)S(1)}, bf16[1536,128]{1,0:T(8,128...) custom-call(s32[6,8]{1,0:T(8,128)S(1)} %copy-done.6, ...), custom_call_target="tpu_custom_call" | custom-call | flops 2768399872 | tf_op jit(solution)/shard_map/pallas_call | solution.py:531
  9.2 0.0 collective-permute-done.1.refs_2_
  9.2 0.1 collective-permute-done.2.refs_3_
  9.3 0.6 %shard_map.102 = (bf16[4,240,128]{2,1,0:T(8,128)(2,1)S(1)}, bf16[4,112,128]{2,1,0:T(8,128)(2,1)S(1)}, bf16[1536,128]{1,0:T(8,128)(2,1)S(1)}) custom-call(s32[2]{0:T(128)S(1)} %pad_add_fusion.index_ref, bf16[240,128]{1,0:T(8,128)(2,1)S(1)} %get-tuple-element.41.refs_0_, ...), custom_call_target="tpu_custom_call", output_to_operand_aliasing={{2}: (5, {})} | custom-call | flops 346049984 | tf_op jit(solution)/shard_map/pallas_call | solution.py:531
  9.9 1.5 %collective-permute-start.3 = (bf16[1536,128]{1,0:T(8,128)(2,1)S(1)}, bf16[1536,128]{1,0:T(8,128)(2,1)S(1)}, u32[]{:S(2)}, u32[]{:S(2)}) collective-permute-start(bf16[1536,128]{1,0:T(8,128)(2,1)S(1)} %get-tuple-element.46), channel_id=1, source_target_pairs={{0,4},{2,6},{4,0},{6,2},{8,12},{10,14},{12,8},{14,10},{16,20},{18,... | collective-permute-start | bytes 1179656 | tf_op jit(solution)/shard_map/ppermute | solution.py:573
  11.4 2.6 %collective-permute-start.6 = (bf16[4,112,128]{2,1,0:T(8,128)(2,1)S(1)}, bf16[4,112,128]{2,1,0:T(8,128)(2,1)S(1)}, u32[]{:S(2)}, u32[]{:S(2)}) collective-permute-start(bf16[4,112,128]{2,1,0:T(8,128)(2,1)S(1)} %get-tuple-element.53), channel_id=1, source_target_pairs={{0,16},{2,18},{4,20},{6,22},{8,24},{10,26},{12,28},{14,30},{16,0},... | collective-permute-start | bytes 344072 | tf_op jit(solution)/shard_map/ppermute | solution.py:573
  14.0 1.4 %collective-permute-start.7 = (bf16[4,112,128]{2,1,0:T(8,128)(2,1)S(1)}, bf16[4,112,128]{2,1,0:T(8,128)(2,1)S(1)}, u32[]{:S(2)}, u32[]{:S(2)}) collective-permute-start(bf16[4,112,128]{2,1,0:T(8,128)(2,1)S(1)} %get-tuple-element.53), channel_id=1, source_target_pairs={{0,24},{2,26},{4,28},{6,30},{8,16},{10,18},{12,20},{14,22},{16,8},... | collective-permute-start | bytes 344072 | tf_op jit(solution)/shard_map/ppermute | solution.py:573
  15.4 0.2 collective-permute-start.5
  15.6 4.1 %collective-permute-done.13.refs_2_ = bf16[256,1024]{1,0:T(8,128)(2,1)S(1)} collective-permute-done((bf16[256,1024]{1,0:T(8,128)(2,1)S(1)}, bf16[256,1024]{1,0:T(8,128)(2,1)S(1)}, u32[]{:S(2)}, u32[]{:S(2)}) %collective-permute-start.13) | collective-permute-done | bytes 524320 | tf_op jit(solution)/shard_map/ppermute | solution.py:578
  19.7 0.0 collective-permute-start.14
  19.7 1.8 %collective-permute-done.3.refs_0_ = bf16[1536,128]{1,0:T(8,128)(2,1)S(1)} collective-permute-done((bf16[1536,128]{1,0:T(8,128)(2,1)S(1)}, bf16[1536,128]{1,0:T(8,128)(2,1)S(1)}, u32[]{:S(2)}, u32[]{:S(2)}) %collective-permute-start.3) | collective-permute-done | bytes 393248 | tf_op jit(solution)/shard_map/ppermute | solution.py:573
  21.5 0.0 copy-done.5
  21.5 3.1 %shard_map.103 = (f32[2,4,256,128]{3,2,1,0:T(8,128)S(1)}, f32[2,4,128,128]{3,2,1,0:T(8,128)S(1)}, f32[2,128,128]{2,1,0:T(8,128)S(1)}, bf16[4,128,128]{2,1,0:T(8,128)(2,1)S(1)}, bf16[256,512]{1,0:T(8,128)(2,1)S(1)}) custom-call(s32[2]{0:T(128)S(1)} %pad_add_fusion.index_ref, bf16[1536,128]{1,0:T(8,128)(2,1)S(1)} %collective-permute-done.3.refs_0_, ...), custom_call_target="tpu_custom_call" | custom-call | flops 3921900032 | tf_op jit(solution)/shard_map/pallas_call | solution.py:531
  24.6 1.5 %collective-permute-start.4 = (bf16[256,512]{1,0:T(8,128)(2,1)S(1)}, bf16[256,512]{1,0:T(8,128)(2,1)S(1)}, u32[]{:S(2)}, u32[]{:S(2)}) collective-permute-start(bf16[256,512]{1,0:T(8,128)(2,1)S(1)} %get-tuple-element.51), channel_id=1, source_target_pairs={{0,1},{1,0},{2,3},{3,2},{4,5},{5,4},{6,7},{7,6},{8,9},{9,8},{10,11... | collective-permute-start | bytes 786440 | tf_op jit(solution)/shard_map/ppermute | solution.py:666
  26.2 0.0 collective-permute-done.6.refs_2_
  26.2 0.0 collective-permute-done.7.refs_3_
  26.2 0.5 collective-permute-done.5.refs_1_
  26.6 4.2 %shard_map.104 = (bf16[256,128]{1,0:T(8,128)(2,1)S(1)}, bf16[256,128]{1,0:T(8,128)(2,1)S(1)}, bf16[256,128]{1,0:T(8,128)(2,1)S(1)}, bf16[256,128]{1,0:T(8,128)(2,1)S(1)}) custom-call(s32[6,8]{1,0:T(8,128)S(1)} %copy-done.6, s32[2]{0:T(128)S(1)} %pad_add_fusion.index_ref, bf16[4,240,128]{2,1,0:T(8,128)(2,1)S(1)} %get-tuple-element.52.refs_0_, ...), custom_call_target="tpu_custom_call" | custom-call | flops 6920999936 | tf_op jit(solution)/shard_map/pallas_call | solution.py:531
  30.8 0.1 collective-permute-start.8
  30.9 1.0 %collective-permute-start.9 = (bf16[256,128]{1,0:T(8,128)(2,1)S(1)}, bf16[256,128]{1,0:T(8,128)(2,1)S(1)}, u32[]{:S(2)}, u32[]{:S(2)}) collective-permute-start(bf16[256,128]{1,0:T(8,128)(2,1)S(1)} %get-tuple-element.61), channel_id=1, source_target_pairs={{0,4},{2,6},{4,0},{6,2},{8,12},{10,14},{12,8},{14,10},{16,20},{18,... | collective-permute-start | bytes 196616 | tf_op jit(solution)/shard_map/ppermute | solution.py:573
  31.9 0.3 collective-permute-done.8.core_ref.refs_1_
  32.2 0.0 copy-start.2
  32.2 0.7 %collective-permute-start.10 = (bf16[256,128]{1,0:T(8,128)(2,1)S(1)}, bf16[256,128]{1,0:T(8,128)(2,1)S(1)}, u32[]{:S(2)}, u32[]{:S(2)}) collective-permute-start(bf16[256,128]{1,0:T(8,128)(2,1)S(1)} %get-tuple-element.63), channel_id=1, source_target_pairs={{0,6},{2,4},{4,2},{6,0},{8,14},{10,12},{12,10},{14,8},{16,22},{18,... | collective-permute-start | bytes 196616 | tf_op jit(solution)/shard_map/ppermute | solution.py:573
  32.9 1.4 %collective-permute-start.11 = (bf16[512,128]{1,0:T(8,128)(2,1)S(1)}, bf16[512,128]{1,0:T(8,128)(2,1)S(1)}, u32[]{:S(2)}, u32[]{:S(2)}) collective-permute-start(bf16[512,128]{1,0:T(8,128)(2,1)S(1)} %get-tuple-element.64), channel_id=1, source_target_pairs={{0,1},{1,0},{2,3},{3,2},{4,5},{5,4},{6,7},{7,6},{8,9},{9,8},{10,11... | collective-permute-start | bytes 393224 | tf_op jit(solution)/shard_map/ppermute | solution.py:664
  34.3 1.3 %collective-permute-done.9.refs_2_.first_ref = bf16[256,128]{1,0:T(8,128)(2,1)S(1)} collective-permute-done((bf16[256,128]{1,0:T(8,128)(2,1)S(1)}, bf16[256,128]{1,0:T(8,128)(2,1)S(1)}, u32[]{:S(2)}, u32[]{:S(2)}) %collective-permute-start.9) | collective-permute-done | bytes 65568 | tf_op jit(solution)/shard_map/ppermute | solution.py:573
  35.7 0.9 %collective-permute-done.10.refs_3_.second_ref = bf16[256,128]{1,0:T(8,128)(2,1)S(1)} collective-permute-done((bf16[256,128]{1,0:T(8,128)(2,1)S(1)}, bf16[256,128]{1,0:T(8,128)(2,1)S(1)}, u32[]{:S(2)}, u32[]{:S(2)}) %collective-permute-start.10) | collective-permute-done | bytes 65568 | tf_op jit(solution)/shard_map/ppermute | solution.py:573
  36.6 1.5 %collective-permute-start.15 = (bf16[256,128]{1,0:T(8,128)(2,1)S(1)}, bf16[256,128]{1,0:T(8,128)(2,1)S(1)}, u32[]{:S(2)}, u32[]{:S(2)}) collective-permute-start(bf16[256,128]{1,0:T(8,128)(2,1)S(1)} %get-tuple-element.67), channel_id=1, source_target_pairs={{0,1},{1,0},{2,3},{3,2},{4,5},{5,4},{6,7},{7,6},{8,9},{9,8},{10,11... | collective-permute-start | bytes 196616 | tf_op jit(solution)/shard_map/ppermute | solution.py:665
  38.1 0.0 copy-start
  38.1 0.0 copy-start.1
  38.1 0.0 copy-start.4
  38.1 0.6 %collective-permute-start.12 = (bf16[256,128]{1,0:T(8,128)(2,1)S(1)}, bf16[256,128]{1,0:T(8,128)(2,1)S(1)}, u32[]{:S(2)}, u32[]{:S(2)}) collective-permute-start(bf16[256,128]{1,0:T(8,128)(2,1)S(1)} %get-tuple-element.65), channel_id=1, source_target_pairs={{0,1},{1,0},{2,3},{3,2},{4,5},{5,4},{6,7},{7,6},{8,9},{9,8},{10,11... | collective-permute-start | bytes 196616 | tf_op jit(solution)/shard_map/ppermute | solution.py:665
  38.7 0.0 collective-permute-done.4.other_residual_ref
  38.7 1.1 %shard_map.106.own_ref = f32[256,1024]{1,0:T(8,128)S(1)} custom-call(s32[2]{0:T(128)S(1)} %pad_add_fusion.index_ref, bf16[256,512]{1,0:T(8,128)(2,1)S(1)} %copy-done.5, bf16[256,512]{1,0:T(8,128)(2,1)S(1)} %collective-permute-done.4.other_residual_ref, bf16[512,1024]{1,0:T(8,128)(2,1)S(1)} %copy-done.3, ...), custom_call_target="tpu_custom_call" | custom-call | flops 1384199936 | tf_op jit(solution)/shard_map/pallas_call | solution.py:531
  39.8 0.0 collective-permute-done.11.refs_0_
  39.8 1.5 %collective-permute-done.15.refs_1_ = bf16[256,128]{1,0:T(8,128)(2,1)S(1)} collective-permute-done((bf16[256,128]{1,0:T(8,128)(2,1)S(1)}, bf16[256,128]{1,0:T(8,128)(2,1)S(1)}, u32[]{:S(2)}, u32[]{:S(2)}) %collective-permute-start.15) | collective-permute-done | bytes 65568 | tf_op jit(solution)/shard_map/ppermute | solution.py:665
  41.3 0.0 collective-permute-done.14.refs_3_
  41.3 0.0 copy-done.2
  41.3 0.0 copy-done
  41.3 0.0 copy-done.1
  41.3 0.0 copy-done.4
  41.3 2.0 %shard_map.109 = (bf16[128,512]{1,0:T(8,128)(2,1)S(1)}, f32[128,512]{1,0:T(8,128)S(1)}) custom-call(s32[2]{0:T(128)S(1)} %pad_add_fusion.index_ref, f32[256,1024]{1,0:T(8,128)S(1)} %shard_map.106.own_ref, bf16[512,128]{1,0:T(8,128)(2,1)S(1)} %collective-permute-done.11.refs_0_, bf16[256,128]{1,0:T(8,128)(2,1)S(1)} %collective-permute-done.15.refs_1_, ...), custom_call_target="tpu_custom_call" | custom-call | flops 2307000064 | tf_op jit(solution)/shard_map/pallas_call | solution.py:531
  43.3 1.8 %collective-permute-start.17 = (bf16[128,512]{1,0:T(8,128)(2,1)S(1)}, bf16[128,512]{1,0:T(8,128)(2,1)S(1)}, u32[]{:S(2)}, u32[]{:S(2)}) collective-permute-start(bf16[128,512]{1,0:T(8,128)(2,1)S(1)} %get-tuple-element.70), channel_id=1, source_target_pairs={{0,1},{1,0},{2,3},{3,2},{4,5},{5,4},{6,7},{7,6},{8,9},{9,8},{10,11... | collective-permute-start | bytes 393224 | tf_op jit(solution)/shard_map/ppermute | solution.py:703
  45.2 0.0 collective-permute-done.12.refs_1_
  45.2 2.0 %shard_map.108 = (bf16[128,512]{1,0:T(8,128)(2,1)S(1)}, f32[128,512]{1,0:T(8,128)S(1)}) custom-call(s32[2]{0:T(128)S(1)} %pad_add_fusion.index_ref, f32[256,1024]{1,0:T(8,128)S(1)} %shard_map.106.own_ref, bf16[512,128]{1,0:T(8,128)(2,1)S(1)} %collective-permute-done.11.refs_0_, bf16[256,128]{1,0:T(8,128)(2,1)S(1)} %collective-permute-done.12.refs_1_, ...), custom_call_target="tpu_custom_call" | custom-call | flops 2307000064 | tf_op jit(solution)/shard_map/pallas_call | solution.py:531
  47.2 0.3 collective-permute-start.16
  47.5 1.3 %collective-permute-done.17.refs_3_ = bf16[128,512]{1,0:T(8,128)(2,1)S(1)} collective-permute-done((bf16[128,512]{1,0:T(8,128)(2,1)S(1)}, bf16[128,512]{1,0:T(8,128)(2,1)S(1)}, u32[]{:S(2)}, u32[]{:S(2)}) %collective-permute-start.17) | collective-permute-done | bytes 131104 | tf_op jit(solution)/shard_map/ppermute | solution.py:703
  48.8 3.4 %collective-permute-done.16.refs_2_ = bf16[128,512]{1,0:T(8,128)(2,1)S(1)} collective-permute-done((bf16[128,512]{1,0:T(8,128)(2,1)S(1)}, bf16[128,512]{1,0:T(8,128)(2,1)S(1)}, u32[]{:S(2)}, u32[]{:S(2)}) %collective-permute-start.16) | collective-permute-done | bytes 131104 | tf_op jit(solution)/shard_map/ppermute | solution.py:703
  52.2 0.8 %shard_map.110 = bf16[256,512]{1,0:T(8,128)(2,1)} custom-call(f32[128,512]{1,0:T(8,128)S(1)} %get-tuple-element.66.refs_0_, f32[128,512]{1,0:T(8,128)S(1)} %get-tuple-element.68.refs_1_, bf16[128,512]{1,0:T(8,128)(2,1)S(1)} %collective-permute-done.16.refs_2_, bf16[128,512]{1,0:T(8,128)(2,1)S(1)} %collective-permute-done.17.refs_3_), custom_call_target="tpu_custom_call" | custom-call | flops 922800000 | tf_op jit(solution)/shard_map/pallas_call | solution.py:531
  (3 shorter events, 0.1 us)
Async XLA Ops:
  0.0 1.2 %copy-start.6 = (s32[6,8]{1,0:T(8,128)S(1)}, s32[6,8]{1,0:T(8,128)}, u32[]{:S(2)}) copy-start(s32[6,8]{1,0:T(8,128)} %offset_ref.5) | copy-start | bytes 580
  1.2 4.2 %copy-start.3 = (bf16[512,1024]{1,0:T(8,128)(2,1)S(1)}, bf16[512,1024]{1,0:T(8,128)(2,1)}, u32[]{:S(2)}) copy-start(bf16[512,1024]{1,0:T(8,128)(2,1)} %weight_ref.1) | copy-start | bytes 3145732
  2.3 5.0 %collective-permute-start = (bf16[1536,128]{1,0:T(8,128)(2,1)S(1)}, bf16[1536,128]{1,0:T(8,128)(2,1)S(1)}, u32[]{:S(2)}, u32[]{:S(2)}) collective-permute-start(bf16[1536,128]{1,0:T(8,128)(2,1)S(1)} %get-tuple-element.39), channel_id=1, source_target_pairs={{0,2},{2,0},{4,6},{6,4},{8,10},{10,8},{12,14},{14,12},{16,18},{18,... | collective-permute-start | bytes 1179656 | tf_op jit(solution)/shard_map/ppermute | solution.py:573
  2.8 6.4 %collective-permute-start.1 = (bf16[240,128]{1,0:T(8,128)(2,1)S(1)}, bf16[240,128]{1,0:T(8,128)(2,1)S(1)}, u32[]{:S(2)}, u32[]{:S(2)}) collective-permute-start(bf16[240,128]{1,0:T(8,128)(2,1)S(1)} %get-tuple-element.43), channel_id=1, source_target_pairs={{0,4},{2,6},{4,0},{6,2},{8,12},{10,14},{12,8},{14,10},{16,20},{18,... | collective-permute-start | bytes 184328 | tf_op jit(solution)/shard_map/ppermute | solution.py:573
  5.4 4.0 %collective-permute-start.2 = (bf16[240,128]{1,0:T(8,128)(2,1)S(1)}, bf16[240,128]{1,0:T(8,128)(2,1)S(1)}, u32[]{:S(2)}, u32[]{:S(2)}) collective-permute-start(bf16[240,128]{1,0:T(8,128)(2,1)S(1)} %get-tuple-element.44), channel_id=1, source_target_pairs={{0,6},{2,4},{4,2},{6,0},{8,14},{10,12},{12,10},{14,8},{16,22},{18,... | collective-permute-start | bytes 184328 | tf_op jit(solution)/shard_map/ppermute | solution.py:573
  5.5 14.2 %collective-permute-start.13 = (bf16[256,1024]{1,0:T(8,128)(2,1)S(1)}, bf16[256,1024]{1,0:T(8,128)(2,1)S(1)}, u32[]{:S(2)}, u32[]{:S(2)}) collective-permute-start(bf16[256,1024]{1,0:T(8,128)(2,1)S(1)} %constant_dynamic-slice_fusion), channel_id=1, source_target_pairs={{0,1},{1,0},{2,3},{3,2},{4,5},{5,4},{6,7},{7,6},{8,9},{9,8},{10,11... | collective-permute-start | bytes 1572872 | tf_op jit(solution)/shard_map/ppermute | solution.py:578
  7.2 14.2 %copy-start.5 = (bf16[256,512]{1,0:T(8,128)(2,1)S(1)}, bf16[256,512]{1,0:T(8,128)(2,1)}, u32[]{:S(2)}) copy-start(bf16[256,512]{1,0:T(8,128)(2,1)} %residual_ref.1) | copy-start | bytes 786436
  9.9 11.5 %collective-permute-start.3 = (bf16[1536,128]{1,0:T(8,128)(2,1)S(1)}, bf16[1536,128]{1,0:T(8,128)(2,1)S(1)}, u32[]{:S(2)}, u32[]{:S(2)}) collective-permute-start(bf16[1536,128]{1,0:T(8,128)(2,1)S(1)} %get-tuple-element.46), channel_id=1, source_target_pairs={{0,4},{2,6},{4,0},{6,2},{8,12},{10,14},{12,8},{14,10},{16,20},{18,... | collective-permute-start | bytes 1179656 | tf_op jit(solution)/shard_map/ppermute | solution.py:573
  11.4 14.7 %collective-permute-start.6 = (bf16[4,112,128]{2,1,0:T(8,128)(2,1)S(1)}, bf16[4,112,128]{2,1,0:T(8,128)(2,1)S(1)}, u32[]{:S(2)}, u32[]{:S(2)}) collective-permute-start(bf16[4,112,128]{2,1,0:T(8,128)(2,1)S(1)} %get-tuple-element.53), channel_id=1, source_target_pairs={{0,16},{2,18},{4,20},{6,22},{8,24},{10,26},{12,28},{14,30},{16,0},... | collective-permute-start | bytes 344072 | tf_op jit(solution)/shard_map/ppermute | solution.py:573
  14.0 12.1 %collective-permute-start.7 = (bf16[4,112,128]{2,1,0:T(8,128)(2,1)S(1)}, bf16[4,112,128]{2,1,0:T(8,128)(2,1)S(1)}, u32[]{:S(2)}, u32[]{:S(2)}) collective-permute-start(bf16[4,112,128]{2,1,0:T(8,128)(2,1)S(1)} %get-tuple-element.53), channel_id=1, source_target_pairs={{0,24},{2,26},{4,28},{6,30},{8,16},{10,18},{12,20},{14,22},{16,8},... | collective-permute-start | bytes 344072 | tf_op jit(solution)/shard_map/ppermute | solution.py:573
  15.4 11.2 %collective-permute-start.5 = (bf16[4,240,128]{2,1,0:T(8,128)(2,1)S(1)}, bf16[4,240,128]{2,1,0:T(8,128)(2,1)S(1)}, u32[]{:S(2)}, u32[]{:S(2)}) collective-permute-start(bf16[4,240,128]{2,1,0:T(8,128)(2,1)S(1)} %get-tuple-element.52.refs_0_), channel_id=1, source_target_pairs={{0,8},{2,10},{4,12},{6,14},{8,0},{10,2},{12,4},{14,6},{16,24},{18,... | collective-permute-start | bytes 737288 | tf_op jit(solution)/shard_map/ppermute | solution.py:573
  19.7 21.6 %collective-permute-start.14 = (bf16[256,1024]{1,0:T(8,128)(2,1)S(1)}, bf16[256,1024]{1,0:T(8,128)(2,1)S(1)}, u32[]{:S(2)}, u32[]{:S(2)}) collective-permute-start(bf16[256,1024]{1,0:T(8,128)(2,1)S(1)} %collective-permute-done.13.refs_2_), channel_id=1, source_target_pairs={{0,2},{2,0},{4,6},{6,4},{8,10},{10,8},{12,14},{14,12},{16,18},{18,... | collective-permute-start | bytes 1572872 | tf_op jit(solution)/shard_map/ppermute | solution.py:573
  24.6 14.1 %collective-permute-start.4 = (bf16[256,512]{1,0:T(8,128)(2,1)S(1)}, bf16[256,512]{1,0:T(8,128)(2,1)S(1)}, u32[]{:S(2)}, u32[]{:S(2)}) collective-permute-start(bf16[256,512]{1,0:T(8,128)(2,1)S(1)} %get-tuple-element.51), channel_id=1, source_target_pairs={{0,1},{1,0},{2,3},{3,2},{4,5},{5,4},{6,7},{7,6},{8,9},{9,8},{10,11... | collective-permute-start | bytes 786440 | tf_op jit(solution)/shard_map/ppermute | solution.py:666
  30.8 1.3 %collective-permute-start.8 = (bf16[256,128]{1,0:T(8,128)(2,1)S(1)}, bf16[256,128]{1,0:T(8,128)(2,1)S(1)}, u32[]{:S(2)}, u32[]{:S(2)}) collective-permute-start(bf16[256,128]{1,0:T(8,128)(2,1)S(1)} %get-tuple-element.60), channel_id=1, source_target_pairs={{0,2},{2,0},{4,6},{6,4},{8,10},{10,8},{12,14},{14,12},{16,18},{18,... | collective-permute-start | bytes 196616 | tf_op jit(solution)/shard_map/ppermute | solution.py:573
  30.9 4.7 %collective-permute-start.9 = (bf16[256,128]{1,0:T(8,128)(2,1)S(1)}, bf16[256,128]{1,0:T(8,128)(2,1)S(1)}, u32[]{:S(2)}, u32[]{:S(2)}) collective-permute-start(bf16[256,128]{1,0:T(8,128)(2,1)S(1)} %get-tuple-element.61), channel_id=1, source_target_pairs={{0,4},{2,6},{4,0},{6,2},{8,12},{10,14},{12,8},{14,10},{16,20},{18,... | collective-permute-start | bytes 196616 | tf_op jit(solution)/shard_map/ppermute | solution.py:573
  32.2 9.1 %copy-start.2 = (bf16[1024,1024]{1,0:T(8,128)(2,1)S(1)}, bf16[1024,1024]{1,0:T(8,128)(2,1)}, u32[]{:S(2)}) copy-start(bf16[1024,1024]{1,0:T(8,128)(2,1)} %refs_7_.3) | copy-start | bytes 6291460
  32.2 4.4 %collective-permute-start.10 = (bf16[256,128]{1,0:T(8,128)(2,1)S(1)}, bf16[256,128]{1,0:T(8,128)(2,1)S(1)}, u32[]{:S(2)}, u32[]{:S(2)}) collective-permute-start(bf16[256,128]{1,0:T(8,128)(2,1)S(1)} %get-tuple-element.63), channel_id=1, source_target_pairs={{0,6},{2,4},{4,2},{6,0},{8,14},{10,12},{12,10},{14,8},{16,22},{18,... | collective-permute-start | bytes 196616 | tf_op jit(solution)/shard_map/ppermute | solution.py:573
  32.9 6.9 %collective-permute-start.11 = (bf16[512,128]{1,0:T(8,128)(2,1)S(1)}, bf16[512,128]{1,0:T(8,128)(2,1)S(1)}, u32[]{:S(2)}, u32[]{:S(2)}) collective-permute-start(bf16[512,128]{1,0:T(8,128)(2,1)S(1)} %get-tuple-element.64), channel_id=1, source_target_pairs={{0,1},{1,0},{2,3},{3,2},{4,5},{5,4},{6,7},{7,6},{8,9},{9,8},{10,11... | collective-permute-start | bytes 393224 | tf_op jit(solution)/shard_map/ppermute | solution.py:664
  36.6 4.7 %collective-permute-start.15 = (bf16[256,128]{1,0:T(8,128)(2,1)S(1)}, bf16[256,128]{1,0:T(8,128)(2,1)S(1)}, u32[]{:S(2)}, u32[]{:S(2)}) collective-permute-start(bf16[256,128]{1,0:T(8,128)(2,1)S(1)} %get-tuple-element.67), channel_id=1, source_target_pairs={{0,1},{1,0},{2,3},{3,2},{4,5},{5,4},{6,7},{7,6},{8,9},{9,8},{10,11... | collective-permute-start | bytes 196616 | tf_op jit(solution)/shard_map/ppermute | solution.py:665
  38.1 3.2 %copy-start = (bf16[1024,1024]{1,0:T(8,128)(2,1)S(1)}, bf16[1024,1024]{1,0:T(8,128)(2,1)}, u32[]{:S(2)}) copy-start(bf16[1024,1024]{1,0:T(8,128)(2,1)} %refs_5_.5) | copy-start | bytes 6291460
  38.1 3.2 %copy-start.1 = (bf16[1024,1024]{1,0:T(8,128)(2,1)S(1)}, bf16[1024,1024]{1,0:T(8,128)(2,1)}, u32[]{:S(2)}) copy-start(bf16[1024,1024]{1,0:T(8,128)(2,1)} %refs_6_.3) | copy-start | bytes 6291460
  38.1 3.2 %copy-start.4 = (f32[1024]{0:T(1024)S(1)}, f32[1024]{0:T(1024)}, u32[]{:S(2)}) copy-start(f32[1024]{0:T(1024)} %param.16) | copy-start | bytes 12292
  38.1 7.0 %collective-permute-start.12 = (bf16[256,128]{1,0:T(8,128)(2,1)S(1)}, bf16[256,128]{1,0:T(8,128)(2,1)S(1)}, u32[]{:S(2)}, u32[]{:S(2)}) collective-permute-start(bf16[256,128]{1,0:T(8,128)(2,1)S(1)} %get-tuple-element.65), channel_id=1, source_target_pairs={{0,1},{1,0},{2,3},{3,2},{4,5},{5,4},{6,7},{7,6},{8,9},{9,8},{10,11... | collective-permute-start | bytes 196616 | tf_op jit(solution)/shard_map/ppermute | solution.py:665
  43.3 5.4 %collective-permute-start.17 = (bf16[128,512]{1,0:T(8,128)(2,1)S(1)}, bf16[128,512]{1,0:T(8,128)(2,1)S(1)}, u32[]{:S(2)}, u32[]{:S(2)}) collective-permute-start(bf16[128,512]{1,0:T(8,128)(2,1)S(1)} %get-tuple-element.70), channel_id=1, source_target_pairs={{0,1},{1,0},{2,3},{3,2},{4,5},{5,4},{6,7},{7,6},{8,9},{9,8},{10,11... | collective-permute-start | bytes 393224 | tf_op jit(solution)/shard_map/ppermute | solution.py:703
  47.2 5.0 %collective-permute-start.16 = (bf16[128,512]{1,0:T(8,128)(2,1)S(1)}, bf16[128,512]{1,0:T(8,128)(2,1)S(1)}, u32[]{:S(2)}, u32[]{:S(2)}) collective-permute-start(bf16[128,512]{1,0:T(8,128)(2,1)S(1)} %get-tuple-element.69), channel_id=1, source_target_pairs={{0,1},{1,0},{2,3},{3,2},{4,5},{5,4},{6,7},{7,6},{8,9},{9,8},{10,11... | collective-permute-start | bytes 393224 | tf_op jit(solution)/shard_map/ppermute | solution.py:703

commit v5 on v4

--- a/solution.py
+++ b/solution.py
@@ -15,6 +15,7 @@
 PEAK_FLOPS = 1153.5e12
 MIB = 1024 * 1024
 CHUNKS = 2
+BLOCK = 256
 
 masked_score = -1e30
 
@@ -124,7 +125,7 @@
     values = [jnp.where(lane < dim, jnp.ones_like(pairs), pairs) for _, pairs, _, _ in jobs]
     pieces = []
     for number, (query, _, _, _) in enumerate(jobs):
-        block = min(128, query.shape[0])
+        block = min(BLOCK, query.shape[0])
         pieces += [(start, number, block) for start in range(0, query.shape[0], block)]
     pieces.sort(key=lambda piece: piece[0])
     done = {}
@@ -145,7 +146,7 @@
         for (start, number, block), score in zip(now, scores):
             _, _, before, columns = jobs[number]
             end = before + start + block
-            if before == 0 and block == 128:
+            if before == 0 and block % LANES == 0:
                 row = lax.broadcasted_iota(jnp.int32, (block, block), 0)
                 col = lax.broadcasted_iota(jnp.int32, (block, block), 1)
                 last = jnp.where(col <= row, score[:, start:], masked_score)

time: 53.1 us -> 53.3 us (level)
  no operation moved by 1% of the time
where the time goes in v5:
time: 53.3 us; the launch traced here: 53.2 us
  starting transfers between devices  19.5 us (37%)
  Pallas kernels  16.8 us (32%)
  waiting for transfers between devices  15.4 us (29%)
  other arithmetic  1.23 us (2%)
    pallas_call x11, Pallas kernels, call(): pl.pallas_call(kernel, out_shape=out_shape, in_specs=specs, out_specs=out...  16.8 us
    ppermute x11, starting transfers between devices, across(): lax.ppermute(block, 'seq', [(i, i ^ distance) for i in range(seq_count)])  10.5 us
    ppermute x11, waiting for transfers between devices, across(): lax.ppermute(block, 'seq', [(i, i ^ distance) for i in range(seq_count)])  4.98 us
    ppermute x2, waiting for transfers between devices, shards(): theirs.append(lax.ppermute(send, 'tp', swap))  4.75 us
    ppermute x1, waiting for transfers between devices, shards(): part = lax.ppermute(part, 'tp', swap)  4.25 us
    ppermute x2, starting transfers between devices, shards(): theirs.append(lax.ppermute(send, 'tp', swap))  2.16 us
    ppermute x2, starting transfers between devices, shards(): parts = [lax.ppermute(block, 'tp', swap) for block in parts]  2.11 us
    ppermute x1, starting transfers between devices, shards(): part = lax.ppermute(part, 'tp', swap)  1.76 us
  transfers between devices with their start and end apart: 18, of which 10 were waited for; matrix products, arithmetic and copies ran while one was open for 0% of the time, Pallas kernels for 28%

profile of v5, /device:TPU:0, one launch (start us, length us, event | category | flops | bytes accessed | tf_op | source)
XLA Modules:
  0.0 53.2 jit_solution(3345628242640189694)
XLA Ops:
  0.0 0.0 copy-start.6
  0.0 0.1 pad_add_fusion.index_ref
  0.1 1.2 %pad_maximum_fusion.source_ref = bf16[768,512]{1,0:T(8,128)(2,1)S(1)} fusion(bf16[256,512]{1,0:T(8,128)(2,1)} %param.13, bf16[256,512]{1,0:T(8,128)(2,1)} %param.12, bf16[256,512]{1,0:T(8,128)(2,1)} %param.11), kind=kLoop, calls=%fused_computation | loop fusion | flops 2359296 | bytes 1572864 | tf_op jit(solution)/shard_map/concatenate | solution.py:582
  1.2 0.0 copy-done.6
  1.2 0.0 copy-start.3
  1.3 1.0 %shard_map.100 = (bf16[240,128]{1,0:T(8,128)(2,1)S(1)}, bf16[240,128]{1,0:T(8,128)(2,1)S(1)}, bf16[768,128]{1,0:T(8,128)(2,1)S(1)}, bf16[1536,128]{1,0:T(8,128)(2,1)S(1)}, bf16[768,128]{1,0:T(8,128)(2,1)S(1)}) custom-call(s32[6,8]{1,0:T(8,128)S(1)} %copy-done.6, s32[2]{0:T(128)S(1)} %pad_add_fusion.index_ref, bf16[768,512]{1,0:T(8,128)(2,1)S(1)} %pad_maximum_fusion.source_ref), custom_call_target="tpu_custom_call" | custom-call | flops 1153500032 | tf_op jit(solution)/shard_map/pallas_call | solution.py:532
  2.3 0.5 collective-permute-start
  2.8 2.6 %collective-permute-start.1 = (bf16[240,128]{1,0:T(8,128)(2,1)S(1)}, bf16[240,128]{1,0:T(8,128)(2,1)S(1)}, u32[]{:S(2)}, u32[]{:S(2)}) collective-permute-start(bf16[240,128]{1,0:T(8,128)(2,1)S(1)} %get-tuple-element.43), channel_id=1, source_target_pairs={{0,4},{2,6},{4,0},{6,2},{8,12},{10,14},{12,8},{14,10},{16,20},{18,... | collective-permute-start | bytes 184328 | tf_op jit(solution)/shard_map/ppermute | solution.py:574
  5.4 0.1 collective-permute-start.2
  5.4 0.0 copy-done.3
  5.5 1.8 %collective-permute-start.13 = (bf16[256,1024]{1,0:T(8,128)(2,1)S(1)}, bf16[256,1024]{1,0:T(8,128)(2,1)S(1)}, u32[]{:S(2)}, u32[]{:S(2)}) collective-permute-start(bf16[256,1024]{1,0:T(8,128)(2,1)S(1)} %constant_dynamic-slice_fusion), channel_id=1, source_target_pairs={{0,1},{1,0},{2,3},{3,2},{4,5},{5,4},{6,7},{7,6},{8,9},{9,8},{10,11... | collective-permute-start | bytes 1572872 | tf_op jit(solution)/shard_map/ppermute | solution.py:579
  7.2 0.0 collective-permute-done.pair_ref
  7.2 0.0 copy-start.5
  7.3 1.8 %shard_map.101 = (f32[2,2,256,128]{3,2,1,0:T(8,128)S(1)}, bf16[240,128]{1,0:T(8,128)(2,1)S(1)}, bf16[240,128]{1,0:T(8,128)(2,1)S(1)}, bf16[1536,128]{1,0:T(8,128...) custom-call(s32[6,8]{1,0:T(8,128)S(1)} %copy-done.6, ...), custom_call_target="tpu_custom_call" | custom-call | flops 2768399872 | tf_op jit(solution)/shard_map/pallas_call | solution.py:532
  9.1 0.0 collective-permute-done.1.refs_2_
  9.1 0.3 collective-permute-done.2.refs_3_
  9.3 0.6 %shard_map.102 = (bf16[4,240,128]{2,1,0:T(8,128)(2,1)S(1)}, bf16[4,112,128]{2,1,0:T(8,128)(2,1)S(1)}, bf16[1536,128]{1,0:T(8,128)(2,1)S(1)}) custom-call(s32[2]{0:T(128)S(1)} %pad_add_fusion.index_ref, bf16[240,128]{1,0:T(8,128)(2,1)S(1)} %get-tuple-element.41.refs_0_, ...), custom_call_target="tpu_custom_call", output_to_operand_aliasing={{2}: (5, {})} | custom-call | flops 346049984 | tf_op jit(solution)/shard_map/pallas_call | solution.py:532
  9.9 1.3 %collective-permute-start.3 = (bf16[1536,128]{1,0:T(8,128)(2,1)S(1)}, bf16[1536,128]{1,0:T(8,128)(2,1)S(1)}, u32[]{:S(2)}, u32[]{:S(2)}) collective-permute-start(bf16[1536,128]{1,0:T(8,128)(2,1)S(1)} %get-tuple-element.46), channel_id=1, source_target_pairs={{0,4},{2,6},{4,0},{6,2},{8,12},{10,14},{12,8},{14,10},{16,20},{18,... | collective-permute-start | bytes 1179656 | tf_op jit(solution)/shard_map/ppermute | solution.py:574
  11.3 2.6 %collective-permute-start.6 = (bf16[4,112,128]{2,1,0:T(8,128)(2,1)S(1)}, bf16[4,112,128]{2,1,0:T(8,128)(2,1)S(1)}, u32[]{:S(2)}, u32[]{:S(2)}) collective-permute-start(bf16[4,112,128]{2,1,0:T(8,128)(2,1)S(1)} %get-tuple-element.53), channel_id=1, source_target_pairs={{0,16},{2,18},{4,20},{6,22},{8,24},{10,26},{12,28},{14,30},{16,0},... | collective-permute-start | bytes 344072 | tf_op jit(solution)/shard_map/ppermute | solution.py:574
  13.9 1.3 %collective-permute-start.7 = (bf16[4,112,128]{2,1,0:T(8,128)(2,1)S(1)}, bf16[4,112,128]{2,1,0:T(8,128)(2,1)S(1)}, u32[]{:S(2)}, u32[]{:S(2)}) collective-permute-start(bf16[4,112,128]{2,1,0:T(8,128)(2,1)S(1)} %get-tuple-element.53), channel_id=1, source_target_pairs={{0,24},{2,26},{4,28},{6,30},{8,16},{10,18},{12,20},{14,22},{16,8},... | collective-permute-start | bytes 344072 | tf_op jit(solution)/shard_map/ppermute | solution.py:574
  15.2 0.2 collective-permute-start.5
  15.4 4.2 %collective-permute-done.13.refs_2_ = bf16[256,1024]{1,0:T(8,128)(2,1)S(1)} collective-permute-done((bf16[256,1024]{1,0:T(8,128)(2,1)S(1)}, bf16[256,1024]{1,0:T(8,128)(2,1)S(1)}, u32[]{:S(2)}, u32[]{:S(2)}) %collective-permute-start.13) | collective-permute-done | bytes 524320 | tf_op jit(solution)/shard_map/ppermute | solution.py:579
  19.7 0.0 collective-permute-start.14
  19.7 1.8 %collective-permute-done.3.refs_0_ = bf16[1536,128]{1,0:T(8,128)(2,1)S(1)} collective-permute-done((bf16[1536,128]{1,0:T(8,128)(2,1)S(1)}, bf16[1536,128]{1,0:T(8,128)(2,1)S(1)}, u32[]{:S(2)}, u32[]{:S(2)}) %collective-permute-start.3) | collective-permute-done | bytes 393248 | tf_op jit(solution)/shard_map/ppermute | solution.py:574
  21.5 0.0 copy-done.5
  21.5 3.1 %shard_map.103 = (f32[2,4,256,128]{3,2,1,0:T(8,128)S(1)}, f32[2,4,128,128]{3,2,1,0:T(8,128)S(1)}, f32[2,128,128]{2,1,0:T(8,128)S(1)}, bf16[4,128,128]{2,1,0:T(8,128)(2,1)S(1)}, bf16[256,512]{1,0:T(8,128)(2,1)S(1)}) custom-call(s32[2]{0:T(128)S(1)} %pad_add_fusion.index_ref, bf16[1536,128]{1,0:T(8,128)(2,1)S(1)} %collective-permute-done.3.refs_0_, ...), custom_call_target="tpu_custom_call" | custom-call | flops 3921900032 | tf_op jit(solution)/shard_map/pallas_call | solution.py:532
  24.6 1.6 %collective-permute-start.4 = (bf16[256,512]{1,0:T(8,128)(2,1)S(1)}, bf16[256,512]{1,0:T(8,128)(2,1)S(1)}, u32[]{:S(2)}, u32[]{:S(2)}) collective-permute-start(bf16[256,512]{1,0:T(8,128)(2,1)S(1)} %get-tuple-element.51), channel_id=1, source_target_pairs={{0,1},{1,0},{2,3},{3,2},{4,5},{5,4},{6,7},{7,6},{8,9},{9,8},{10,11... | collective-permute-start | bytes 786440 | tf_op jit(solution)/shard_map/ppermute | solution.py:667
  26.1 0.0 collective-permute-done.6.refs_2_
  26.1 0.0 collective-permute-done.7.refs_3_
  26.1 0.4 collective-permute-done.5.refs_1_
  26.6 4.5 %shard_map.104 = (bf16[256,128]{1,0:T(8,128)(2,1)S(1)}, bf16[256,128]{1,0:T(8,128)(2,1)S(1)}, bf16[256,128]{1,0:T(8,128)(2,1)S(1)}, bf16[256,128]{1,0:T(8,128)(2,1)S(1)}) custom-call(s32[6,8]{1,0:T(8,128)S(1)} %copy-done.6, s32[2]{0:T(128)S(1)} %pad_add_fusion.index_ref, bf16[4,240,128]{2,1,0:T(8,128)(2,1)S(1)} %get-tuple-element.52.refs_0_, ...), custom_call_target="tpu_custom_call" | custom-call | flops 6920999936 | tf_op jit(solution)/shard_map/pallas_call | solution.py:532
  31.0 0.1 collective-permute-start.8
  31.1 1.0 %collective-permute-start.9 = (bf16[256,128]{1,0:T(8,128)(2,1)S(1)}, bf16[256,128]{1,0:T(8,128)(2,1)S(1)}, u32[]{:S(2)}, u32[]{:S(2)}) collective-permute-start(bf16[256,128]{1,0:T(8,128)(2,1)S(1)} %get-tuple-element.61), channel_id=1, source_target_pairs={{0,4},{2,6},{4,0},{6,2},{8,12},{10,14},{12,8},{14,10},{16,20},{18,... | collective-permute-start | bytes 196616 | tf_op jit(solution)/shard_map/ppermute | solution.py:574
  32.1 0.2 collective-permute-done.8.core_ref.refs_1_
  32.4 0.0 copy-start.2
  32.4 0.8 %collective-permute-start.10 = (bf16[256,128]{1,0:T(8,128)(2,1)S(1)}, bf16[256,128]{1,0:T(8,128)(2,1)S(1)}, u32[]{:S(2)}, u32[]{:S(2)}) collective-permute-start(bf16[256,128]{1,0:T(8,128)(2,1)S(1)} %get-tuple-element.63), channel_id=1, source_target_pairs={{0,6},{2,4},{4,2},{6,0},{8,14},{10,12},{12,10},{14,8},{16,22},{18,... | collective-permute-start | bytes 196616 | tf_op jit(solution)/shard_map/ppermute | solution.py:574
  33.1 1.4 %collective-permute-start.11 = (bf16[512,128]{1,0:T(8,128)(2,1)S(1)}, bf16[512,128]{1,0:T(8,128)(2,1)S(1)}, u32[]{:S(2)}, u32[]{:S(2)}) collective-permute-start(bf16[512,128]{1,0:T(8,128)(2,1)S(1)} %get-tuple-element.64), channel_id=1, source_target_pairs={{0,1},{1,0},{2,3},{3,2},{4,5},{5,4},{6,7},{7,6},{8,9},{9,8},{10,11... | collective-permute-start | bytes 393224 | tf_op jit(solution)/shard_map/ppermute | solution.py:665
  34.6 1.3 %collective-permute-done.9.refs_2_.first_ref = bf16[256,128]{1,0:T(8,128)(2,1)S(1)} collective-permute-done((bf16[256,128]{1,0:T(8,128)(2,1)S(1)}, bf16[256,128]{1,0:T(8,128)(2,1)S(1)}, u32[]{:S(2)}, u32[]{:S(2)}) %collective-permute-start.9) | collective-permute-done | bytes 65568 | tf_op jit(solution)/shard_map/ppermute | solution.py:574
  35.9 0.9 %collective-permute-done.10.refs_3_.second_ref = bf16[256,128]{1,0:T(8,128)(2,1)S(1)} collective-permute-done((bf16[256,128]{1,0:T(8,128)(2,1)S(1)}, bf16[256,128]{1,0:T(8,128)(2,1)S(1)}, u32[]{:S(2)}, u32[]{:S(2)}) %collective-permute-start.10) | collective-permute-done | bytes 65568 | tf_op jit(solution)/shard_map/ppermute | solution.py:574
  36.8 1.6 %collective-permute-start.15 = (bf16[256,128]{1,0:T(8,128)(2,1)S(1)}, bf16[256,128]{1,0:T(8,128)(2,1)S(1)}, u32[]{:S(2)}, u32[]{:S(2)}) collective-permute-start(bf16[256,128]{1,0:T(8,128)(2,1)S(1)} %get-tuple-element.67), channel_id=1, source_target_pairs={{0,1},{1,0},{2,3},{3,2},{4,5},{5,4},{6,7},{7,6},{8,9},{9,8},{10,11... | collective-permute-start | bytes 196616 | tf_op jit(solution)/shard_map/ppermute | solution.py:666
  38.4 0.0 copy-start
  38.4 0.0 copy-start.1
  38.4 0.0 copy-start.4
  38.4 0.5 %collective-permute-start.12 = (bf16[256,128]{1,0:T(8,128)(2,1)S(1)}, bf16[256,128]{1,0:T(8,128)(2,1)S(1)}, u32[]{:S(2)}, u32[]{:S(2)}) collective-permute-start(bf16[256,128]{1,0:T(8,128)(2,1)S(1)} %get-tuple-element.65), channel_id=1, source_target_pairs={{0,1},{1,0},{2,3},{3,2},{4,5},{5,4},{6,7},{7,6},{8,9},{9,8},{10,11... | collective-permute-start | bytes 196616 | tf_op jit(solution)/shard_map/ppermute | solution.py:666
  38.9 0.0 collective-permute-done.4.other_residual_ref
  38.9 1.1 %shard_map.106.own_ref = f32[256,1024]{1,0:T(8,128)S(1)} custom-call(s32[2]{0:T(128)S(1)} %pad_add_fusion.index_ref, bf16[256,512]{1,0:T(8,128)(2,1)S(1)} %copy-done.5, bf16[256,512]{1,0:T(8,128)(2,1)S(1)} %collective-permute-done.4.other_residual_ref, bf16[512,1024]{1,0:T(8,128)(2,1)S(1)} %copy-done.3, ...), custom_call_target="tpu_custom_call" | custom-call | flops 1384199936 | tf_op jit(solution)/shard_map/pallas_call | solution.py:532
  40.0 0.0 collective-permute-done.11.refs_0_
  40.1 1.4 %collective-permute-done.15.refs_1_ = bf16[256,128]{1,0:T(8,128)(2,1)S(1)} collective-permute-done((bf16[256,128]{1,0:T(8,128)(2,1)S(1)}, bf16[256,128]{1,0:T(8,128)(2,1)S(1)}, u32[]{:S(2)}, u32[]{:S(2)}) %collective-permute-start.15) | collective-permute-done | bytes 65568 | tf_op jit(solution)/shard_map/ppermute | solution.py:666
  41.5 0.0 collective-permute-done.14.refs_3_
  41.5 0.0 copy-done.2
  41.5 0.0 copy-done
  41.5 0.0 copy-done.1
  41.5 0.0 copy-done.4
  41.5 2.0 %shard_map.109 = (bf16[128,512]{1,0:T(8,128)(2,1)S(1)}, f32[128,512]{1,0:T(8,128)S(1)}) custom-call(s32[2]{0:T(128)S(1)} %pad_add_fusion.index_ref, f32[256,1024]{1,0:T(8,128)S(1)} %shard_map.106.own_ref, bf16[512,128]{1,0:T(8,128)(2,1)S(1)} %collective-permute-done.11.refs_0_, bf16[256,128]{1,0:T(8,128)(2,1)S(1)} %collective-permute-done.15.refs_1_, ...), custom_call_target="tpu_custom_call" | custom-call | flops 2307000064 | tf_op jit(solution)/shard_map/pallas_call | solution.py:532
  43.5 1.9 %collective-permute-start.17 = (bf16[128,512]{1,0:T(8,128)(2,1)S(1)}, bf16[128,512]{1,0:T(8,128)(2,1)S(1)}, u32[]{:S(2)}, u32[]{:S(2)}) collective-permute-start(bf16[128,512]{1,0:T(8,128)(2,1)S(1)} %get-tuple-element.70), channel_id=1, source_target_pairs={{0,1},{1,0},{2,3},{3,2},{4,5},{5,4},{6,7},{7,6},{8,9},{9,8},{10,11... | collective-permute-start | bytes 393224 | tf_op jit(solution)/shard_map/ppermute | solution.py:704
  45.4 0.0 collective-permute-done.12.refs_1_
  45.4 2.0 %shard_map.108 = (bf16[128,512]{1,0:T(8,128)(2,1)S(1)}, f32[128,512]{1,0:T(8,128)S(1)}) custom-call(s32[2]{0:T(128)S(1)} %pad_add_fusion.index_ref, f32[256,1024]{1,0:T(8,128)S(1)} %shard_map.106.own_ref, bf16[512,128]{1,0:T(8,128)(2,1)S(1)} %collective-permute-done.11.refs_0_, bf16[256,128]{1,0:T(8,128)(2,1)S(1)} %collective-permute-done.12.refs_1_, ...), custom_call_target="tpu_custom_call" | custom-call | flops 2307000064 | tf_op jit(solution)/shard_map/pallas_call | solution.py:532
  47.4 0.3 collective-permute-start.16
  47.7 1.3 %collective-permute-done.17.refs_3_ = bf16[128,512]{1,0:T(8,128)(2,1)S(1)} collective-permute-done((bf16[128,512]{1,0:T(8,128)(2,1)S(1)}, bf16[128,512]{1,0:T(8,128)(2,1)S(1)}, u32[]{:S(2)}, u32[]{:S(2)}) %collective-permute-start.17) | collective-permute-done | bytes 131104 | tf_op jit(solution)/shard_map/ppermute | solution.py:704
  48.9 3.5 %collective-permute-done.16.refs_2_ = bf16[128,512]{1,0:T(8,128)(2,1)S(1)} collective-permute-done((bf16[128,512]{1,0:T(8,128)(2,1)S(1)}, bf16[128,512]{1,0:T(8,128)(2,1)S(1)}, u32[]{:S(2)}, u32[]{:S(2)}) %collective-permute-start.16) | collective-permute-done | bytes 131104 | tf_op jit(solution)/shard_map/ppermute | solution.py:704
  52.4 0.8 %shard_map.110 = bf16[256,512]{1,0:T(8,128)(2,1)} custom-call(f32[128,512]{1,0:T(8,128)S(1)} %get-tuple-element.66.refs_0_, f32[128,512]{1,0:T(8,128)S(1)} %get-tuple-element.68.refs_1_, bf16[128,512]{1,0:T(8,128)(2,1)S(1)} %collective-permute-done.16.refs_2_, bf16[128,512]{1,0:T(8,128)(2,1)S(1)} %collective-permute-done.17.refs_3_), custom_call_target="tpu_custom_call" | custom-call | flops 922800000 | tf_op jit(solution)/shard_map/pallas_call | solution.py:532
  (3 shorter events, 0.1 us)
Async XLA Ops:
  0.0 1.2 %copy-start.6 = (s32[6,8]{1,0:T(8,128)S(1)}, s32[6,8]{1,0:T(8,128)}, u32[]{:S(2)}) copy-start(s32[6,8]{1,0:T(8,128)} %offset_ref.5) | copy-start | bytes 580
  1.2 4.2 %copy-start.3 = (bf16[512,1024]{1,0:T(8,128)(2,1)S(1)}, bf16[512,1024]{1,0:T(8,128)(2,1)}, u32[]{:S(2)}) copy-start(bf16[512,1024]{1,0:T(8,128)(2,1)} %weight_ref.1) | copy-start | bytes 3145732
  2.3 5.0 %collective-permute-start = (bf16[1536,128]{1,0:T(8,128)(2,1)S(1)}, bf16[1536,128]{1,0:T(8,128)(2,1)S(1)}, u32[]{:S(2)}, u32[]{:S(2)}) collective-permute-start(bf16[1536,128]{1,0:T(8,128)(2,1)S(1)} %get-tuple-element.39), channel_id=1, source_target_pairs={{0,2},{2,0},{4,6},{6,4},{8,10},{10,8},{12,14},{14,12},{16,18},{18,... | collective-permute-start | bytes 1179656 | tf_op jit(solution)/shard_map/ppermute | solution.py:574
  2.8 6.3 %collective-permute-start.1 = (bf16[240,128]{1,0:T(8,128)(2,1)S(1)}, bf16[240,128]{1,0:T(8,128)(2,1)S(1)}, u32[]{:S(2)}, u32[]{:S(2)}) collective-permute-start(bf16[240,128]{1,0:T(8,128)(2,1)S(1)} %get-tuple-element.43), channel_id=1, source_target_pairs={{0,4},{2,6},{4,0},{6,2},{8,12},{10,14},{12,8},{14,10},{16,20},{18,... | collective-permute-start | bytes 184328 | tf_op jit(solution)/shard_map/ppermute | solution.py:574
  5.4 4.0 %collective-permute-start.2 = (bf16[240,128]{1,0:T(8,128)(2,1)S(1)}, bf16[240,128]{1,0:T(8,128)(2,1)S(1)}, u32[]{:S(2)}, u32[]{:S(2)}) collective-permute-start(bf16[240,128]{1,0:T(8,128)(2,1)S(1)} %get-tuple-element.44), channel_id=1, source_target_pairs={{0,6},{2,4},{4,2},{6,0},{8,14},{10,12},{12,10},{14,8},{16,22},{18,... | collective-permute-start | bytes 184328 | tf_op jit(solution)/shard_map/ppermute | solution.py:574
  5.5 14.2 %collective-permute-start.13 = (bf16[256,1024]{1,0:T(8,128)(2,1)S(1)}, bf16[256,1024]{1,0:T(8,128)(2,1)S(1)}, u32[]{:S(2)}, u32[]{:S(2)}) collective-permute-start(bf16[256,1024]{1,0:T(8,128)(2,1)S(1)} %constant_dynamic-slice_fusion), channel_id=1, source_target_pairs={{0,1},{1,0},{2,3},{3,2},{4,5},{5,4},{6,7},{7,6},{8,9},{9,8},{10,11... | collective-permute-start | bytes 1572872 | tf_op jit(solution)/shard_map/ppermute | solution.py:579
  7.2 14.2 %copy-start.5 = (bf16[256,512]{1,0:T(8,128)(2,1)S(1)}, bf16[256,512]{1,0:T(8,128)(2,1)}, u32[]{:S(2)}) copy-start(bf16[256,512]{1,0:T(8,128)(2,1)} %residual_ref.1) | copy-start | bytes 786436
  9.9 11.5 %collective-permute-start.3 = (bf16[1536,128]{1,0:T(8,128)(2,1)S(1)}, bf16[1536,128]{1,0:T(8,128)(2,1)S(1)}, u32[]{:S(2)}, u32[]{:S(2)}) collective-permute-start(bf16[1536,128]{1,0:T(8,128)(2,1)S(1)} %get-tuple-element.46), channel_id=1, source_target_pairs={{0,4},{2,6},{4,0},{6,2},{8,12},{10,14},{12,8},{14,10},{16,20},{18,... | collective-permute-start | bytes 1179656 | tf_op jit(solution)/shard_map/ppermute | solution.py:574
  11.3 14.9 %collective-permute-start.6 = (bf16[4,112,128]{2,1,0:T(8,128)(2,1)S(1)}, bf16[4,112,128]{2,1,0:T(8,128)(2,1)S(1)}, u32[]{:S(2)}, u32[]{:S(2)}) collective-permute-start(bf16[4,112,128]{2,1,0:T(8,128)(2,1)S(1)} %get-tuple-element.53), channel_id=1, source_target_pairs={{0,16},{2,18},{4,20},{6,22},{8,24},{10,26},{12,28},{14,30},{16,0},... | collective-permute-start | bytes 344072 | tf_op jit(solution)/shard_map/ppermute | solution.py:574
  13.9 12.3 %collective-permute-start.7 = (bf16[4,112,128]{2,1,0:T(8,128)(2,1)S(1)}, bf16[4,112,128]{2,1,0:T(8,128)(2,1)S(1)}, u32[]{:S(2)}, u32[]{:S(2)}) collective-permute-start(bf16[4,112,128]{2,1,0:T(8,128)(2,1)S(1)} %get-tuple-element.53), channel_id=1, source_target_pairs={{0,24},{2,26},{4,28},{6,30},{8,16},{10,18},{12,20},{14,22},{16,8},... | collective-permute-start | bytes 344072 | tf_op jit(solution)/shard_map/ppermute | solution.py:574
  15.2 11.4 %collective-permute-start.5 = (bf16[4,240,128]{2,1,0:T(8,128)(2,1)S(1)}, bf16[4,240,128]{2,1,0:T(8,128)(2,1)S(1)}, u32[]{:S(2)}, u32[]{:S(2)}) collective-permute-start(bf16[4,240,128]{2,1,0:T(8,128)(2,1)S(1)} %get-tuple-element.52.refs_0_), channel_id=1, source_target_pairs={{0,8},{2,10},{4,12},{6,14},{8,0},{10,2},{12,4},{14,6},{16,24},{18,... | collective-permute-start | bytes 737288 | tf_op jit(solution)/shard_map/ppermute | solution.py:574
  19.7 21.8 %collective-permute-start.14 = (bf16[256,1024]{1,0:T(8,128)(2,1)S(1)}, bf16[256,1024]{1,0:T(8,128)(2,1)S(1)}, u32[]{:S(2)}, u32[]{:S(2)}) collective-permute-start(bf16[256,1024]{1,0:T(8,128)(2,1)S(1)} %collective-permute-done.13.refs_2_), channel_id=1, source_target_pairs={{0,2},{2,0},{4,6},{6,4},{8,10},{10,8},{12,14},{14,12},{16,18},{18,... | collective-permute-start | bytes 1572872 | tf_op jit(solution)/shard_map/ppermute | solution.py:574
  24.6 14.3 %collective-permute-start.4 = (bf16[256,512]{1,0:T(8,128)(2,1)S(1)}, bf16[256,512]{1,0:T(8,128)(2,1)S(1)}, u32[]{:S(2)}, u32[]{:S(2)}) collective-permute-start(bf16[256,512]{1,0:T(8,128)(2,1)S(1)} %get-tuple-element.51), channel_id=1, source_target_pairs={{0,1},{1,0},{2,3},{3,2},{4,5},{5,4},{6,7},{7,6},{8,9},{9,8},{10,11... | collective-permute-start | bytes 786440 | tf_op jit(solution)/shard_map/ppermute | solution.py:667
  31.0 1.3 %collective-permute-start.8 = (bf16[256,128]{1,0:T(8,128)(2,1)S(1)}, bf16[256,128]{1,0:T(8,128)(2,1)S(1)}, u32[]{:S(2)}, u32[]{:S(2)}) collective-permute-start(bf16[256,128]{1,0:T(8,128)(2,1)S(1)} %get-tuple-element.60), channel_id=1, source_target_pairs={{0,2},{2,0},{4,6},{6,4},{8,10},{10,8},{12,14},{14,12},{16,18},{18,... | collective-permute-start | bytes 196616 | tf_op jit(solution)/shard_map/ppermute | solution.py:574
  31.1 4.7 %collective-permute-start.9 = (bf16[256,128]{1,0:T(8,128)(2,1)S(1)}, bf16[256,128]{1,0:T(8,128)(2,1)S(1)}, u32[]{:S(2)}, u32[]{:S(2)}) collective-permute-start(bf16[256,128]{1,0:T(8,128)(2,1)S(1)} %get-tuple-element.61), channel_id=1, source_target_pairs={{0,4},{2,6},{4,0},{6,2},{8,12},{10,14},{12,8},{14,10},{16,20},{18,... | collective-permute-start | bytes 196616 | tf_op jit(solution)/shard_map/ppermute | solution.py:574
  32.4 9.1 %copy-start.2 = (bf16[1024,1024]{1,0:T(8,128)(2,1)S(1)}, bf16[1024,1024]{1,0:T(8,128)(2,1)}, u32[]{:S(2)}) copy-start(bf16[1024,1024]{1,0:T(8,128)(2,1)} %refs_7_.3) | copy-start | bytes 6291460
  32.4 4.4 %collective-permute-start.10 = (bf16[256,128]{1,0:T(8,128)(2,1)S(1)}, bf16[256,128]{1,0:T(8,128)(2,1)S(1)}, u32[]{:S(2)}, u32[]{:S(2)}) collective-permute-start(bf16[256,128]{1,0:T(8,128)(2,1)S(1)} %get-tuple-element.63), channel_id=1, source_target_pairs={{0,6},{2,4},{4,2},{6,0},{8,14},{10,12},{12,10},{14,8},{16,22},{18,... | collective-permute-start | bytes 196616 | tf_op jit(solution)/shard_map/ppermute | solution.py:574
  33.1 6.9 %collective-permute-start.11 = (bf16[512,128]{1,0:T(8,128)(2,1)S(1)}, bf16[512,128]{1,0:T(8,128)(2,1)S(1)}, u32[]{:S(2)}, u32[]{:S(2)}) collective-permute-start(bf16[512,128]{1,0:T(8,128)(2,1)S(1)} %get-tuple-element.64), channel_id=1, source_target_pairs={{0,1},{1,0},{2,3},{3,2},{4,5},{5,4},{6,7},{7,6},{8,9},{9,8},{10,11... | collective-permute-start | bytes 393224 | tf_op jit(solution)/shard_map/ppermute | solution.py:665
  36.8 4.7 %collective-permute-start.15 = (bf16[256,128]{1,0:T(8,128)(2,1)S(1)}, bf16[256,128]{1,0:T(8,128)(2,1)S(1)}, u32[]{:S(2)}, u32[]{:S(2)}) collective-permute-start(bf16[256,128]{1,0:T(8,128)(2,1)S(1)} %get-tuple-element.67), channel_id=1, source_target_pairs={{0,1},{1,0},{2,3},{3,2},{4,5},{5,4},{6,7},{7,6},{8,9},{9,8},{10,11... | collective-permute-start | bytes 196616 | tf_op jit(solution)/shard_map/ppermute | solution.py:666
  38.4 3.1 %copy-start = (bf16[1024,1024]{1,0:T(8,128)(2,1)S(1)}, bf16[1024,1024]{1,0:T(8,128)(2,1)}, u32[]{:S(2)}) copy-start(bf16[1024,1024]{1,0:T(8,128)(2,1)} %refs_5_.5) | copy-start | bytes 6291460
  38.4 3.1 %copy-start.1 = (bf16[1024,1024]{1,0:T(8,128)(2,1)S(1)}, bf16[1024,1024]{1,0:T(8,128)(2,1)}, u32[]{:S(2)}) copy-start(bf16[1024,1024]{1,0:T(8,128)(2,1)} %refs_6_.3) | copy-start | bytes 6291460
  38.4 3.1 %copy-start.4 = (f32[1024]{0:T(1024)S(1)}, f32[1024]{0:T(1024)}, u32[]{:S(2)}) copy-start(f32[1024]{0:T(1024)} %param.16) | copy-start | bytes 12292
  38.4 7.0 %collective-permute-start.12 = (bf16[256,128]{1,0:T(8,128)(2,1)S(1)}, bf16[256,128]{1,0:T(8,128)(2,1)S(1)}, u32[]{:S(2)}, u32[]{:S(2)}) collective-permute-start(bf16[256,128]{1,0:T(8,128)(2,1)S(1)} %get-tuple-element.65), channel_id=1, source_target_pairs={{0,1},{1,0},{2,3},{3,2},{4,5},{5,4},{6,7},{7,6},{8,9},{9,8},{10,11... | collective-permute-start | bytes 196616 | tf_op jit(solution)/shard_map/ppermute | solution.py:666
  43.5 5.4 %collective-permute-start.17 = (bf16[128,512]{1,0:T(8,128)(2,1)S(1)}, bf16[128,512]{1,0:T(8,128)(2,1)S(1)}, u32[]{:S(2)}, u32[]{:S(2)}) collective-permute-start(bf16[128,512]{1,0:T(8,128)(2,1)S(1)} %get-tuple-element.70), channel_id=1, source_target_pairs={{0,1},{1,0},{2,3},{3,2},{4,5},{5,4},{6,7},{7,6},{8,9},{9,8},{10,11... | collective-permute-start | bytes 393224 | tf_op jit(solution)/shard_map/ppermute | solution.py:704
  47.4 5.0 %collective-permute-start.16 = (bf16[128,512]{1,0:T(8,128)(2,1)S(1)}, bf16[128,512]{1,0:T(8,128)(2,1)S(1)}, u32[]{:S(2)}, u32[]{:S(2)}) collective-permute-start(bf16[128,512]{1,0:T(8,128)(2,1)S(1)} %get-tuple-element.69), channel_id=1, source_target_pairs={{0,1},{1,0},{2,3},{3,2},{4,5},{5,4},{6,7},{7,6},{8,9},{9,8},{10,11... | collective-permute-start | bytes 393224 | tf_op jit(solution)/shard_map/ppermute | solution.py:704

commit v6 on v4

--- a/solution.py
+++ b/solution.py
@@ -332,7 +332,7 @@
                 jobs.append((query.astype(jnp.bfloat16), pairs, (span - 1) * length, columns))
                 slots.append((branch, head, count))
             first += each * count
-    for (branch, head, count), (top, accum) in zip(slots, attend(jobs, 2 * len(jobs))):
+    for (branch, head, count), (top, accum) in zip(slots, attend(jobs, 5)):
         into = slice(starts[branch], starts[branch] + count)
         far[head, :, into, :] = accum.reshape(NEAR, count, LANES)
         tops[head, into, :] = top_lanes(top, count, branch)

time: 53.1 us -> 52.9 us (level)
  no operation moved by 1% of the time
where the time goes in v6:
time: 52.9 us; the launch traced here: 52.8 us
  starting transfers between devices  19.7 us (37%)
  Pallas kernels  16.6 us (31%)
  waiting for transfers between devices  15.1 us (29%)
  other arithmetic  1.23 us (2%)
    pallas_call x11, Pallas kernels, call(): pl.pallas_call(kernel, out_shape=out_shape, in_specs=specs, out_specs=out...  16.6 us
    ppermute x11, starting transfers between devices, across(): lax.ppermute(block, 'seq', [(i, i ^ distance) for i in range(seq_count)])  10.7 us
    ppermute x11, waiting for transfers between devices, across(): lax.ppermute(block, 'seq', [(i, i ^ distance) for i in range(seq_count)])  4.88 us
    ppermute x2, waiting for transfers between devices, shards(): theirs.append(lax.ppermute(send, 'tp', swap))  4.69 us
    ppermute x1, waiting for transfers between devices, shards(): part = lax.ppermute(part, 'tp', swap)  4.05 us
    ppermute x2, starting transfers between devices, shards(): theirs.append(lax.ppermute(send, 'tp', swap))  2.17 us
    ppermute x2, starting transfers between devices, shards(): parts = [lax.ppermute(block, 'tp', swap) for block in parts]  2.11 us
    ppermute x1, starting transfers between devices, shards(): part = lax.ppermute(part, 'tp', swap)  1.76 us
  transfers between devices with their start and end apart: 18, of which 10 were waited for; matrix products, arithmetic and copies ran while one was open for 0% of the time, Pallas kernels for 28%

profile of v6, /device:TPU:0, one launch (start us, length us, event | category | flops | bytes accessed | tf_op | source)
XLA Modules:
  0.0 52.8 jit_solution(1210717135980640268)
XLA Ops:
  0.0 0.0 copy-start.6
  0.0 0.1 pad_add_fusion.index_ref
  0.1 1.2 %pad_maximum_fusion.source_ref = bf16[768,512]{1,0:T(8,128)(2,1)S(1)} fusion(bf16[256,512]{1,0:T(8,128)(2,1)} %param.13, bf16[256,512]{1,0:T(8,128)(2,1)} %param.12, bf16[256,512]{1,0:T(8,128)(2,1)} %param.11), kind=kLoop, calls=%fused_computation | loop fusion | flops 2359296 | bytes 1572864 | tf_op jit(solution)/shard_map/concatenate | solution.py:581
  1.2 0.0 copy-done.6
  1.2 0.0 copy-start.3
  1.3 1.0 %shard_map.100 = (bf16[240,128]{1,0:T(8,128)(2,1)S(1)}, bf16[240,128]{1,0:T(8,128)(2,1)S(1)}, bf16[768,128]{1,0:T(8,128)(2,1)S(1)}, bf16[1536,128]{1,0:T(8,128)(2,1)S(1)}, bf16[768,128]{1,0:T(8,128)(2,1)S(1)}) custom-call(s32[6,8]{1,0:T(8,128)S(1)} %copy-done.6, s32[2]{0:T(128)S(1)} %pad_add_fusion.index_ref, bf16[768,512]{1,0:T(8,128)(2,1)S(1)} %pad_maximum_fusion.source_ref), custom_call_target="tpu_custom_call" | custom-call | flops 1153500032 | tf_op jit(solution)/shard_map/pallas_call | solution.py:531
  2.3 0.5 collective-permute-start
  2.8 2.6 %collective-permute-start.1 = (bf16[240,128]{1,0:T(8,128)(2,1)S(1)}, bf16[240,128]{1,0:T(8,128)(2,1)S(1)}, u32[]{:S(2)}, u32[]{:S(2)}) collective-permute-start(bf16[240,128]{1,0:T(8,128)(2,1)S(1)} %get-tuple-element.43), channel_id=1, source_target_pairs={{0,4},{2,6},{4,0},{6,2},{8,12},{10,14},{12,8},{14,10},{16,20},{18,... | collective-permute-start | bytes 184328 | tf_op jit(solution)/shard_map/ppermute | solution.py:573
  5.4 0.1 collective-permute-start.2
  5.4 0.0 copy-done.3
  5.5 1.8 %collective-permute-start.13 = (bf16[256,1024]{1,0:T(8,128)(2,1)S(1)}, bf16[256,1024]{1,0:T(8,128)(2,1)S(1)}, u32[]{:S(2)}, u32[]{:S(2)}) collective-permute-start(bf16[256,1024]{1,0:T(8,128)(2,1)S(1)} %constant_dynamic-slice_fusion), channel_id=1, source_target_pairs={{0,1},{1,0},{2,3},{3,2},{4,5},{5,4},{6,7},{7,6},{8,9},{9,8},{10,11... | collective-permute-start | bytes 1572872 | tf_op jit(solution)/shard_map/ppermute | solution.py:578
  7.2 0.0 collective-permute-done.pair_ref
  7.2 0.0 copy-start.5
  7.3 2.0 %shard_map.101 = (f32[2,2,256,128]{3,2,1,0:T(8,128)S(1)}, bf16[240,128]{1,0:T(8,128)(2,1)S(1)}, bf16[240,128]{1,0:T(8,128)(2,1)S(1)}, bf16[1536,128]{1,0:T(8,128...) custom-call(s32[6,8]{1,0:T(8,128)S(1)} %copy-done.6, ...), custom_call_target="tpu_custom_call" | custom-call | flops 2768399872 | tf_op jit(solution)/shard_map/pallas_call | solution.py:531
  9.2 0.0 collective-permute-done.1.refs_2_
  9.2 0.1 collective-permute-done.2.refs_3_
  9.3 0.6 %shard_map.102 = (bf16[4,240,128]{2,1,0:T(8,128)(2,1)S(1)}, bf16[4,112,128]{2,1,0:T(8,128)(2,1)S(1)}, bf16[1536,128]{1,0:T(8,128)(2,1)S(1)}) custom-call(s32[2]{0:T(128)S(1)} %pad_add_fusion.index_ref, bf16[240,128]{1,0:T(8,128)(2,1)S(1)} %get-tuple-element.41.refs_0_, ...), custom_call_target="tpu_custom_call", output_to_operand_aliasing={{2}: (5, {})} | custom-call | flops 346049984 | tf_op jit(solution)/shard_map/pallas_call | solution.py:531
  9.9 1.5 %collective-permute-start.3 = (bf16[1536,128]{1,0:T(8,128)(2,1)S(1)}, bf16[1536,128]{1,0:T(8,128)(2,1)S(1)}, u32[]{:S(2)}, u32[]{:S(2)}) collective-permute-start(bf16[1536,128]{1,0:T(8,128)(2,1)S(1)} %get-tuple-element.46), channel_id=1, source_target_pairs={{0,4},{2,6},{4,0},{6,2},{8,12},{10,14},{12,8},{14,10},{16,20},{18,... | collective-permute-start | bytes 1179656 | tf_op jit(solution)/shard_map/ppermute | solution.py:573
  11.4 2.6 %collective-permute-start.6 = (bf16[4,112,128]{2,1,0:T(8,128)(2,1)S(1)}, bf16[4,112,128]{2,1,0:T(8,128)(2,1)S(1)}, u32[]{:S(2)}, u32[]{:S(2)}) collective-permute-start(bf16[4,112,128]{2,1,0:T(8,128)(2,1)S(1)} %get-tuple-element.53), channel_id=1, source_target_pairs={{0,16},{2,18},{4,20},{6,22},{8,24},{10,26},{12,28},{14,30},{16,0},... | collective-permute-start | bytes 344072 | tf_op jit(solution)/shard_map/ppermute | solution.py:573
  14.0 1.4 %collective-permute-start.7 = (bf16[4,112,128]{2,1,0:T(8,128)(2,1)S(1)}, bf16[4,112,128]{2,1,0:T(8,128)(2,1)S(1)}, u32[]{:S(2)}, u32[]{:S(2)}) collective-permute-start(bf16[4,112,128]{2,1,0:T(8,128)(2,1)S(1)} %get-tuple-element.53), channel_id=1, source_target_pairs={{0,24},{2,26},{4,28},{6,30},{8,16},{10,18},{12,20},{14,22},{16,8},... | collective-permute-start | bytes 344072 | tf_op jit(solution)/shard_map/ppermute | solution.py:573
  15.4 0.2 collective-permute-start.5
  15.6 4.1 %collective-permute-done.13.refs_2_ = bf16[256,1024]{1,0:T(8,128)(2,1)S(1)} collective-permute-done((bf16[256,1024]{1,0:T(8,128)(2,1)S(1)}, bf16[256,1024]{1,0:T(8,128)(2,1)S(1)}, u32[]{:S(2)}, u32[]{:S(2)}) %collective-permute-start.13) | collective-permute-done | bytes 524320 | tf_op jit(solution)/shard_map/ppermute | solution.py:578
  19.7 0.0 collective-permute-start.14
  19.7 1.8 %collective-permute-done.3.refs_0_ = bf16[1536,128]{1,0:T(8,128)(2,1)S(1)} collective-permute-done((bf16[1536,128]{1,0:T(8,128)(2,1)S(1)}, bf16[1536,128]{1,0:T(8,128)(2,1)S(1)}, u32[]{:S(2)}, u32[]{:S(2)}) %collective-permute-start.3) | collective-permute-done | bytes 393248 | tf_op jit(solution)/shard_map/ppermute | solution.py:573
  21.5 0.0 copy-done.5
  21.5 3.1 %shard_map.103 = (f32[2,4,256,128]{3,2,1,0:T(8,128)S(1)}, f32[2,4,128,128]{3,2,1,0:T(8,128)S(1)}, f32[2,128,128]{2,1,0:T(8,128)S(1)}, bf16[4,128,128]{2,1,0:T(8,128)(2,1)S(1)}, bf16[256,512]{1,0:T(8,128)(2,1)S(1)}) custom-call(s32[2]{0:T(128)S(1)} %pad_add_fusion.index_ref, bf16[1536,128]{1,0:T(8,128)(2,1)S(1)} %collective-permute-done.3.refs_0_, ...), custom_call_target="tpu_custom_call" | custom-call | flops 3921900032 | tf_op jit(solution)/shard_map/pallas_call | solution.py:531
  24.6 1.5 %collective-permute-start.4 = (bf16[256,512]{1,0:T(8,128)(2,1)S(1)}, bf16[256,512]{1,0:T(8,128)(2,1)S(1)}, u32[]{:S(2)}, u32[]{:S(2)}) collective-permute-start(bf16[256,512]{1,0:T(8,128)(2,1)S(1)} %get-tuple-element.51), channel_id=1, source_target_pairs={{0,1},{1,0},{2,3},{3,2},{4,5},{5,4},{6,7},{7,6},{8,9},{9,8},{10,11... | collective-permute-start | bytes 786440 | tf_op jit(solution)/shard_map/ppermute | solution.py:666
  26.2 0.0 collective-permute-done.6.refs_2_
  26.2 0.0 collective-permute-done.7.refs_3_
  26.2 0.5 collective-permute-done.5.refs_1_
  26.6 4.0 %shard_map.104 = (bf16[256,128]{1,0:T(8,128)(2,1)S(1)}, bf16[256,128]{1,0:T(8,128)(2,1)S(1)}, bf16[256,128]{1,0:T(8,128)(2,1)S(1)}, bf16[256,128]{1,0:T(8,128)(2,1)S(1)}) custom-call(s32[6,8]{1,0:T(8,128)S(1)} %copy-done.6, s32[2]{0:T(128)S(1)} %pad_add_fusion.index_ref, bf16[4,240,128]{2,1,0:T(8,128)(2,1)S(1)} %get-tuple-element.52.refs_0_, ...), custom_call_target="tpu_custom_call" | custom-call | flops 6920999936 | tf_op jit(solution)/shard_map/pallas_call | solution.py:531
  30.7 0.1 collective-permute-start.8
  30.7 1.0 %collective-permute-start.9 = (bf16[256,128]{1,0:T(8,128)(2,1)S(1)}, bf16[256,128]{1,0:T(8,128)(2,1)S(1)}, u32[]{:S(2)}, u32[]{:S(2)}) collective-permute-start(bf16[256,128]{1,0:T(8,128)(2,1)S(1)} %get-tuple-element.61), channel_id=1, source_target_pairs={{0,4},{2,6},{4,0},{6,2},{8,12},{10,14},{12,8},{14,10},{16,20},{18,... | collective-permute-start | bytes 196616 | tf_op jit(solution)/shard_map/ppermute | solution.py:573
  31.7 0.3 collective-permute-done.8.core_ref.refs_1_
  32.0 0.0 copy-start.2
  32.0 0.7 %collective-permute-start.10 = (bf16[256,128]{1,0:T(8,128)(2,1)S(1)}, bf16[256,128]{1,0:T(8,128)(2,1)S(1)}, u32[]{:S(2)}, u32[]{:S(2)}) collective-permute-start(bf16[256,128]{1,0:T(8,128)(2,1)S(1)} %get-tuple-element.63), channel_id=1, source_target_pairs={{0,6},{2,4},{4,2},{6,0},{8,14},{10,12},{12,10},{14,8},{16,22},{18,... | collective-permute-start | bytes 196616 | tf_op jit(solution)/shard_map/ppermute | solution.py:573
  32.8 1.4 %collective-permute-start.11 = (bf16[512,128]{1,0:T(8,128)(2,1)S(1)}, bf16[512,128]{1,0:T(8,128)(2,1)S(1)}, u32[]{:S(2)}, u32[]{:S(2)}) collective-permute-start(bf16[512,128]{1,0:T(8,128)(2,1)S(1)} %get-tuple-element.64), channel_id=1, source_target_pairs={{0,1},{1,0},{2,3},{3,2},{4,5},{5,4},{6,7},{7,6},{8,9},{9,8},{10,11... | collective-permute-start | bytes 393224 | tf_op jit(solution)/shard_map/ppermute | solution.py:664
  34.2 1.3 %collective-permute-done.9.refs_2_.first_ref = bf16[256,128]{1,0:T(8,128)(2,1)S(1)} collective-permute-done((bf16[256,128]{1,0:T(8,128)(2,1)S(1)}, bf16[256,128]{1,0:T(8,128)(2,1)S(1)}, u32[]{:S(2)}, u32[]{:S(2)}) %collective-permute-start.9) | collective-permute-done | bytes 65568 | tf_op jit(solution)/shard_map/ppermute | solution.py:573
  35.5 0.9 %collective-permute-done.10.refs_3_.second_ref = bf16[256,128]{1,0:T(8,128)(2,1)S(1)} collective-permute-done((bf16[256,128]{1,0:T(8,128)(2,1)S(1)}, bf16[256,128]{1,0:T(8,128)(2,1)S(1)}, u32[]{:S(2)}, u32[]{:S(2)}) %collective-permute-start.10) | collective-permute-done | bytes 65568 | tf_op jit(solution)/shard_map/ppermute | solution.py:573
  36.4 1.5 %collective-permute-start.15 = (bf16[256,128]{1,0:T(8,128)(2,1)S(1)}, bf16[256,128]{1,0:T(8,128)(2,1)S(1)}, u32[]{:S(2)}, u32[]{:S(2)}) collective-permute-start(bf16[256,128]{1,0:T(8,128)(2,1)S(1)} %get-tuple-element.67), channel_id=1, source_target_pairs={{0,1},{1,0},{2,3},{3,2},{4,5},{5,4},{6,7},{7,6},{8,9},{9,8},{10,11... | collective-permute-start | bytes 196616 | tf_op jit(solution)/shard_map/ppermute | solution.py:665
  38.0 0.0 copy-start
  38.0 0.0 copy-start.1
  38.0 0.0 copy-start.4
  38.0 0.6 %collective-permute-start.12 = (bf16[256,128]{1,0:T(8,128)(2,1)S(1)}, bf16[256,128]{1,0:T(8,128)(2,1)S(1)}, u32[]{:S(2)}, u32[]{:S(2)}) collective-permute-start(bf16[256,128]{1,0:T(8,128)(2,1)S(1)} %get-tuple-element.65), channel_id=1, source_target_pairs={{0,1},{1,0},{2,3},{3,2},{4,5},{5,4},{6,7},{7,6},{8,9},{9,8},{10,11... | collective-permute-start | bytes 196616 | tf_op jit(solution)/shard_map/ppermute | solution.py:665
  38.5 0.0 collective-permute-done.4.other_residual_ref
  38.5 1.1 %shard_map.106.own_ref = f32[256,1024]{1,0:T(8,128)S(1)} custom-call(s32[2]{0:T(128)S(1)} %pad_add_fusion.index_ref, bf16[256,512]{1,0:T(8,128)(2,1)S(1)} %copy-done.5, bf16[256,512]{1,0:T(8,128)(2,1)S(1)} %collective-permute-done.4.other_residual_ref, bf16[512,1024]{1,0:T(8,128)(2,1)S(1)} %copy-done.3, ...), custom_call_target="tpu_custom_call" | custom-call | flops 1384199936 | tf_op jit(solution)/shard_map/pallas_call | solution.py:531
  39.7 0.0 collective-permute-done.11.refs_0_
  39.7 1.5 %collective-permute-done.15.refs_1_ = bf16[256,128]{1,0:T(8,128)(2,1)S(1)} collective-permute-done((bf16[256,128]{1,0:T(8,128)(2,1)S(1)}, bf16[256,128]{1,0:T(8,128)(2,1)S(1)}, u32[]{:S(2)}, u32[]{:S(2)}) %collective-permute-start.15) | collective-permute-done | bytes 65568 | tf_op jit(solution)/shard_map/ppermute | solution.py:665
  41.1 0.0 collective-permute-done.14.refs_3_
  41.1 0.0 copy-done.2
  41.1 0.0 copy-done
  41.2 0.0 copy-done.1
  41.2 0.0 copy-done.4
  41.2 2.0 %shard_map.109 = (bf16[128,512]{1,0:T(8,128)(2,1)S(1)}, f32[128,512]{1,0:T(8,128)S(1)}) custom-call(s32[2]{0:T(128)S(1)} %pad_add_fusion.index_ref, f32[256,1024]{1,0:T(8,128)S(1)} %shard_map.106.own_ref, bf16[512,128]{1,0:T(8,128)(2,1)S(1)} %collective-permute-done.11.refs_0_, bf16[256,128]{1,0:T(8,128)(2,1)S(1)} %collective-permute-done.15.refs_1_, ...), custom_call_target="tpu_custom_call" | custom-call | flops 2307000064 | tf_op jit(solution)/shard_map/pallas_call | solution.py:531
  43.2 1.8 %collective-permute-start.17 = (bf16[128,512]{1,0:T(8,128)(2,1)S(1)}, bf16[128,512]{1,0:T(8,128)(2,1)S(1)}, u32[]{:S(2)}, u32[]{:S(2)}) collective-permute-start(bf16[128,512]{1,0:T(8,128)(2,1)S(1)} %get-tuple-element.70), channel_id=1, source_target_pairs={{0,1},{1,0},{2,3},{3,2},{4,5},{5,4},{6,7},{7,6},{8,9},{9,8},{10,11... | collective-permute-start | bytes 393224 | tf_op jit(solution)/shard_map/ppermute | solution.py:703
  45.0 0.0 collective-permute-done.12.refs_1_
  45.0 2.0 %shard_map.108 = (bf16[128,512]{1,0:T(8,128)(2,1)S(1)}, f32[128,512]{1,0:T(8,128)S(1)}) custom-call(s32[2]{0:T(128)S(1)} %pad_add_fusion.index_ref, f32[256,1024]{1,0:T(8,128)S(1)} %shard_map.106.own_ref, bf16[512,128]{1,0:T(8,128)(2,1)S(1)} %collective-permute-done.11.refs_0_, bf16[256,128]{1,0:T(8,128)(2,1)S(1)} %collective-permute-done.12.refs_1_, ...), custom_call_target="tpu_custom_call" | custom-call | flops 2307000064 | tf_op jit(solution)/shard_map/pallas_call | solution.py:531
  47.0 0.3 collective-permute-start.16
  47.3 1.3 %collective-permute-done.17.refs_3_ = bf16[128,512]{1,0:T(8,128)(2,1)S(1)} collective-permute-done((bf16[128,512]{1,0:T(8,128)(2,1)S(1)}, bf16[128,512]{1,0:T(8,128)(2,1)S(1)}, u32[]{:S(2)}, u32[]{:S(2)}) %collective-permute-start.17) | collective-permute-done | bytes 131104 | tf_op jit(solution)/shard_map/ppermute | solution.py:703
  48.6 3.4 %collective-permute-done.16.refs_2_ = bf16[128,512]{1,0:T(8,128)(2,1)S(1)} collective-permute-done((bf16[128,512]{1,0:T(8,128)(2,1)S(1)}, bf16[128,512]{1,0:T(8,128)(2,1)S(1)}, u32[]{:S(2)}, u32[]{:S(2)}) %collective-permute-start.16) | collective-permute-done | bytes 131104 | tf_op jit(solution)/shard_map/ppermute | solution.py:703
  52.0 0.8 %shard_map.110 = bf16[256,512]{1,0:T(8,128)(2,1)} custom-call(f32[128,512]{1,0:T(8,128)S(1)} %get-tuple-element.66.refs_0_, f32[128,512]{1,0:T(8,128)S(1)} %get-tuple-element.68.refs_1_, bf16[128,512]{1,0:T(8,128)(2,1)S(1)} %collective-permute-done.16.refs_2_, bf16[128,512]{1,0:T(8,128)(2,1)S(1)} %collective-permute-done.17.refs_3_), custom_call_target="tpu_custom_call" | custom-call | flops 922800000 | tf_op jit(solution)/shard_map/pallas_call | solution.py:531
  (3 shorter events, 0.1 us)
Async XLA Ops:
  0.0 1.2 %copy-start.6 = (s32[6,8]{1,0:T(8,128)S(1)}, s32[6,8]{1,0:T(8,128)}, u32[]{:S(2)}) copy-start(s32[6,8]{1,0:T(8,128)} %offset_ref.5) | copy-start | bytes 580
  1.2 4.2 %copy-start.3 = (bf16[512,1024]{1,0:T(8,128)(2,1)S(1)}, bf16[512,1024]{1,0:T(8,128)(2,1)}, u32[]{:S(2)}) copy-start(bf16[512,1024]{1,0:T(8,128)(2,1)} %weight_ref.1) | copy-start | bytes 3145732
  2.3 5.0 %collective-permute-start = (bf16[1536,128]{1,0:T(8,128)(2,1)S(1)}, bf16[1536,128]{1,0:T(8,128)(2,1)S(1)}, u32[]{:S(2)}, u32[]{:S(2)}) collective-permute-start(bf16[1536,128]{1,0:T(8,128)(2,1)S(1)} %get-tuple-element.39), channel_id=1, source_target_pairs={{0,2},{2,0},{4,6},{6,4},{8,10},{10,8},{12,14},{14,12},{16,18},{18,... | collective-permute-start | bytes 1179656 | tf_op jit(solution)/shard_map/ppermute | solution.py:573
  2.8 6.4 %collective-permute-start.1 = (bf16[240,128]{1,0:T(8,128)(2,1)S(1)}, bf16[240,128]{1,0:T(8,128)(2,1)S(1)}, u32[]{:S(2)}, u32[]{:S(2)}) collective-permute-start(bf16[240,128]{1,0:T(8,128)(2,1)S(1)} %get-tuple-element.43), channel_id=1, source_target_pairs={{0,4},{2,6},{4,0},{6,2},{8,12},{10,14},{12,8},{14,10},{16,20},{18,... | collective-permute-start | bytes 184328 | tf_op jit(solution)/shard_map/ppermute | solution.py:573
  5.4 4.0 %collective-permute-start.2 = (bf16[240,128]{1,0:T(8,128)(2,1)S(1)}, bf16[240,128]{1,0:T(8,128)(2,1)S(1)}, u32[]{:S(2)}, u32[]{:S(2)}) collective-permute-start(bf16[240,128]{1,0:T(8,128)(2,1)S(1)} %get-tuple-element.44), channel_id=1, source_target_pairs={{0,6},{2,4},{4,2},{6,0},{8,14},{10,12},{12,10},{14,8},{16,22},{18,... | collective-permute-start | bytes 184328 | tf_op jit(solution)/shard_map/ppermute | solution.py:573
  5.5 14.2 %collective-permute-start.13 = (bf16[256,1024]{1,0:T(8,128)(2,1)S(1)}, bf16[256,1024]{1,0:T(8,128)(2,1)S(1)}, u32[]{:S(2)}, u32[]{:S(2)}) collective-permute-start(bf16[256,1024]{1,0:T(8,128)(2,1)S(1)} %constant_dynamic-slice_fusion), channel_id=1, source_target_pairs={{0,1},{1,0},{2,3},{3,2},{4,5},{5,4},{6,7},{7,6},{8,9},{9,8},{10,11... | collective-permute-start | bytes 1572872 | tf_op jit(solution)/shard_map/ppermute | solution.py:578
  7.2 14.2 %copy-start.5 = (bf16[256,512]{1,0:T(8,128)(2,1)S(1)}, bf16[256,512]{1,0:T(8,128)(2,1)}, u32[]{:S(2)}) copy-start(bf16[256,512]{1,0:T(8,128)(2,1)} %residual_ref.1) | copy-start | bytes 786436
  9.9 11.5 %collective-permute-start.3 = (bf16[1536,128]{1,0:T(8,128)(2,1)S(1)}, bf16[1536,128]{1,0:T(8,128)(2,1)S(1)}, u32[]{:S(2)}, u32[]{:S(2)}) collective-permute-start(bf16[1536,128]{1,0:T(8,128)(2,1)S(1)} %get-tuple-element.46), channel_id=1, source_target_pairs={{0,4},{2,6},{4,0},{6,2},{8,12},{10,14},{12,8},{14,10},{16,20},{18,... | collective-permute-start | bytes 1179656 | tf_op jit(solution)/shard_map/ppermute | solution.py:573
  11.4 14.7 %collective-permute-start.6 = (bf16[4,112,128]{2,1,0:T(8,128)(2,1)S(1)}, bf16[4,112,128]{2,1,0:T(8,128)(2,1)S(1)}, u32[]{:S(2)}, u32[]{:S(2)}) collective-permute-start(bf16[4,112,128]{2,1,0:T(8,128)(2,1)S(1)} %get-tuple-element.53), channel_id=1, source_target_pairs={{0,16},{2,18},{4,20},{6,22},{8,24},{10,26},{12,28},{14,30},{16,0},... | collective-permute-start | bytes 344072 | tf_op jit(solution)/shard_map/ppermute | solution.py:573
  14.0 12.1 %collective-permute-start.7 = (bf16[4,112,128]{2,1,0:T(8,128)(2,1)S(1)}, bf16[4,112,128]{2,1,0:T(8,128)(2,1)S(1)}, u32[]{:S(2)}, u32[]{:S(2)}) collective-permute-start(bf16[4,112,128]{2,1,0:T(8,128)(2,1)S(1)} %get-tuple-element.53), channel_id=1, source_target_pairs={{0,24},{2,26},{4,28},{6,30},{8,16},{10,18},{12,20},{14,22},{16,8},... | collective-permute-start | bytes 344072 | tf_op jit(solution)/shard_map/ppermute | solution.py:573
  15.4 11.2 %collective-permute-start.5 = (bf16[4,240,128]{2,1,0:T(8,128)(2,1)S(1)}, bf16[4,240,128]{2,1,0:T(8,128)(2,1)S(1)}, u32[]{:S(2)}, u32[]{:S(2)}) collective-permute-start(bf16[4,240,128]{2,1,0:T(8,128)(2,1)S(1)} %get-tuple-element.52.refs_0_), channel_id=1, source_target_pairs={{0,8},{2,10},{4,12},{6,14},{8,0},{10,2},{12,4},{14,6},{16,24},{18,... | collective-permute-start | bytes 737288 | tf_op jit(solution)/shard_map/ppermute | solution.py:573
  19.7 21.5 %collective-permute-start.14 = (bf16[256,1024]{1,0:T(8,128)(2,1)S(1)}, bf16[256,1024]{1,0:T(8,128)(2,1)S(1)}, u32[]{:S(2)}, u32[]{:S(2)}) collective-permute-start(bf16[256,1024]{1,0:T(8,128)(2,1)S(1)} %collective-permute-done.13.refs_2_), channel_id=1, source_target_pairs={{0,2},{2,0},{4,6},{6,4},{8,10},{10,8},{12,14},{14,12},{16,18},{18,... | collective-permute-start | bytes 1572872 | tf_op jit(solution)/shard_map/ppermute | solution.py:573
  24.6 13.9 %collective-permute-start.4 = (bf16[256,512]{1,0:T(8,128)(2,1)S(1)}, bf16[256,512]{1,0:T(8,128)(2,1)S(1)}, u32[]{:S(2)}, u32[]{:S(2)}) collective-permute-start(bf16[256,512]{1,0:T(8,128)(2,1)S(1)} %get-tuple-element.51), channel_id=1, source_target_pairs={{0,1},{1,0},{2,3},{3,2},{4,5},{5,4},{6,7},{7,6},{8,9},{9,8},{10,11... | collective-permute-start | bytes 786440 | tf_op jit(solution)/shard_map/ppermute | solution.py:666
  30.7 1.3 %collective-permute-start.8 = (bf16[256,128]{1,0:T(8,128)(2,1)S(1)}, bf16[256,128]{1,0:T(8,128)(2,1)S(1)}, u32[]{:S(2)}, u32[]{:S(2)}) collective-permute-start(bf16[256,128]{1,0:T(8,128)(2,1)S(1)} %get-tuple-element.60), channel_id=1, source_target_pairs={{0,2},{2,0},{4,6},{6,4},{8,10},{10,8},{12,14},{14,12},{16,18},{18,... | collective-permute-start | bytes 196616 | tf_op jit(solution)/shard_map/ppermute | solution.py:573
  30.7 4.7 %collective-permute-start.9 = (bf16[256,128]{1,0:T(8,128)(2,1)S(1)}, bf16[256,128]{1,0:T(8,128)(2,1)S(1)}, u32[]{:S(2)}, u32[]{:S(2)}) collective-permute-start(bf16[256,128]{1,0:T(8,128)(2,1)S(1)} %get-tuple-element.61), channel_id=1, source_target_pairs={{0,4},{2,6},{4,0},{6,2},{8,12},{10,14},{12,8},{14,10},{16,20},{18,... | collective-permute-start | bytes 196616 | tf_op jit(solution)/shard_map/ppermute | solution.py:573
  32.0 9.2 %copy-start.2 = (bf16[1024,1024]{1,0:T(8,128)(2,1)S(1)}, bf16[1024,1024]{1,0:T(8,128)(2,1)}, u32[]{:S(2)}) copy-start(bf16[1024,1024]{1,0:T(8,128)(2,1)} %refs_7_.3) | copy-start | bytes 6291460
  32.0 4.4 %collective-permute-start.10 = (bf16[256,128]{1,0:T(8,128)(2,1)S(1)}, bf16[256,128]{1,0:T(8,128)(2,1)S(1)}, u32[]{:S(2)}, u32[]{:S(2)}) collective-permute-start(bf16[256,128]{1,0:T(8,128)(2,1)S(1)} %get-tuple-element.63), channel_id=1, source_target_pairs={{0,6},{2,4},{4,2},{6,0},{8,14},{10,12},{12,10},{14,8},{16,22},{18,... | collective-permute-start | bytes 196616 | tf_op jit(solution)/shard_map/ppermute | solution.py:573
  32.8 6.9 %collective-permute-start.11 = (bf16[512,128]{1,0:T(8,128)(2,1)S(1)}, bf16[512,128]{1,0:T(8,128)(2,1)S(1)}, u32[]{:S(2)}, u32[]{:S(2)}) collective-permute-start(bf16[512,128]{1,0:T(8,128)(2,1)S(1)} %get-tuple-element.64), channel_id=1, source_target_pairs={{0,1},{1,0},{2,3},{3,2},{4,5},{5,4},{6,7},{7,6},{8,9},{9,8},{10,11... | collective-permute-start | bytes 393224 | tf_op jit(solution)/shard_map/ppermute | solution.py:664
  36.4 4.7 %collective-permute-start.15 = (bf16[256,128]{1,0:T(8,128)(2,1)S(1)}, bf16[256,128]{1,0:T(8,128)(2,1)S(1)}, u32[]{:S(2)}, u32[]{:S(2)}) collective-permute-start(bf16[256,128]{1,0:T(8,128)(2,1)S(1)} %get-tuple-element.67), channel_id=1, source_target_pairs={{0,1},{1,0},{2,3},{3,2},{4,5},{5,4},{6,7},{7,6},{8,9},{9,8},{10,11... | collective-permute-start | bytes 196616 | tf_op jit(solution)/shard_map/ppermute | solution.py:665
  38.0 3.2 %copy-start = (bf16[1024,1024]{1,0:T(8,128)(2,1)S(1)}, bf16[1024,1024]{1,0:T(8,128)(2,1)}, u32[]{:S(2)}) copy-start(bf16[1024,1024]{1,0:T(8,128)(2,1)} %refs_5_.5) | copy-start | bytes 6291460
  38.0 3.2 %copy-start.1 = (bf16[1024,1024]{1,0:T(8,128)(2,1)S(1)}, bf16[1024,1024]{1,0:T(8,128)(2,1)}, u32[]{:S(2)}) copy-start(bf16[1024,1024]{1,0:T(8,128)(2,1)} %refs_6_.3) | copy-start | bytes 6291460
  38.0 3.2 %copy-start.4 = (f32[1024]{0:T(1024)S(1)}, f32[1024]{0:T(1024)}, u32[]{:S(2)}) copy-start(f32[1024]{0:T(1024)} %param.16) | copy-start | bytes 12292
  38.0 7.0 %collective-permute-start.12 = (bf16[256,128]{1,0:T(8,128)(2,1)S(1)}, bf16[256,128]{1,0:T(8,128)(2,1)S(1)}, u32[]{:S(2)}, u32[]{:S(2)}) collective-permute-start(bf16[256,128]{1,0:T(8,128)(2,1)S(1)} %get-tuple-element.65), channel_id=1, source_target_pairs={{0,1},{1,0},{2,3},{3,2},{4,5},{5,4},{6,7},{7,6},{8,9},{9,8},{10,11... | collective-permute-start | bytes 196616 | tf_op jit(solution)/shard_map/ppermute | solution.py:665
  43.2 5.4 %collective-permute-start.17 = (bf16[128,512]{1,0:T(8,128)(2,1)S(1)}, bf16[128,512]{1,0:T(8,128)(2,1)S(1)}, u32[]{:S(2)}, u32[]{:S(2)}) collective-permute-start(bf16[128,512]{1,0:T(8,128)(2,1)S(1)} %get-tuple-element.70), channel_id=1, source_target_pairs={{0,1},{1,0},{2,3},{3,2},{4,5},{5,4},{6,7},{7,6},{8,9},{9,8},{10,11... | collective-permute-start | bytes 393224 | tf_op jit(solution)/shard_map/ppermute | solution.py:703
  47.0 5.0 %collective-permute-start.16 = (bf16[128,512]{1,0:T(8,128)(2,1)S(1)}, bf16[128,512]{1,0:T(8,128)(2,1)S(1)}, u32[]{:S(2)}, u32[]{:S(2)}) collective-permute-start(bf16[128,512]{1,0:T(8,128)(2,1)S(1)} %get-tuple-element.69), channel_id=1, source_target_pairs={{0,1},{1,0},{2,3},{3,2},{4,5},{5,4},{6,7},{7,6},{8,9},{9,8},{10,11... | collective-permute-start | bytes 393224 | tf_op jit(solution)/shard_map/ppermute | solution.py:703
